TPU v7x, 32 devices: a whole 2x2x4 slice. The times are simulated.
32 devices in a mesh: vec: 8 (over z, y), gz: 4 (over x, core).
Axes of the slice: x: 2, y: 2, z: 4, core: 2. Of those that a mesh axis runs over, the one named last changes fastest.
Arguments:
- base_flow: float32 [3, 128, 128, 128], P(None, 'gz'), may hold values from -6 to 6
- tangents: float32 [8, 3, 128, 128, 128], P('vec', None, 'gz'), may hold values from -6 to 6
- shells: int32 [4], replicated, may hold values from 1 to 31
Outputs:
- base_next: float32 [3, 128, 128, 128], P(None, 'gz', 'vec')
- ortho_tangents: float32 [8, 3, 128, 128, 128], P('vec', None, 'gz')
- growth: float32 [8], replicated
Inputs may be any that keep to these rules, and one draw needn't show every extreme that they name: `shells`: repeats may occur.
All inputs are finite; a program needn't handle non-finite values.
Results may differ from a plain program's by a relative error of at most 0.00017.
Values sent between devices are 32-bit elements; how exact they have to be, the bound alone decides.
No kernel may reach another device: no remote copies, remote signals or barrier semaphores. Data moves between devices by JAX's collectives and lax.ppermute only.
A program may use at most 256 MiB of HBM per device.

v0:
```python
import math

import jax
import jax.numpy as jnp
from jax import lax
from jax.sharding import PartitionSpec as P

NX = 128
NY = 128
NZ = 128


time_step = 0.005
viscosity = 0.01
forcing_amplitude = 4.0
highest = lax.Precision.HIGHEST


def padded_2(block, sides, width):
    for axis, dim in sides:
        count = lax.axis_size(axis)
        forward = [(i, i + 1) for i in range(count - 1)]
        forward.append((count - 1, 0))
        backward = [(target, source) for source, target in forward]
        low = lax.ppermute(
            lax.slice_in_dim(block, block.shape[dim] - width, None, axis=dim), axis, forward
        )
        high = lax.ppermute(lax.slice_in_dim(block, 0, width, axis=dim), axis, backward)
        block = jnp.concatenate([low, block, high], axis=dim)
    return block


def grid_spacing():
    return 2.0 * math.pi / NX


def dft_tables(length):
    indices = jnp.arange(length, dtype=jnp.int32)
    angles = (
        2.0 * math.pi / length * (indices[:, None] * indices[None, :] % length).astype(jnp.float32)
    )
    return (jnp.cos(angles), jnp.sin(angles))


def forward(real_in, imag_in):
    number, layers = (real_in.shape[0], real_in.shape[1])
    cos_x, sin_x = dft_tables(NX)
    cos_y, sin_y = dft_tables(NY)
    cos_z, sin_z = dft_tables(NZ)
    real_x = jnp.einsum("mzyx,xk->mzyk", real_in, cos_x, precision=highest) + jnp.einsum(
        "mzyx,xk->mzyk", imag_in, sin_x, precision=highest
    )
    imag_x = jnp.einsum("mzyx,xk->mzyk", imag_in, cos_x, precision=highest) - jnp.einsum(
        "mzyx,xk->mzyk", real_in, sin_x, precision=highest
    )
    real_y = jnp.einsum("mzyx,yk->mzkx", real_x, cos_y, precision=highest) + jnp.einsum(
        "mzyx,yk->mzkx", imag_x, sin_y, precision=highest
    )
    imag_y = jnp.einsum("mzyx,yk->mzkx", imag_x, cos_y, precision=highest) - jnp.einsum(
        "mzyx,yk->mzkx", real_x, sin_y, precision=highest
    )
    flat_shape = (number, layers, NY * NX)
    real_c, imag_c = (
        lax.all_to_all(real_y.reshape(flat_shape), "gz", split_axis=2, concat_axis=1, tiled=True),
        lax.all_to_all(imag_y.reshape(flat_shape), "gz", split_axis=2, concat_axis=1, tiled=True),
    )
    real_z = jnp.einsum("mzp,zk->mkp", real_c, cos_z, precision=highest) + jnp.einsum(
        "mzp,zk->mkp", imag_c, sin_z, precision=highest
    )
    imag_z = jnp.einsum("mzp,zk->mkp", imag_c, cos_z, precision=highest) - jnp.einsum(
        "mzp,zk->mkp", real_c, sin_z, precision=highest
    )
    return (real_z, imag_z)


def backward(real_z, imag_z, layers):
    number = real_z.shape[0]
    cos_x, sin_x = dft_tables(NX)
    cos_y, sin_y = dft_tables(NY)
    cos_z, sin_z = dft_tables(NZ)
    real_c = jnp.einsum("mkp,kz->mzp", real_z, cos_z, precision=highest) - jnp.einsum(
        "mkp,kz->mzp", imag_z, sin_z, precision=highest
    )
    imag_c = jnp.einsum("mkp,kz->mzp", imag_z, cos_z, precision=highest) + jnp.einsum(
        "mkp,kz->mzp", real_z, sin_z, precision=highest
    )
    real_s, imag_s = (
        lax.all_to_all(real_c, "gz", split_axis=1, concat_axis=2, tiled=True),
        lax.all_to_all(imag_c, "gz", split_axis=1, concat_axis=2, tiled=True),
    )
    real_s = real_s.reshape(number, layers, NY, NX)
    imag_s = imag_s.reshape(number, layers, NY, NX)
    real_y = jnp.einsum("mzkx,ky->mzyx", real_s, cos_y, precision=highest) - jnp.einsum(
        "mzkx,ky->mzyx", imag_s, sin_y, precision=highest
    )
    imag_y = jnp.einsum("mzkx,ky->mzyx", imag_s, cos_y, precision=highest) + jnp.einsum(
        "mzkx,ky->mzyx", real_s, sin_y, precision=highest
    )
    real_out = jnp.einsum("mzyk,kx->mzyx", real_y, cos_x, precision=highest) - jnp.einsum(
        "mzyk,kx->mzyx", imag_y, sin_x, precision=highest
    )
    imag_out = jnp.einsum("mzyk,kx->mzyx", imag_y, cos_x, precision=highest) + jnp.einsum(
        "mzyk,kx->mzyx", real_y, sin_x, precision=highest
    )
    scale = 1.0 / (NX * NY * NZ)
    return (real_out * scale, imag_out * scale)


def inverse_symbol(width):
    spacing = grid_spacing()
    wave_z = jnp.arange(NZ, dtype=jnp.int32)[:, None]
    flat_index = lax.axis_index("gz") * width + jnp.arange(width, dtype=jnp.int32)[None, :]
    wave_y = flat_index // NX
    wave_x = flat_index % NX

    def slope(wave, length):
        return jnp.sin(2.0 * math.pi / length * wave.astype(jnp.float32)) / spacing

    shape = (NZ, width)
    squared = jnp.broadcast_to(slope(wave_x, NX), shape) ** 2
    squared = squared + jnp.broadcast_to(slope(wave_y, NY), shape) ** 2
    squared = squared + jnp.broadcast_to(slope(wave_z, NZ), shape) ** 2
    resting = (wave_x % (NX // 2) == 0) & (wave_y % (NY // 2) == 0) & (wave_z % (NZ // 2) == 0)
    return jnp.where(resting, 0.0, 1.0 / jnp.where(resting, 1.0, squared))


def project_potential(inner, padded_rate, layers):
    spacing = grid_spacing()
    spread = jnp.roll(inner[:, 0], -1, 3) - jnp.roll(inner[:, 0], 1, 3)
    spread = spread + jnp.roll(inner[:, 1], -1, 2) - jnp.roll(inner[:, 1], 1, 2)
    spread = (spread + padded_rate[:, 2:] - padded_rate[:, :-2]) / (2.0 * spacing)
    real_z, imag_z = forward(spread[0::2], spread[1::2])
    inverse = inverse_symbol(real_z.shape[2])
    real_p, imag_p = backward(-real_z * inverse, -imag_z * inverse, layers)
    potential = jnp.stack([real_p, imag_p], axis=1).reshape(spread.shape)
    padded_phi = padded_2(potential, (("gz", 1),), 1)
    slope_x = (jnp.roll(potential, -1, 3) - jnp.roll(potential, 1, 3)) / (2.0 * spacing)
    slope_y = (jnp.roll(potential, -1, 2) - jnp.roll(potential, 1, 2)) / (2.0 * spacing)
    slope_z = (padded_phi[:, 2:] - padded_phi[:, :-2]) / (2.0 * spacing)
    return inner - jnp.stack([slope_x, slope_y, slope_z], axis=1)


def tendencies(velocity, tangent, shells, depth):
    spacing = grid_spacing()
    number, layers = (tangent.shape[0], tangent.shape[2])
    stacked = jnp.concatenate([velocity[None], tangent], axis=0).reshape(
        (number + 1) * 3, layers, NY, NX
    )
    padded = padded_2(stacked, (("gz", 1),), depth)
    interior = padded[:, 1:-1]
    extent = interior.shape[1]
    full_shape = (number + 1, 3, extent, NY, NX)
    slopes = [
        ((jnp.roll(interior, -1, 3) - jnp.roll(interior, 1, 3)) / (2.0 * spacing)).reshape(
            full_shape
        ),
        ((jnp.roll(interior, -1, 2) - jnp.roll(interior, 1, 2)) / (2.0 * spacing)).reshape(
            full_shape
        ),
        ((padded[:, 2:] - padded[:, :-2]) / (2.0 * spacing)).reshape(full_shape),
    ]
    laplacian = (
        jnp.roll(interior, -1, 3)
        + jnp.roll(interior, 1, 3)
        + jnp.roll(interior, -1, 2)
        + jnp.roll(interior, 1, 2)
    )
    laplacian = (
        (laplacian + padded[:, 2:] + padded[:, :-2] - 6.0 * interior) / (spacing * spacing)
    ).reshape(full_shape)
    fields = interior.reshape(full_shape)
    base_part_field = fields[0]
    tangent_field = fields[1:]
    positions = (
        lax.axis_index("gz") * layers - (depth - 1) + jnp.arange(extent, dtype=jnp.int32)
    ) % NZ
    angles = 2.0 * math.pi / NZ * (shells[:, None] * positions[None, :] % NZ).astype(jnp.float32)
    profile = forcing_amplitude * jnp.sum(jnp.sin(angles), axis=0)
    zeros = jnp.zeros((extent, NY, NX), jnp.float32)
    forcing = jnp.stack([jnp.broadcast_to(profile[:, None, None], (extent, NY, NX)), zeros, zeros])
    base_advect = jnp.zeros_like(base_part_field)
    tangent_advect = jnp.zeros_like(tangent_field)
    for direction in range(3):
        base_advect = base_advect + base_part_field[direction][None] * slopes[direction][0]
        tangent_advect = (
            tangent_advect + base_part_field[direction][None, None] * slopes[direction][1:]
        )
        tangent_advect = (
            tangent_advect + tangent_field[:, direction][:, None] * slopes[direction][0][None]
        )
    base_part = -base_advect + viscosity * laplacian[0] + forcing
    tangent_part = -tangent_advect + viscosity * laplacian[1:]
    return jnp.concatenate([base_part[None], tangent_part], axis=0)


def advance(velocity, tangent, shells):
    layers = velocity.shape[1]
    rates = tendencies(velocity, tangent, shells, 1)
    padded_rate = padded_2(rates[:, 2], (("gz", 1),), 1)
    rates = project_potential(rates, padded_rate, layers)
    return (velocity + time_step * rates[0], tangent + time_step * rates[1:])


def per_device(base_flow, tangents, shells):
    base_next, tangent_c = advance(base_flow, tangents, shells)
    row_count = NY // lax.axis_size("vec")
    base_rows = lax.dynamic_slice_in_dim(base_next, lax.axis_index("vec") * row_count, row_count, 2)
    flattened = tangent_c.reshape(tangents.shape[0], -1)
    cell_columns = lax.all_to_all(flattened, "vec", split_axis=1, concat_axis=0, tiled=True)
    partial_gram = jnp.dot(cell_columns, cell_columns.T, precision=highest)
    gram_matrix = lax.psum(partial_gram, ("vec", "gz")) / (3.0 * NZ * NY * NX)
    factor = jnp.linalg.cholesky(gram_matrix)
    ortho_rows = lax.linalg.triangular_solve(factor, cell_columns, left_side=True, lower=True)
    returned = lax.all_to_all(ortho_rows, "vec", split_axis=0, concat_axis=1, tiled=True)
    return (base_rows, returned.reshape(tangents.shape), jnp.log(jnp.diagonal(factor)))


def solution(mesh):
    in_specs = (P(None, "gz", None, None), P("vec", None, "gz", None, None), P())
    out_specs = (P(None, "gz", "vec", None), P("vec", None, "gz", None, None), P())
    return jax.shard_map(
        per_device, mesh=mesh, in_specs=in_specs, out_specs=out_specs, check_vma=False
    )
```

profile of v0, /device:TPU:0, one launch (start us, length us, event | category | flops | bytes accessed | tf_op | source)
XLA Modules:
  0.0 1000.1 jit_solution(6002546598891207132)
XLA Ops:
  0.6 11.4 %pad_maximum_fusion.3 = f32[2,3,32,128,128]{4,3,2,1,0:T(8,128)} fusion(f32[1,3,32,128,128]{4,3,2,1,0:T(8,128)} %param.4, f32[1,3,32,128,128]{4,3,2,1,0:T(8,128)} %bitcast.226), kind=kLoop, calls=%fused_computation.12 | loop fusion | flops 3145728 | bytes 25165824 | tf_op jit(solution)/shard_map/concatenate | solution.py:146
  16.3 22.1 %fusion.234 = (f32[6,32,127,128]{3,2,1,0:T(8,128)}, f32[6,32,127,128]{3,2,1,0:T(8,128)}) fusion(f32[6,32,128,128]{3,2,1,0:T(8,128)} %bitcast.204), kind=kLoop, calls=%fused_computation.309 | loop fusion | bytes 49938432 | tf_op jit(solution)/shard_map/jit(_roll_static)/slice | solution.py:157
  38.6 10.1 %fusion.231 = (f32[6,32,128,127]{3,2,1,0:T(8,128)}, f32[6,32,128,127]{3,2,1,0:T(8,128)}) fusion(f32[6,32,128,128]{3,2,1,0:T(8,128)S(1)} %bitcast.209), kind=kLoop, calls=%fused_computation.306 | loop fusion | bytes 49938432 | tf_op jit(solution)/shard_map/jit(_roll_static)/slice | solution.py:154
  48.7 9.9 fusion.232
  58.6 2.9 slice_bitcast_fusion.13
  61.8 15.3 %subtract_multiply_fusion.2 = f32[6,32,128,128]{3,2,1,0:T(8,128)} fusion(f32[6,32,127,128]{3,2,1,0:T(8,128)} %get-tuple-element.21, f32[6,32,1,128]{3,2,1,0:T(1,128)S(1)} %get-tuple-element.23, f32[6,32,1,128]{3,2,1,0:T(1,128)S(1)} %get-tuple-element.22, f32[6,32,127,128]{3,2,1,0:T(8,128)} %get-tuple-element.20), kind=kLoop, calls=%fused_computation.19 | loop fusion | flops 12582912 | bytes 37748736 | tf_op jit(solution)/shard_map/div | solution.py:157
  77.0 3.3 slice_bitcast_fusion.10
  81.6 5.7 subtract_multiply_fusion.1
  87.3 47.4 %subtract_multiply_fusion.3 = (f32[6,32,128,128]{3,2,1,0:T(8,128)}, f32[6,32,128,128]{3,2,1,0:T(8,128)}) fusion(f32[6,32,128,127]{3,2,1,0:T(8,128)} %get-tuple-element.15, f32[6,32,128,1]{3,2,1,0:T(8,128)} %get-tuple-element.17, f32[6,32,128,1]{3,2,1,0:T(8,128)} %get-tuple-element.16, f32[6,32,128,127]{3,2,1,0:T(8,128)} %get-tuple-element.14, ...), kind=kLoop, calls=%fused_computation.20 | loop fusion | flops 50331648 | bytes 88866816 | tf_op jit(solution)/shard_map/div | solution.py:154
  136.3 21.9 %fusion.13 = (f32[1,3,32,128,128]{4,3,2,0,1:T(8,128)S(1)}, f32[1,3,32,128,128]{4,3,2,0,1:T(8,128)S(1)}) fusion(f32[6,32,128,128]{3,2,1,0:T(8,128)} %get-tuple-element.8, f32[1,32,128,128]{3,2,1,0:T(8,128)} %stack_broadcast_in_dim.2, f32[6,32,128,128]{3,2,1,0:T(8,128)} %subtract_multiply_fusion.1, f32[6,32,128,128]{3,2,1,0:T(8,128)} %subtract_multiply_fusion.2, ...), kind=kLoop, calls=%fused_computation.40 | loop fusion | flops 36175872 | bytes 77594624 | tf_op jit(solution)/shard_map/broadcast_in_dim | solution.py:193
  158.2 4.3 fusion.28
  167.0 4.8 fusion.240
  171.8 4.2 fusion.238
  177.8 3.0 collective-permute-done.2
  182.2 7.8 fusion.35
  201.9 4.1 subtract_bitcast_fusion
  206.0 6.3 copy.139
  212.8 74.5 %reduce.8 = f32[16384,32]{1,0:T(8,128)} reduce(f32[16384,1,32]{2,1,0:T(1,128)} %bitcast.222, f32[]{:T(128)} %broadcast.589), dimensions={1}, to_apply=%bitcast.183.reduce_sub_computation | reduce | bytes 4194308
  287.4 7.1 reshape.513
  294.5 4.4 all-to-all-start.1
  298.9 3.7 fusion.79
  302.7 3.5 add_bitcast_fusion
  306.2 6.3 copy.135
  312.5 74.5 %reduce.6 = f32[16384,32]{1,0:T(8,128)} reduce(f32[16384,1,32]{2,1,0:T(1,128)} %bitcast.223, f32[]{:T(128)} %broadcast.589), dimensions={1}, to_apply=%bitcast.181.reduce_sub_computation | reduce | bytes 4194308
  387.1 7.2 reshape.511
  394.2 4.6 all-to-all-start
  399.1 7.7 reduce.9
  406.8 17.1 %reshape.514 = f32[16384,1,32]{2,1,0:T(1,128)} reshape(f32[4,131072]{1,0:T(4,128)S(1)} %reduce.9) | data formatting | bytes 4194304
  424.0 5.5 copy.140
  432.1 3.5 fusion.95
  435.6 7.7 reduce.7
  443.3 16.9 %reshape.512 = f32[16384,1,32]{2,1,0:T(1,128)} reshape(f32[4,131072]{1,0:T(4,128)S(1)} %reduce.7) | data formatting | bytes 4194304
  460.2 5.7 copy.136
  469.4 2.7 fusion.22
  474.3 2.8 fusion.24
  481.1 3.5 copy.108
  484.6 4.4 all-to-all-start.3
  489.1 3.7 fusion.99
  495.1 3.5 copy.105
  498.6 16.3 %all-to-all-done.3 = f32[1,128,4096]{2,0,1:T(1,128)} async-done(((f32[1,128,4096]{2,0,1:T(1,128)}), f32[1,128,4096]{2,0,1:T(1,128)}, u32[]{:S(2)}, u32[]{:S(2)}) %all-to-all-start.3) | async-done | bytes 2097184 | tf_op jit(solution)/shard_map/all_to_all | solution.py:89
  514.8 4.6 all-to-all-start.2
  519.5 4.7 copy.157
  524.2 2.7 reshape.490
  526.9 3.5 fusion.71
  530.4 14.8 %all-to-all-done.2 = f32[1,128,4096]{2,0,1:T(1,128)} async-done(((f32[1,128,4096]{2,0,1:T(1,128)}), f32[1,128,4096]{2,0,1:T(1,128)}, u32[]{:S(2)}, u32[]{:S(2)}) %all-to-all-start.2) | async-done | bytes 2097184 | tf_op jit(solution)/shard_map/all_to_all | solution.py:88
  545.2 4.7 copy.158
  550.0 3.8 reshape.489
  553.8 3.7 fusion.81
  571.5 4.9 slice_bitcast_fusion.3
  576.3 4.9 slice_bitcast_fusion.2
  581.2 4.1 slice_bitcast_fusion
  586.0 8.1 fusion.39
  594.1 6.8 fusion.40
  603.6 9.7 fusion
  613.3 7.4 fusion.1
  620.7 145.3 %all_to_all.89 = f32[1,8,196608]{2,0,1:T(1,128)S(1)} all-to-all(f32[1,8,196608]{2,0,1:T(1,128)S(1)} %bitcast.229), channel_id=1, replica_groups=mesh['vec'=8,'gz'=4] {'vec'}, dimensions={1} | all-to-all | bytes 12582912 | tf_op jit(solution)/shard_map/all_to_all | solution.py:209
  766.0 2.7 copy-done
  768.7 14.5 %fusion.15 = f32[8,8]{0,1:T(8,128)S(1)} fusion(f32[1,8,196608]{2,0,1:T(1,128)S(1)} %all_to_all.89), kind=kOutput, calls=%fused_computation.42 | convolution fusion | flops 150994944 | bytes 6291712 | tf_op jit(solution)/shard_map/dot_general | solution.py:210
  783.2 39.3 %psum.7 = f32[8,8]{0,1:T(8,128)S(1)} all-reduce(f32[8,8]{0,1:T(8,128)S(1)} %fusion.15), channel_id=1, replica_groups=mesh['vec'=8,'gz'=4] {'vec','gz'}, use_global_device_ids=true, to_apply=%region_1.2 | all-reduce | flops 64 | bytes 512 | tf_op jit(solution)/shard_map/psum | solution.py:211
  825.2 11.9 %convolution_bitcast_fusion = f32[8,1,196608]{2,0,1:T(8,128)S(1)} fusion(f32[1,8,196608]{2,0,1:T(1,128)} %copy-done, f32[1,8,8]{1,2,0:T(8,128)S(1)} %custom-call.6), kind=kOutput, calls=%fused_computation.1 | convolution fusion | flops 150994944 | bytes 12583168 | tf_op jit(solution)/shard_map/triangular_solve | solution.py:213
  837.1 14.1 %copy.122 = f32[8,1,196608]{2,1,0:T(1,128)} copy(f32[8,1,196608]{2,0,1:T(8,128)S(1)} %convolution_bitcast_fusion) | data formatting | bytes 12582912 | tf_op jit(solution)/shard_map/all_to_all | solution.py:214
  851.2 4.8 all-to-all-start.5
  859.6 134.0 %all-to-all-done.5 = f32[8,1,196608]{2,1,0:T(1,128)} async-done(((f32[8,1,196608]{2,1,0:T(1,128)}), f32[8,1,196608]{2,1,0:T(1,128)}, u32[]{:S(2)}, u32[]{:S(2)}) %all-to-all-start.5) | async-done | bytes 6291488 | tf_op jit(solution)/shard_map/all_to_all | solution.py:214
  993.6 6.3 copy.160
  (124 shorter events, 65.6 us)
Async XLA Ops:
  13.9 66.4 %collective-permute-start = (f32[6,1,128,128]{3,2,1,0:T(8,128)}, f32[6,1,128,128]{3,2,1,0:T(8,128)S(1)}, u32[]{:S(2)}, u32[]{:S(2)}) collective-permute-start(f32[6,1,128,128]{3,2,1,0:T(8,128)} %get-tuple-element.19), channel_id=1, source_target_pairs={{1,0},{2,1},{3,2},{0,3},{5,4},{6,5},{7,6},{4,7},{9,8},{10,9},{11,1... | collective-permute-start | bytes 1179656 | tf_op jit(solution)/shard_map/ppermute | solution.py:28
  16.3 22.2 %slice-start = ((s8[12582912]{0:T(1024)(128)(4,1)}), s8[4194304]{0:T(1024)(128)(4,1)S(1)}, s32[]{:S(2)}) async-start(s8[12582912]{0:T(1024)(128)(4,1)} %bitcast.206), calls=%async_computation.6 | async-start | bytes 8388608
  16.3 22.2 %slice-start.1 = ((s8[12582912]{0:T(1024)(128)(4,1)}), s8[4194304]{0:T(1024)(128)(4,1)S(1)}, s32[]{:S(2)}) async-start(s8[12582912]{0:T(1024)(128)(4,1)} %bitcast.206), calls=%async_computation.7 | async-start | bytes 8388608
  16.3 22.2 %slice-start.2 = ((s8[12582912]{0:T(1024)(128)(4,1)}), s8[4194304]{0:T(1024)(128)(4,1)S(1)}, s32[]{:S(2)}) async-start(s8[12582912]{0:T(1024)(128)(4,1)} %bitcast.206), calls=%async_computation.8 | async-start | bytes 8388608
  16.3 64.0 %collective-permute-start.1 = (f32[6,1,128,128]{3,2,1,0:T(8,128)S(1)}, f32[6,1,128,128]{3,2,1,0:T(8,128)S(1)}, u32[]{:S(2)}, u32[]{:S(2)}) collective-permute-start(f32[6,1,128,128]{3,2,1,0:T(8,128)S(1)} %get-tuple-element.18), channel_id=1, source_target_pairs={{0,1},{1,2},{2,3},{3,0},{4,5},{5,6},{6,7},{7,4},{8,9},{9,10},{10,1... | collective-permute-start | bytes 1179656 | tf_op jit(solution)/shard_map/ppermute | solution.py:25
  16.3 42.3 %slice-start.14 = ((s8[6291456]{0:T(1024)(128)(4,1)}), s8[4194304]{0:T(1024)(128)(4,1)S(1)}, s32[]{:S(2)}) async-start(s8[6291456]{0:T(1024)(128)(4,1)} %bitcast.227), calls=%async_computation.20 | async-start | bytes 8388608
  38.6 20.0 %slice-start.15 = ((s8[6291456]{0:T(1024)(128)(4,1)}), s8[2097152]{0:T(1024)(128)(4,1)S(1)}, s32[]{:S(2)}) async-start(s8[6291456]{0:T(1024)(128)(4,1)} %bitcast.227), calls=%async_computation.21 | async-start | bytes 4194304
  58.6 3.0 copy-start.12
  58.6 18.4 %slice-start.10 = ((s8[6291456]{0:T(1024)(128)(4,1)}), s8[2097152]{0:T(1024)(128)(4,1)S(1)}, s32[]{:S(2)}) async-start(s8[6291456]{0:T(1024)(128)(4,1)} %bitcast.218), calls=%async_computation.16 | async-start | bytes 4194304
  61.7 18.6 %slice-start.3 = ((s8[12582912]{0:T(1024)(128)(4,1)}), s8[4194304]{0:T(1024)(128)(4,1)S(1)}, s32[]{:S(2)}) async-start(s8[12582912]{0:T(1024)(128)(4,1)} %bitcast.211), calls=%async_computation.9 | async-start | bytes 8388608
  61.7 15.3 %slice-start.11 = ((s8[6291456]{0:T(1024)(128)(4,1)}), s8[4194304]{0:T(1024)(128)(4,1)S(1)}, s32[]{:S(2)}) async-start(s8[6291456]{0:T(1024)(128)(4,1)} %bitcast.218), calls=%async_computation.17 | async-start | bytes 8388608
  61.8 18.6 %slice-start.4 = ((s8[12582912]{0:T(1024)(128)(4,1)}), s8[4194304]{0:T(1024)(128)(4,1)S(1)}, s32[]{:S(2)}) async-start(s8[12582912]{0:T(1024)(128)(4,1)} %bitcast.211), calls=%async_computation.10 | async-start | bytes 8388608
  61.8 19.8 %slice-start.5 = ((s8[12582912]{0:T(1024)(128)(4,1)}), s8[4194304]{0:T(1024)(128)(4,1)S(1)}, s32[]{:S(2)}) async-start(s8[12582912]{0:T(1024)(128)(4,1)} %bitcast.211), calls=%async_computation.11 | async-start | bytes 8388608
  158.1 5.2 copy-start.1
  158.1 7.3 copy-start.2
  167.0 4.8 copy-start.3
  171.8 4.2 copy-start.6
  176.0 4.9 collective-permute-start.2
  177.8 4.4 collective-permute-start.3
  200.5 1.4 copy-start.4
  294.5 99.7 %all-to-all-start.1 = ((f32[4,1,131072]{2,1,0:T(1,128)}), f32[4,1,131072]{2,1,0:T(1,128)}, u32[]{:S(2)}, u32[]{:S(2)}) async-start(f32[4,1,131072]{2,1,0:T(1,128)} %reshape.513), calls=%async_computation.1 | async-start | bytes 4194304 | tf_op jit(solution)/shard_map/all_to_all | solution.py:65
  394.2 41.4 %all-to-all-start = ((f32[4,1,131072]{2,1,0:T(1,128)}), f32[4,1,131072]{2,1,0:T(1,128)}, u32[]{:S(2)}, u32[]{:S(2)}) async-start(f32[4,1,131072]{2,1,0:T(1,128)} %reshape.511), calls=%async_computation | async-start | bytes 4194304 | tf_op jit(solution)/shard_map/all_to_all | solution.py:64
  430.7 1.4 copy-start.9
  465.9 3.4 copy-start.11
  472.1 2.2 copy-start.10
  477.1 1.4 copy-start.8
  484.6 30.2 %all-to-all-start.3 = ((f32[1,128,4096]{2,0,1:T(1,128)}), f32[1,128,4096]{2,0,1:T(1,128)}, u32[]{:S(2)}, u32[]{:S(2)}) async-start(f32[1,128,4096]{2,0,1:T(1,128)} %copy.108), calls=%async_computation.3 | async-start | bytes 4194304 | tf_op jit(solution)/shard_map/all_to_all | solution.py:89
  514.8 30.4 %all-to-all-start.2 = ((f32[1,128,4096]{2,0,1:T(1,128)}), f32[1,128,4096]{2,0,1:T(1,128)}, u32[]{:S(2)}, u32[]{:S(2)}) async-start(f32[1,128,4096]{2,0,1:T(1,128)} %copy.105), calls=%async_computation.2 | async-start | bytes 4194304 | tf_op jit(solution)/shard_map/all_to_all | solution.py:88
  559.7 4.3 copy-start.5
  559.8 4.3 copy-start.7
  585.4 15.5 %collective-permute-start.4 = (f32[2,1,128,128]{3,2,1,0:T(8,128)S(1)}, f32[2,1,128,128]{3,2,1,0:T(8,128)S(1)}, u32[]{:S(2)}, u32[]{:S(2)}) collective-permute-start(f32[2,1,128,128]{3,2,1,0:T(8,128)S(1)} %get-tuple-element.38), channel_id=1, source_target_pairs={{1,0},{2,1},{3,2},{0,3},{5,4},{6,5},{7,6},{4,7},{9,8},{10,9},{11,1... | collective-permute-start | bytes 393224 | tf_op jit(solution)/shard_map/ppermute | solution.py:28
  585.5 15.5 %collective-permute-start.5 = (f32[2,1,128,128]{3,2,1,0:T(8,128)S(1)}, f32[2,1,128,128]{3,2,1,0:T(8,128)S(1)}, u32[]{:S(2)}, u32[]{:S(2)}) collective-permute-start(f32[2,1,128,128]{3,2,1,0:T(8,128)S(1)} %get-tuple-element.39), channel_id=1, source_target_pairs={{0,1},{1,2},{2,3},{3,0},{4,5},{5,6},{6,7},{7,4},{8,9},{9,10},{10,1... | collective-permute-start | bytes 393224 | tf_op jit(solution)/shard_map/ppermute | solution.py:25
  594.1 9.5 slice-start.6
  594.1 9.5 slice-start.8
  594.1 9.5 slice-start.7
  594.1 9.5 slice-start.9
  600.9 12.4 %slice-start.12 = ((s8[6291456]{0:T(1024)(128)(4,1)}), s8[2097152]{0:T(1024)(128)(4,1)S(1)}, s32[]{:S(2)}) async-start(s8[6291456]{0:T(1024)(128)(4,1)} %bitcast.220), calls=%async_computation.18 | async-start | bytes 4194304
  603.6 9.7 slice-start.13
  766.0 2.7 copy-start
  851.2 142.4 %all-to-all-start.5 = ((f32[8,1,196608]{2,1,0:T(1,128)}), f32[8,1,196608]{2,1,0:T(1,128)}, u32[]{:S(2)}, u32[]{:S(2)}) async-start(f32[8,1,196608]{2,1,0:T(1,128)} %copy.122), calls=%async_computation.5 | async-start | bytes 12582912 | tf_op jit(solution)/shard_map/all_to_all | solution.py:214
where the time goes:
time: 1010 us; the launch traced here: 1000 us
  other arithmetic  319 us (32%)
  local copies, waits for them, and re-layouts  207 us (20%)
  blocking collectives  185 us (18%)
  waiting for transfers between devices  169 us (17%)
  matrix products  90.8 us (9%)
  starting transfers between devices  27.6 us (3%)
    unnamed x9, other arithmetic  149 us
    all_to_all x1, blocking collectives, per_device(): lax.all_to_all(flattened, 'vec', split_axis=1, concat_axis=0, tiled=True)  145 us
    all_to_all x1, waiting for transfers between devices, per_device(): lax.all_to_all(ortho_rows, 'vec', split_axis=0, concat_axis=1, tiled=True)  134 us
    unnamed x64, local copies, waits for them, and re-layouts  66.2 us
    div x1, other arithmetic, tendencies(): (jnp.roll(interior, -1, 3) - jnp.roll(interior, 1, 3)) / (2.0 * spacing)  47.4 us
    psum x1, blocking collectives, per_device(): gram_matrix = lax.psum(partial_gram, ('vec', 'gz')) / (3.0 * NZ * NY * NX)  39.3 us
    slice x2, local copies, waits for them, and re-layouts, tendencies(): jnp.roll(interior, -1, 2) - jnp.roll(interior, 1, 2)  22.3 us
    broadcast_in_dim x1, other arithmetic, tendencies(): return jnp.concatenate([base_part[None], tangent_part], axis=0)  21.9 us
  transfers between devices with their start and end apart: 11, of which 5 were waited for; matrix products, arithmetic and copies ran while one was open for 23% of the time, Pallas kernels for 0%

commit v1 on v0

v1 whole, which is shorter than its diff:
```python
import functools
import math

import jax
import jax.numpy as jnp
import ml_dtypes
import numpy as np
from jax import lax
from jax.experimental import pallas as pl
from jax.experimental.pallas import tpu as pltpu
from jax.sharding import PartitionSpec as P

time_step = 0.005
viscosity = 0.01
forcing_amplitude = 4.0

TILE = 16
PAD = 8
VMEM_BYTES = 52 * 1024 * 1024


def spacing_of(nx):
    return 2.0 * math.pi / nx


def real_basis(length):
    cells = np.arange(length)
    columns = [np.full(length, 1.0 / np.sqrt(length)), (-1.0) ** cells / np.sqrt(length)]
    waves = [0, length // 2]
    for wave in range(1, length // 2):
        angle = 2.0 * np.pi * ((cells * wave) % length) / length
        columns += [np.sqrt(2.0 / length) * np.cos(angle), np.sqrt(2.0 / length) * np.sin(angle)]
        waves += [wave, wave]
    sines = np.sin(2.0 * np.pi * np.array(waves) / length) ** 2
    sines[:2] = 0.0
    return np.stack(columns, axis=1), sines


def halves(matrix):
    high = matrix.astype(np.float32).astype(ml_dtypes.bfloat16)
    low = (matrix - high.astype(np.float64)).astype(np.float32).astype(ml_dtypes.bfloat16)
    return high, low


def right_table(matrix):
    high, low = halves(matrix)
    return np.concatenate(
        [np.concatenate([high, low], axis=1), np.concatenate([high, low], axis=1)], axis=0
    )


def left_table(matrix):
    high, low = halves(matrix)
    return np.concatenate(
        [np.concatenate([high, high], axis=1), np.concatenate([low, low], axis=1)], axis=0
    )


def column_tables(sines_y, sines_x):
    four = 4.0 * (sines_y[:, None] + sines_x[None, :])
    resting = four == 0.0
    decay = 1.0 / (1.0 + four / 2.0 + np.sqrt(four + four * four / 4.0))
    green = np.where(resting, 0.0, -decay / np.where(resting, 1.0, 1.0 - decay * decay))
    return decay, green, resting


def split_cat(data, axis):
    high = data.astype(jnp.bfloat16)
    low = (data - high.astype(jnp.float32)).astype(jnp.bfloat16)
    return jnp.concatenate([high, low], axis=axis)


def right_product(data, table):
    out = jnp.dot(split_cat(data, 1), table, preferred_element_type=jnp.float32)
    width = out.shape[1] // 2
    return out[:, :width] + out[:, width:]


def left_product(table, data):
    out = jnp.dot(table, split_cat(data, 0), preferred_element_type=jnp.float32)
    height = out.shape[0] // 2
    return out[:height] + out[height:]


def rate_kernel(tangent, chunk, layers, *refs):
    if tangent:
        (place, u_hbm, v_hbm, lo_hbm, hi_hbm, decay, mark, qx, qy) = refs[:9]
        (a_out, f_out, m_out, us, vs, rz, ry, dv, pw, sems, halo_sems) = refs[9:]
    else:
        (place, profile, v_hbm, lo_hbm, hi_hbm, decay, mark, qx, qy) = refs[:9]
        (a_out, f_out, m_out, vs, rz, ry, dv, pw, sems, halo_sems) = refs[9:]
        us = vs
    step = pl.program_id(0)
    steps = layers // chunk
    ny, nx = f_out.shape[1], f_out.shape[2]
    space = spacing_of(nx)
    adv_scale = -time_step / (2.0 * space)
    lap_scale = viscosity * time_step / (space * space)
    fields = [(v_hbm, vs)]
    if tangent:
        fields.append((u_hbm, us))
    inner = pl.ds(PAD, ny)

    def chunk_copies(k):
        return [
            pltpu.make_async_copy(
                source.at[:, pl.ds(k * chunk, chunk)],
                target.at[:, pl.ds(k * chunk + 2, chunk), inner],
                sems.at[k, i],
            )
            for i, (source, target) in enumerate(fields)
        ]

    def halo_copies(side):
        source = (lo_hbm, hi_hbm)[side]
        near, far = ((1, 0), (layers + 2, layers + 3))[side]
        out = [
            pltpu.make_async_copy(
                source.at[pl.ds(0, 3)], vs.at[:, near, inner], halo_sems.at[side, 0]
            ),
            pltpu.make_async_copy(source.at[6], vs.at[2, far, inner], halo_sems.at[side, 1]),
        ]
        if tangent:
            out += [
                pltpu.make_async_copy(
                    source.at[pl.ds(3, 3)], us.at[:, near, inner], halo_sems.at[side, 2]
                ),
                pltpu.make_async_copy(source.at[7], us.at[2, far, inner], halo_sems.at[side, 3]),
            ]
        return out

    def wrap_rows(ref, index):
        ref[index + (pl.ds(0, PAD),)] = ref[index + (pl.ds(ny, PAD),)]
        ref[index + (pl.ds(ny + PAD, PAD),)] = ref[index + (pl.ds(PAD, PAD),)]

    def wrap_layers(first, count):
        def body(i, carry):
            for _, ref in fields:
                for c in range(3):
                    wrap_rows(ref, (c, first + i))
            return carry

        lax.fori_loop(0, count, body, 0)

    def wait_chunk(k):
        for copy in chunk_copies(k):
            copy.wait()
        wrap_layers(k * chunk + 2, chunk)

    def wait_halo(side):
        for copy in halo_copies(side):
            copy.wait()
        near, far = ((1, 0), (layers + 2, layers + 3))[side]
        wrap_layers(near, 1)
        for _, ref in fields:
            wrap_rows(ref, (2, far))

    def rate_tile(layer, y0, comps):
        rows = pl.ds(PAD + y0, TILE)
        flow = [vs[c, layer, rows] for c in range(3)]
        drift = [us[c, layer, rows] for c in range(3)] if tangent else flow
        out = []

        def neighbours(ref, c, centre):
            return (
                pltpu.roll(centre, nx - 1, 1),
                pltpu.roll(centre, 1, 1),
                ref[c, layer, pl.ds(PAD + y0 + 1, TILE)],
                ref[c, layer, pl.ds(PAD + y0 - 1, TILE)],
                ref[c, layer + 1, rows],
                ref[c, layer - 1, rows],
            )

        for c in comps:
            xp, xm, yp, ym, zp, zm = neighbours(us, c, drift[c])
            adv = flow[0] * (xp - xm) + flow[1] * (yp - ym) + flow[2] * (zp - zm)
            lap = ((xp + xm) + (yp + ym)) + ((zp + zm) - 6.0 * drift[c])
            if tangent:
                xp, xm, yp, ym, zp, zm = neighbours(vs, c, flow[c])
                adv = adv + (
                    drift[0] * (xp - xm) + drift[1] * (yp - ym) + drift[2] * (zp - zm)
                )
            out.append(adv_scale * adv + lap_scale * lap)
        return drift, out

    def z_rate(layer, slot):
        for y0 in range(0, ny, TILE):
            _, (rate,) = rate_tile(layer, y0, (2,))
            rz[slot, pl.ds(y0, TILE)] = rate

    @pl.when(step == 0)
    def _():
        for copy in halo_copies(0):
            copy.start()
        for k in range(steps):
            for copy in chunk_copies(k):
                copy.start()
        for copy in halo_copies(1):
            copy.start()
        wait_halo(0)
        wait_chunk(0)
        if steps == 1:
            wait_halo(1)
        z_rate(1, 0)
        z_rate(2, 1)
        m_out[...] = jnp.zeros(m_out.shape, jnp.float32)
        start = (place[0] * (layers // 2)).astype(jnp.float32)
        pw[...] = jnp.where(mark[...] > 0.0, start, 1.0)

    @pl.when(step + 1 < steps)
    def _():
        wait_chunk(step + 1)

    if steps > 1:

        @pl.when(step + 1 == steps)
        def _():
            wait_halo(1)

    def layer_body(i, carry):
        layer = step * chunk + i + 2
        for y0 in range(0, ny, TILE):
            rows = pl.ds(y0, TILE)
            drift, (rate_x, rate_y) = rate_tile(layer, y0, (0, 1))
            if not tangent:
                rate_x = rate_x + profile[step * chunk + i]
            a_out[0, i, rows] = drift[0] + rate_x
            a_out[1, i, rows] = drift[1] + rate_y
            a_out[2, i, rows] = drift[2] + rz[1, rows]
            dv[i, rows] = pltpu.roll(rate_x, nx - 1, 1) - pltpu.roll(rate_x, 1, 1)
            ry[pl.ds(PAD + y0, TILE)] = rate_y
        z_rate(layer + 1, 2)
        wrap_rows(ry, ())
        for y0 in range(0, ny, TILE):
            rows = pl.ds(y0, TILE)
            along_y = ry[pl.ds(PAD + y0 + 1, TILE)] - ry[pl.ds(PAD + y0 - 1, TILE)]
            middle, upper = rz[1, rows], rz[2, rows]
            along_z = upper - rz[0, rows]
            dv[i, rows] = dv[i, rows] + (along_y + along_z)
            rz[0, rows] = middle
            rz[1, rows] = upper
        return carry

    lax.fori_loop(0, chunk, layer_body, 0)

    waves = right_product(dv[...].reshape(chunk * ny, nx), qx[...]).reshape(chunk, ny, nx)
    waves = left_product(qy[...], jnp.concatenate([waves[i] for i in range(chunk)], axis=1))
    for i in range(chunk):
        f_out[i] = waves[:, i * nx : (i + 1) * nx]
    for y0 in range(0, ny, TILE):
        rows = pl.ds(y0, TILE)
        rate = decay[rows]
        marks = mark[rows]
        power = pw[rows]
        right = [m_out[0, rows], m_out[1, rows]]
        left = [m_out[2, rows], m_out[3, rows]]
        for i in range(chunk):
            f = f_out[i, rows]
            parity = i % 2
            right[parity] = rate * right[parity] + f
            left[parity] = left[parity] + power * f
            if parity == 1:
                power = rate * power + marks
        pw[rows] = power
        m_out[0, rows], m_out[1, rows] = right
        m_out[2, rows], m_out[3, rows] = left


def solve_kernel(chunk, layers, period, rows_out, *refs):
    (place, f_in, sides, totals, wrap_l, wrap_r, decay, green, mark, qy, qx, a_in) = refs[:12]
    (v_out, qm, hat, phi) = refs[12:]
    step = pl.program_id(0)
    ny, nx = f_in.shape[1], f_in.shape[2]
    tall = rows_out + 2 * PAD
    half = layers // 2

    def sweep(y0, resting):
        size = PAD if resting else TILE
        rows = pl.ds(y0, size)
        rate = decay[rows]
        factor = green[rows]
        left = [sides[p, rows] + wrap_l[rows] * totals[p, rows] for p in range(2)]
        right = [sides[2 + p, rows] + wrap_r[rows] * totals[2 + p, rows] for p in range(2)]
        back = list(right)
        for z in reversed(range(layers)):
            f = f_in[z, rows]
            part = rate * back[z % 2]
            qm[z, rows] = part
            back[z % 2] = part + f
        hat[0, rows] = factor * (left[1] + rate * back[1])
        ahead = list(left)
        for z in range(layers):
            ahead[z % 2] = rate * ahead[z % 2] + f_in[z, rows]
            hat[z + 1, rows] = factor * (ahead[z % 2] + qm[z, rows])
        hat[layers + 1, rows] = factor * (rate * ahead[0] + right[0])

    def resting_columns():
        rows = pl.ds(0, PAD)
        marked = mark[rows] > 0.0
        start = place[0] * half
        for p in range(2):
            own0 = jnp.zeros((PAD, nx), jnp.float32)
            own1 = jnp.zeros((PAD, nx), jnp.float32)
            for j in range(half):
                f = f_in[2 * j + p, rows]
                own0 = own0 + f
                own1 = own1 + (start + j).astype(jnp.float32) * f
            left0 = sides[p, rows]
            right1 = sides[2 + p, rows]
            all0 = totals[p, rows]
            all1 = totals[2 + p, rows]
            right0 = all0 - own0 - left0
            left1 = all1 - own1 - right1
            prefix = jnp.zeros((PAD, nx), jnp.float32)
            twice = jnp.zeros((PAD, nx), jnp.float32)
            first, last = (0, half + 1) if p == 0 else (-1, half)
            for j in range(first, last):
                t = (start + j).astype(jnp.float32)
                if j > 0:
                    twice = twice + prefix
                if 0 <= j < half:
                    prefix = prefix + f_in[2 * j + p, rows]
                value = 0.5 * (t * (left0 - right0 - own0) + (right1 - left1 + own1)) + twice
                value = value - t * (t * all0 - 2.0 * all1) * (0.5 / period)
                z = 2 * j + p + 1
                hat[z, rows] = jnp.where(marked, value, hat[z, rows])

    def invert(first, count, slot):
        cols = jnp.concatenate([hat[first + i] for i in range(count)], axis=1)
        out = left_product(qy[...], cols)
        out = jnp.concatenate([out[:, i * nx : (i + 1) * nx] for i in range(count)], axis=0)
        out = right_product(out, qx[...])
        for i in range(count):
            phi[slot + i] = out[i * tall : (i + 1) * tall]

    @pl.when(step == 0)
    def _():
        def body(i, carry):
            sweep(pl.multiple_of(i * TILE, TILE), False)
            return carry

        lax.fori_loop(0, ny // TILE, body, 0)
        resting_columns()
        invert(0, 2, 0)

    invert(step * chunk + 2, chunk, 2)

    for i in range(chunk):
        for y0 in range(0, rows_out, TILE):
            rows = pl.ds(y0, TILE)
            layer = i + 1
            here = phi[layer, pl.ds(PAD + y0, TILE)]
            v_out[0, i, rows] = a_in[0, i, rows] - (
                pltpu.roll(here, nx - 1, 1) - pltpu.roll(here, 1, 1)
            )
            v_out[1, i, rows] = a_in[1, i, rows] - (
                phi[layer, pl.ds(PAD + y0 + 1, TILE)] - phi[layer, pl.ds(PAD + y0 - 1, TILE)]
            )
            v_out[2, i, rows] = a_in[2, i, rows] - (
                phi[layer + 1, pl.ds(PAD + y0, TILE)] - phi[layer - 1, pl.ds(PAD + y0, TILE)]
            )
    for i in range(2):
        phi[i] = phi[chunk + i]


def pairs_of(count):
    return [(i, j) for i in range(count) for j in range(i + 1)]


def gram_kernel(count, x_ref, out_ref, acc):
    step = pl.program_id(0)
    rows = x_ref.shape[1]

    @pl.when(step == 0)
    def _():
        acc[...] = jnp.zeros(acc.shape, jnp.float32)

    group = 8
    for bi in range(0, count, group):
        for bj in range(0, bi + 1, group):
            pairs = [
                (i, j)
                for i in range(bi, min(bi + group, count))
                for j in range(bj, min(bj + group, count))
                if j <= i
            ]
            slots = [i * (i + 1) // 2 + j for i, j in pairs]

            def body(t, sums):
                part = pl.ds(pl.multiple_of(t * 8, 8), 8)
                needed = sorted({i for i, _ in pairs} | {j for _, j in pairs})
                tile = {i: x_ref[i, part] for i in needed}
                return tuple(s + tile[i] * tile[j] for s, (i, j) in zip(sums, pairs))

            sums = lax.fori_loop(0, rows // 8, body, tuple(acc[s] for s in slots))
            for s, value in zip(slots, sums):
                acc[s] = value

    @pl.when(step == pl.num_programs(0) - 1)
    def _():
        shape = out_ref.shape
        row = lax.broadcasted_iota(jnp.int32, shape, 0)
        lane = lax.broadcasted_iota(jnp.int32, shape, 1)
        out = jnp.zeros(shape, jnp.float32)
        for s, (i, j) in enumerate(pairs_of(count)):
            total = jnp.sum(jnp.sum(acc[s], axis=0, keepdims=True), axis=1, keepdims=True)
            hit = ((row == i) & (lane == j)) | ((row == j) & (lane == i))
            out = jnp.where(hit, total, out)
        out_ref[...] = out


def ortho_kernel(count, cells, parts_ref, x_ref, out_ref, growth_ref, coef):
    step = pl.program_id(0)
    rows = x_ref.shape[1]

    @pl.when(step == 0)
    def _():
        shape = parts_ref.shape[1:]
        row = lax.broadcasted_iota(jnp.int32, shape, 0)
        lane = lax.broadcasted_iota(jnp.int32, shape, 1)
        work = jnp.sum(parts_ref[...], axis=0) / cells
        work = jnp.where(lane == row + count, 1.0, work)
        for k in range(count - 1):
            pivot = work[k : k + 1, k : k + 1]
            scale = jnp.where(row[:, :1] > k, work[:, k : k + 1] / pivot, 0.0)
            work = work - scale * work[k : k + 1, :]
        diagonal = jnp.sum(jnp.where(lane == row, work, 0.0), axis=1, keepdims=True)
        growth_ref[...] = jnp.broadcast_to(0.5 * jnp.log(diagonal), shape)
        work = work / jnp.sqrt(diagonal)
        for s, (i, j) in enumerate(pairs_of(count)):
            coef[s] = jnp.broadcast_to(
                work[i : i + 1, count + j : count + j + 1], coef.shape[1:]
            )

    def body(t, carry):
        part = pl.ds(pl.multiple_of(t * 16, 16), 16)
        tile = [x_ref[i, part] for i in range(count)]
        for i in range(count):
            total = None
            for j in range(i + 1):
                c = coef[i * (i + 1) // 2 + j]
                term = jnp.concatenate([c, c], axis=0) * tile[j]
                total = term if total is None else total + term
            out_ref[i, part] = total
        return carry

    lax.fori_loop(0, rows // 16, body, 0)


def params(limit=VMEM_BYTES):
    return pltpu.CompilerParams(vmem_limit_bytes=limit)


def whole(shape):
    return pl.BlockSpec(shape, lambda *_: (0,) * len(shape))


ANY = pl.BlockSpec(memory_space=pl.ANY)
SMEM = pl.BlockSpec(memory_space=pltpu.SMEM)


def rates(place, extra, velocity, lo, hi, tables):
    _, layers, ny, nx = velocity.shape
    tangent = extra.ndim == 4
    chunk = 4 if layers % 4 == 0 else 2
    field = pltpu.VMEM((3, layers + 4, ny + 2 * PAD, nx), jnp.float32)
    scratch = [field, field] if tangent else [field]
    scratch += [
        pltpu.VMEM((3, ny, nx), jnp.float32),
        pltpu.VMEM((ny + 2 * PAD, nx), jnp.float32),
        pltpu.VMEM((chunk, ny, nx), jnp.float32),
        pltpu.VMEM((ny, nx), jnp.float32),
        pltpu.SemaphoreType.DMA((layers // chunk, 2)),
        pltpu.SemaphoreType.DMA((2, 4)),
    ]
    size = velocity.size
    return pl.pallas_call(
        functools.partial(rate_kernel, tangent, chunk, layers),
        grid=(layers // chunk,),
        in_specs=[SMEM, ANY if tangent else SMEM, ANY, ANY, ANY]
        + [whole(t.shape) for t in tables],
        out_specs=[
            pl.BlockSpec((3, chunk, ny, nx), lambda g: (0, g, 0, 0)),
            pl.BlockSpec((chunk, ny, nx), lambda g: (g, 0, 0)),
            whole((4, ny, nx)),
        ],
        out_shape=[
            jax.ShapeDtypeStruct(velocity.shape, jnp.float32),
            jax.ShapeDtypeStruct((layers, ny, nx), jnp.float32),
            jax.ShapeDtypeStruct((4, ny, nx), jnp.float32),
        ],
        scratch_shapes=scratch,
        compiler_params=params(),
        cost_estimate=pl.CostEstimate(
            flops=60 * size, bytes_accessed=16 * size, transcendentals=0
        ),
        name="tangent_rates" if tangent else "base_rates",
    )(place, extra, velocity, lo, hi, *tables)


def solve(place, f, sides, totals, wraps, tables, a, rows_out, period, block):
    layers, ny, nx = f.shape
    chunk = 4 if layers % 4 == 0 else 2
    tall = rows_out + 2 * PAD
    moments = whole((4, ny, nx))
    return pl.pallas_call(
        functools.partial(solve_kernel, chunk, layers, period, rows_out),
        grid_spec=pltpu.PrefetchScalarGridSpec(
            num_scalar_prefetch=1,
            grid=(layers // chunk,),
            in_specs=[whole(f.shape), moments, moments, whole((ny, nx)), whole((ny, nx))]
            + [whole(t.shape) for t in tables]
            + [pl.BlockSpec((3, chunk, rows_out, nx), lambda g, p: (0, g, p[1] * block, 0))],
            out_specs=pl.BlockSpec((3, chunk, rows_out, nx), lambda g, p: (0, g, 0, 0)),
            scratch_shapes=[
                pltpu.VMEM((layers, ny, nx), jnp.float32),
                pltpu.VMEM((layers + 2, ny, nx), jnp.float32),
                pltpu.VMEM((chunk + 2, tall, nx), jnp.float32),
            ],
        ),
        out_shape=jax.ShapeDtypeStruct((3, layers, rows_out, nx), jnp.float32),
        compiler_params=params(),
        cost_estimate=pl.CostEstimate(
            flops=40 * a.size, bytes_accessed=12 * a.size, transcendentals=0
        ),
        name="tangent_solve" if rows_out == ny else "base_solve",
    )(place, f, sides, totals, *wraps, *tables, a)


def row_chunk(rows):
    best = 16
    for size in range(16, 200, 16):
        if rows % size == 0:
            best = size
    return best


def gram(cells):
    count, rows, nx = cells.shape
    size = row_chunk(rows)
    tall = max(8, count)
    return pl.pallas_call(
        functools.partial(gram_kernel, count),
        grid=(rows // size,),
        in_specs=[pl.BlockSpec((count, size, nx), lambda g: (0, g, 0))],
        out_specs=whole((tall, nx)),
        out_shape=jax.ShapeDtypeStruct((tall, nx), jnp.float32),
        scratch_shapes=[pltpu.VMEM((count * (count + 1) // 2, 8, nx), jnp.float32)],
        compiler_params=params(),
        cost_estimate=pl.CostEstimate(
            flops=count * cells.size, bytes_accessed=4 * cells.size, transcendentals=0
        ),
        name="gram_parts",
    )(cells)


def ortho(parts, cells, total_cells):
    count, rows, nx = cells.shape
    size = row_chunk(rows)
    return pl.pallas_call(
        functools.partial(ortho_kernel, count, total_cells),
        grid=(rows // size,),
        in_specs=[whole(parts.shape), pl.BlockSpec((count, size, nx), lambda g: (0, g, 0))],
        out_specs=[
            pl.BlockSpec((count, size, nx), lambda g: (0, g, 0)),
            whole(parts.shape[1:]),
        ],
        out_shape=[
            jax.ShapeDtypeStruct(cells.shape, jnp.float32),
            jax.ShapeDtypeStruct(parts.shape[1:], jnp.float32),
        ],
        scratch_shapes=[pltpu.VMEM((count * (count + 1) // 2, 8, nx), jnp.float32)],
        compiler_params=params(),
        cost_estimate=pl.CostEstimate(
            flops=count * cells.size, bytes_accessed=8 * cells.size, transcendentals=0
        ),
        name="ortho_rows",
    )(parts, cells)


def ring_shift(block, shift):
    count = lax.axis_size("gz")
    return lax.ppermute(block, "gz", [(i, (i + shift) % count) for i in range(count)])


def side_sums(moments, slab_power):
    count = lax.axis_size("gz")
    here = lax.axis_index("gz")
    right, left = moments[:2], moments[2:]
    from_left = jnp.zeros_like(right)
    from_right = jnp.zeros_like(left)
    span = 1
    while span < count:
        swapped = lax.ppermute(
            jnp.concatenate([right, left], axis=0), "gz", [(i, i ^ span) for i in range(count)]
        )
        other_right, other_left = swapped[:2], swapped[2:]
        inside = here % span
        upper = (here // span) % 2 == 1
        to_left = slab_power(inside)
        to_right = slab_power(span - 1 - inside)
        from_left = jnp.where(upper, from_left + to_left * other_right, from_left)
        from_right = jnp.where(upper, from_right, from_right + to_right * other_left)
        across = slab_power(span)
        right = jnp.where(upper, right + across * other_right, other_right + across * right)
        left = jnp.where(upper, other_left + across * left, left + across * other_left)
        span *= 2
    return jnp.concatenate([from_left, from_right], axis=0), jnp.concatenate([right, left], axis=0)


def per_device(base_flow, tangents, shells):
    _, layers, ny, nx = base_flow.shape
    slabs = lax.axis_size("gz")
    vectors = lax.axis_size("vec")
    here = lax.axis_index("gz")
    mine = lax.axis_index("vec")
    nz = slabs * layers
    period = nz // 2
    tangent = tangents[0]

    basis_x, sines_x = real_basis(nx)
    basis_y, sines_y = real_basis(ny)
    decay64, green64, resting = column_tables(sines_y, sines_x)
    decay = jnp.asarray(decay64, jnp.float32)
    green = jnp.asarray(green64, jnp.float32)
    mark = jnp.asarray(resting, jnp.float32)
    slab_log = jnp.asarray((layers // 2) * np.log(decay64), jnp.float32)
    closing = jnp.asarray(
        np.where(resting, 0.0, 1.0 / np.where(resting, 1.0, 1.0 - decay64**period)), jnp.float32
    )

    def slab_power(exponent):
        return jnp.exp(jnp.asarray(exponent).astype(jnp.float32) * slab_log)

    wraps = (closing * slab_power(here), closing * slab_power(slabs - 1 - here))
    qx_forward = jnp.asarray(right_table(basis_x))
    qy_forward = jnp.asarray(left_table(basis_y.T))
    qx_inverse = jnp.asarray(right_table(basis_x.T))
    rows_out = ny // vectors

    def rows_table(first, count):
        high, low = halves(np.concatenate([basis_y, basis_y, basis_y], axis=0))
        both = []
        for part in (high, low):
            part = lax.dynamic_slice_in_dim(jnp.asarray(part), ny + first - PAD, count + 2 * PAD, 0)
            both.append(jnp.concatenate([part, part], axis=1))
        return jnp.concatenate(both, axis=0)

    def edge(near, far):
        return jnp.concatenate(
            [base_flow[:, near], tangent[:, near], base_flow[2:, far], tangent[2:, far]], axis=0
        )

    lo = ring_shift(edge(layers - 1, layers - 2), 1)
    hi = ring_shift(edge(0, 1), -1)

    rows_run = max(rows_out, TILE)
    block = mine * rows_out // rows_run
    place = jnp.stack([here, block]).astype(jnp.int32)
    rate_tables = (decay, mark, qx_forward, qy_forward)
    a, f, moments = rates(place, tangent, base_flow, lo, hi, rate_tables)
    sides, totals = side_sums(moments, slab_power)
    tables = (decay, green, mark, rows_table(0, ny), qx_inverse)
    advanced = solve(place, f, sides, totals, wraps, tables, a, ny, period, 0)

    piece_rows = 3 * layers * ny // vectors
    cells = lax.all_to_all(
        advanced.reshape(vectors, piece_rows, nx), "vec", split_axis=0, concat_axis=0, tiled=True
    )

    positions = (here * layers + jnp.arange(layers, dtype=jnp.int32)) % nz
    angles = 2.0 * math.pi / nz * (shells[:, None] * positions[None, :] % nz).astype(jnp.float32)
    profile = time_step * forcing_amplitude * jnp.sum(jnp.sin(angles), axis=0)
    base_a, base_f, base_moments = rates(place, profile, base_flow, lo, hi, rate_tables)
    base_sides, base_totals = side_sums(base_moments, slab_power)
    tables = (decay, green, mark, rows_table(block * rows_run, rows_run), qx_inverse)
    base_rows = solve(
        place, base_f, base_sides, base_totals, wraps, tables, base_a, rows_run, period, 1
    )
    if rows_run != rows_out:
        base_rows = lax.dynamic_slice_in_dim(
            base_rows, mine * rows_out - block * rows_run, rows_out, 2
        )

    part = gram(cells)
    devices = slabs * vectors
    if devices <= 64:
        parts = lax.all_to_all(
            jnp.broadcast_to(part[None], (devices,) + part.shape),
            ("vec", "gz"),
            split_axis=0,
            concat_axis=0,
            tiled=True,
        )
    else:
        parts = lax.psum(part, ("vec", "gz"))[None]
    ortho_cells, growth = ortho(parts, cells, 3.0 * nz * ny * nx)
    returned = lax.all_to_all(ortho_cells, "vec", split_axis=0, concat_axis=0, tiled=True)
    return (base_rows, returned.reshape(tangents.shape), growth[:vectors, 0])


def solution(mesh):
    in_specs = (P(None, "gz", None, None), P("vec", None, "gz", None, None), P())
    out_specs = (P(None, "gz", "vec", None), P("vec", None, "gz", None, None), P())
    return jax.shard_map(
        per_device, mesh=mesh, in_specs=in_specs, out_specs=out_specs, check_vma=False
    )
```

time: 1010 us -> 413 us (0.41)
  other arithmetic: 319 us -> 1.36 us
  local copies, waits for them, and re-layouts: 207 us -> 13.4 us
  matrix products: 90.8 us -> 0 us
  Pallas kernels: 0 us -> 82.6 us
  blocking collectives: 185 us -> 155 us
  waiting for transfers between devices: 169 us -> 147 us
  starting transfers between devices: 27.6 us -> 10.8 us
    unnamed x9 -> x0, other arithmetic: 149 us -> none
    div x8 -> x0, other arithmetic: 91.1 us -> none  [the longest x1 47.4 us: tendencies(): (jnp.roll(interior, -1, 3) - jnp.roll(interior, 1, 3)) / (2.0 * spacing)]
    pallas_call x0 -> x6, Pallas kernels: none -> 82.6 us  [the longest x2 45.2 us: rates(): pl.pallas_call(functools.partial(rate_kernel, tangent, chunk, layers), gr...]
    dot_general x25 -> x0, matrix products: 78.9 us -> none  [the longest x1 14.5 us: per_device(): partial_gram = jnp.dot(cell_columns, cell_columns.T, precision=highest)]
    unnamed x64 -> x27, local copies, waits for them, and re-layouts: 66.2 us -> 9.83 us
    slice x11 -> x1, local copies, waits for them, and re-layouts: 54.8 us -> 0.62 us  [per_device(): return (base_rows, returned.reshape(tangents.shape), growth[:vectors, 0])]
    all_to_all x5 -> x1, waiting for transfers between devices: 165 us -> 121 us  [per_device(): lax.all_to_all(ortho_cells, 'vec', split_axis=0, concat_axis=0, tiled=True)]
    psum x1 -> x0, blocking collectives: 39.3 us -> none  [per_device(): gram_matrix = lax.psum(partial_gram, ('vec', 'gz')) / (3.0 * NZ * NY * NX)]
  transfers between devices with their start and end apart: 11 -> 7, of which waited for: 5 -> 6; matrix products, arithmetic and copies ran while one was open for 23% -> 1% of each run, Pallas kernels for 0% -> 6%
where the time goes in v1:
time: 413 us; the launch traced here: 412 us
  blocking collectives  155 us (38%)
  waiting for transfers between devices  147 us (36%)
  Pallas kernels  82.6 us (20%)
  local copies, waits for them, and re-layouts  13.4 us (3%)
  starting transfers between devices  10.8 us (3%)
    all_to_all x1, blocking collectives, per_device(): lax.all_to_all(advanced.reshape(vectors, piece_rows, nx), 'vec', split_ax...  144 us
    all_to_all x1, waiting for transfers between devices, per_device(): lax.all_to_all(ortho_cells, 'vec', split_axis=0, concat_axis=0, tiled=True)  121 us
    pallas_call x2, Pallas kernels, rates(): pl.pallas_call(functools.partial(rate_kernel, tangent, chunk, layers), gr...  45.2 us
    pallas_call x2, Pallas kernels, solve(): pl.pallas_call(functools.partial(solve_kernel, chunk, layers, period, row...  20.4 us
    ppermute x4, waiting for transfers between devices, side_sums(): lax.ppermute(jnp.concatenate([right, left], axis=0), 'gz', [(i, i ^ span)...  15.2 us
    all_to_all x1, blocking collectives, per_device(): lax.all_to_all(jnp.broadcast_to(part[None], (devices,) + part.shape), ('v...  11.3 us
    ppermute x2, waiting for transfers between devices, ring_shift(): lax.ppermute(block, 'gz', [(i, (i + shift) % count) for i in range(count)])  11.3 us
    unnamed x27, local copies, waits for them, and re-layouts  9.83 us
  transfers between devices with their start and end apart: 7, of which 6 were waited for; matrix products, arithmetic and copies ran while one was open for 1% of the time, Pallas kernels for 6%

profile of v1, /device:TPU:0, one launch (start us, length us, event | category | flops | bytes accessed | tf_op | source)
XLA Modules:
  0.0 411.5 jit_solution(1502533513013487874)
XLA Ops:
  0.6 1.0 slice_bitcast_fusion.4
  1.6 1.3 slice_bitcast_fusion
  2.9 0.5 collective-permute-start
  3.5 2.0 collective-permute-start.1
  5.5 0.1 pad_add_fusion.refs_0_
  5.5 0.8 fusion.3
  6.3 8.7 %collective-permute-done.refs_3_ = f32[8,128,128]{2,1,0:T(8,128)S(1)} collective-permute-done((f32[8,128,128]{2,1,0:T(8,128)S(1)}, f32[8,128,128]{2,1,0:T(8,128)S(1)}, u32[]{:S(2)}, u32[]{:S(2)}) %collective-permute-start) | collective-permute-done | bytes 524320 | tf_op jit(solution)/shard_map/ppermute | solution.py:583
  15.1 2.6 collective-permute-done.1.refs_4_
  17.7 0.0 copy-start
  17.7 0.8 copy-done
  18.5 0.0 copy-start.2
  18.5 0.8 copy-done.2
  19.3 0.0 copy-start.5
  19.3 0.9 copy-done.5
  20.2 0.0 copy-start.6
  20.2 0.9 copy-done.6
  21.1 0.0 copy-start.1
  21.1 29.1 %tangent_rates.1 = (f32[3,32,128,128]{3,2,1,0:T(8,128)}, f32[32,128,128]{2,1,0:T(8,128)}, f32[4,128,128]{2,1,0:T(8,128)S(1)}) custom-call(s32[2]{0:T(128)S(1)} %pad_add_fusion.refs_0_, f32[3,32,128,128]{3,2,1,0:T(8,128)} %bitcast.28, f32[3,32,128,128]{3,2,1,0:T(8,128)} %refs_2_.3, f32[8,128,128]{2,1,0:T(8,128)S(1)} %collective-permute-done.refs_3_, ...), custom_call_target="tpu_custom_call" | custom-call | flops 94371840 | bytes 25165824 | tf_op jit(solution)/shard_map/tangent_rates/pallas_call | solution.py:477
  50.3 0.0 copy-start.10
  50.3 0.0 copy-start.11
  50.3 0.0 copy-start.12
  50.3 0.0 copy-start.9
  50.3 0.0 copy-start.3
  50.3 0.0 copy-start.4
  50.3 0.0 copy-start.7
  50.3 0.0 copy-start.8
  50.4 0.1 collective-permute-start.4
  50.4 0.0 copy-done.1
  50.4 16.1 %base_rates.1 = (f32[3,32,128,128]{3,2,1,0:T(8,128)}, f32[32,128,128]{2,1,0:T(8,128)}, f32[4,128,128]{2,1,0:T(8,128)S(1)}) custom-call(s32[2]{0:T(128)S(1)} %pad_add_fusion.refs_0_, f32[32]{0:T(128)S(1)} %broadcast_multiply_fusion.refs_1_, f32[3,32,128,128]{3,2,1,0:T(8,128)} %refs_2_.3, f32[8,128,128]{2,1,0:T(8,128)S(1)} %collective-permute-done.refs_3_, ...), custom_call_target="tpu_custom_call" | custom-call | flops 94371840 | bytes 25165824 | tf_op jit(solution)/shard_map/base_rates/pallas_call | solution.py:477
  66.5 0.5 collective-permute-start.2
  67.0 0.0 collective-permute-done.4
  67.0 1.2 collective-permute-done.2
  68.2 0.0 copy-done.10
  68.2 0.1 add_select_fusion.7
  68.3 2.4 collective-permute-start.5
  70.8 0.0 copy-done.11
  70.8 0.0 copy-done.12
  70.8 6.8 %collective-permute-done.5 = f32[4,128,128]{2,1,0:T(8,128)S(1)} collective-permute-done((f32[4,128,128]{2,1,0:T(8,128)S(1)}, f32[4,128,128]{2,1,0:T(8,128)S(1)}, u32[]{:S(2)}, u32[]{:S(2)}) %collective-permute-start.5) | collective-permute-done | bytes 262176 | tf_op jit(solution)/shard_map/ppermute | solution.py:594
  77.6 0.0 copy-done.9
  77.6 0.1 add_select_fusion.5
  77.7 0.0 copy-done.3
  77.8 0.0 copy-done.4
  77.8 0.0 copy-done.7
  77.8 0.0 copy-done.8
  77.8 11.5 %tangent_solve.1 = f32[3,32,128,128]{3,2,1,0:T(8,128)} custom-call(s32[2]{0:T(128)S(1)} %pad_add_fusion.refs_0_, f32[32,128,128]{2,1,0:T(8,128)} %get-tuple-element.14.refs_1_, f32[4,128,128]{2,1,0:T(8,128)S(1)} %pad_maximum_fusion.6.refs_2_, f32[4,128,128]{2,1,0:T(8,128)S(1)} %pad_maximum_fusion.7.refs_3_, f32[128,128]{1,0:T(8,128)S(1)} %get-tuple-element.44.refs_4_, ...), custom_call_target="tpu_custom_call" | custom-call | flops 62914560 | bytes 18874368 | tf_op jit(solution)/shard_map/tangent_solve/pallas_call | solution.py:506
  89.3 144.0 %all_to_all.15.x_ref = f32[8,1536,128]{2,1,0:T(8,128)} all-to-all(f32[8,1536,128]{2,1,0:T(8,128)} %bitcast.25), channel_id=1, replica_groups=mesh['vec'=8,'gz'=4] {'vec'}, dimensions={0} | all-to-all | bytes 12582912 | tf_op jit(solution)/shard_map/all_to_all | solution.py:667
  233.3 7.3 %gram_parts.1 = f32[8,128]{1,0:T(8,128)S(1)} custom-call(f32[8,1536,128]{2,1,0:T(8,128)} %all_to_all.15.x_ref), custom_call_target="tpu_custom_call" | custom-call | flops 12582912 | bytes 6291456 | tf_op jit(solution)/shard_map/gram_parts/pallas_call | solution.py:542
  240.7 11.3 %all_to_all.16.parts_ref = f32[32,8,128]{2,1,0:T(8,128)S(1)} all-to-all(f32[32,8,128]{2,1,0:T(8,128)S(1)} %broadcast_in_dim.2), channel_id=1, replica_groups=mesh['vec'=8,'gz'=4] {'vec','gz'}, dimensions={0} | all-to-all | bytes 262144 | tf_op jit(solution)/shard_map/all_to_all | solution.py:688
  252.0 9.7 %ortho_rows.1 = (f32[8,1536,128]{2,1,0:T(8,128)}, f32[8,128]{1,0:T(8,128)S(1)}) custom-call(f32[32,8,128]{2,1,0:T(8,128)S(1)} %all_to_all.16.parts_ref, f32[8,1536,128]{2,1,0:T(8,128)} %all_to_all.15.x_ref), custom_call_target="tpu_custom_call" | custom-call | flops 12582912 | bytes 12582912 | tf_op jit(solution)/shard_map/ortho_rows/pallas_call | solution.py:560
  261.7 4.8 %all-to-all-start.2 = ((f32[8,1536,128]{2,1,0:T(8,128)}), f32[8,1536,128]{2,1,0:T(8,128)}, u32[]{:S(2)}, u32[]{:S(2)}) async-start(f32[8,1536,128]{2,1,0:T(8,128)} %get-tuple-element.17), calls=%async_computation.2 | async-start | bytes 12582912 | tf_op jit(solution)/shard_map/all_to_all | solution.py:698
  266.5 0.5 collective-permute-start.3
  267.0 0.7 constant_dynamic-slice_fusion
  267.7 7.3 %collective-permute-done.3 = f32[4,128,128]{2,1,0:T(8,128)S(1)} collective-permute-done((f32[4,128,128]{2,1,0:T(8,128)S(1)}, f32[4,128,128]{2,1,0:T(8,128)S(1)}, u32[]{:S(2)}, u32[]{:S(2)}) %collective-permute-start.3) | collective-permute-done | bytes 262176 | tf_op jit(solution)/shard_map/ppermute | solution.py:594
  275.0 0.1 add_select_fusion.9
  275.1 8.9 %base_solve.1 = f32[3,32,16,128]{3,2,1,0:T(8,128)} custom-call(s32[2]{0:T(128)S(1)} %pad_add_fusion.refs_0_, f32[32,128,128]{2,1,0:T(8,128)} %get-tuple-element.11.refs_1_, f32[4,128,128]{2,1,0:T(8,128)S(1)} %pad_maximum_fusion.3.refs_2_, f32[4,128,128]{2,1,0:T(8,128)S(1)} %pad_maximum_fusion.4.refs_3_, f32[128,128]{1,0:T(8,128)S(1)} %get-tuple-element.44.refs_4_, ...), custom_call_target="tpu_custom_call" | custom-call | flops 62914560 | bytes 18874368 | tf_op jit(solution)/shard_map/base_solve/pallas_call | solution.py:506
  284.0 0.6 slice_reduce_fusion
  284.6 120.6 %all-to-all-done.2 = f32[8,1536,128]{2,1,0:T(8,128)} async-done(((f32[8,1536,128]{2,1,0:T(8,128)}), f32[8,1536,128]{2,1,0:T(8,128)}, u32[]{:S(2)}, u32[]{:S(2)}) %all-to-all-start.2) | async-done | bytes 6291488 | tf_op jit(solution)/shard_map/all_to_all | solution.py:698
  405.2 6.3 %copy.27 = f32[1,3,32,128,128]{4,3,2,1,0:T(8,128)} copy(f32[1,3,32,128,128]{4,3,2,1,0:T(8,128)} %bitcast.12) | data formatting | bytes 12582912
  (13 shorter events, 0.3 us)
Async XLA Ops:
  2.9 12.2 %collective-permute-start = (f32[8,128,128]{2,1,0:T(8,128)S(1)}, f32[8,128,128]{2,1,0:T(8,128)S(1)}, u32[]{:S(2)}, u32[]{:S(2)}) collective-permute-start(f32[8,128,128]{2,1,0:T(8,128)S(1)} %pad_maximum_fusion), channel_id=1, source_target_pairs={{0,1},{1,2},{2,3},{3,0},{4,5},{5,6},{6,7},{7,4},{8,9},{9,10},{10,1... | collective-permute-start | bytes 1572872 | tf_op jit(solution)/shard_map/ppermute | solution.py:583
  3.5 14.2 %collective-permute-start.1 = (f32[8,128,128]{2,1,0:T(8,128)S(1)}, f32[8,128,128]{2,1,0:T(8,128)S(1)}, u32[]{:S(2)}, u32[]{:S(2)}) collective-permute-start(f32[8,128,128]{2,1,0:T(8,128)S(1)} %pad_maximum_fusion.1), channel_id=1, source_target_pairs={{0,3},{1,0},{2,1},{3,2},{4,7},{5,4},{6,5},{7,6},{8,11},{9,8},{10,9... | collective-permute-start | bytes 1572872 | tf_op jit(solution)/shard_map/ppermute | solution.py:583
  17.7 0.8 copy-start
  18.5 0.8 copy-start.2
  19.3 0.9 copy-start.5
  20.2 0.9 copy-start.6
  21.1 29.3 %copy-start.1 = (f32[128,128]{1,0:T(8,128)S(1)}, f32[128,128]{1,0:T(8,128)}, u32[]{:S(2)}) copy-start(f32[128,128]{1,0:T(8,128)} %constant.147.clone.refs_5_.refs_6_) | copy-start | bytes 196612
  50.3 18.0 %copy-start.10 = (f32[128,128]{1,0:T(8,128)S(1)}, f32[128,128]{1,0:T(8,128)}, u32[]{:S(2)}) copy-start(f32[128,128]{1,0:T(8,128)} %constant.160) | copy-start | bytes 196612
  50.3 20.5 %copy-start.11 = (f32[128,128]{1,0:T(8,128)S(1)}, f32[128,128]{1,0:T(8,128)}, u32[]{:S(2)}) copy-start(f32[128,128]{1,0:T(8,128)} %constant.151.clone) | copy-start | bytes 196612
  50.3 20.5 %copy-start.12 = (f32[128,128]{1,0:T(8,128)S(1)}, f32[128,128]{1,0:T(8,128)}, u32[]{:S(2)}) copy-start(f32[128,128]{1,0:T(8,128)} %constant.150.clone) | copy-start | bytes 196612
  50.3 27.3 %copy-start.9 = (f32[128,128]{1,0:T(8,128)S(1)}, f32[128,128]{1,0:T(8,128)}, u32[]{:S(2)}) copy-start(f32[128,128]{1,0:T(8,128)} %constant.162) | copy-start | bytes 196612
  50.3 27.4 %copy-start.3 = (f32[128,128]{1,0:T(8,128)S(1)}, f32[128,128]{1,0:T(8,128)}, u32[]{:S(2)}) copy-start(f32[128,128]{1,0:T(8,128)} %constant.149.clone.refs_6_.refs_8_) | copy-start | bytes 196612
  50.3 27.4 %copy-start.4 = (bf16[256,256]{1,0:T(8,128)(2,1)S(1)}, bf16[256,256]{1,0:T(8,128)(2,1)}, u32[]{:S(2)}) copy-start(bf16[256,256]{1,0:T(8,128)(2,1)} %constant.154.clone.refs_10_) | copy-start | bytes 393220
  50.3 27.4 %copy-start.7 = (f32[128,128]{1,0:T(8,128)S(1)}, f32[128,128]{1,0:T(8,128)}, u32[]{:S(2)}) copy-start(f32[128,128]{1,0:T(8,128)} %constant.148.clone.refs_7_) | copy-start | bytes 196612
  50.3 27.4 %copy-start.8 = (bf16[288,256]{1,0:T(8,128)(2,1)S(1)}, bf16[288,256]{1,0:T(8,128)(2,1)}, u32[]{:S(2)}) copy-start(bf16[288,256]{1,0:T(8,128)(2,1)} %constant.167.refs_9_) | copy-start | bytes 442372
  50.4 16.7 %collective-permute-start.4 = (f32[4,128,128]{2,1,0:T(8,128)S(1)}, f32[4,128,128]{2,1,0:T(8,128)S(1)}, u32[]{:S(2)}, u32[]{:S(2)}) collective-permute-start(f32[4,128,128]{2,1,0:T(8,128)S(1)} %get-tuple-element.15), channel_id=1, source_target_pairs={{0,1},{1,0},{2,3},{3,2},{4,5},{5,4},{6,7},{7,6},{8,9},{9,8},{10,11... | collective-permute-start | bytes 786440 | tf_op jit(solution)/shard_map/ppermute | solution.py:594
  66.5 1.7 collective-permute-start.2
  68.3 9.3 %collective-permute-start.5 = (f32[4,128,128]{2,1,0:T(8,128)S(1)}, f32[4,128,128]{2,1,0:T(8,128)S(1)}, u32[]{:S(2)}, u32[]{:S(2)}) collective-permute-start(f32[4,128,128]{2,1,0:T(8,128)S(1)} %pad_maximum_fusion.5), channel_id=1, source_target_pairs={{0,2},{1,3},{2,0},{3,1},{4,6},{5,7},{6,4},{7,5},{8,10},{9,11},{10,... | collective-permute-start | bytes 786440 | tf_op jit(solution)/shard_map/ppermute | solution.py:594
  261.7 143.5 %all-to-all-start.2 = ((f32[8,1536,128]{2,1,0:T(8,128)}), f32[8,1536,128]{2,1,0:T(8,128)}, u32[]{:S(2)}, u32[]{:S(2)}) async-start(f32[8,1536,128]{2,1,0:T(8,128)} %get-tuple-element.17), calls=%async_computation.2 | async-start | bytes 12582912 | tf_op jit(solution)/shard_map/all_to_all | solution.py:698
  266.5 8.5 %collective-permute-start.3 = (f32[4,128,128]{2,1,0:T(8,128)S(1)}, f32[4,128,128]{2,1,0:T(8,128)S(1)}, u32[]{:S(2)}, u32[]{:S(2)}) collective-permute-start(f32[4,128,128]{2,1,0:T(8,128)S(1)} %pad_maximum_fusion.2), channel_id=1, source_target_pairs={{0,2},{1,3},{2,0},{3,1},{4,6},{5,7},{6,4},{7,5},{8,10},{9,11},{10,... | collective-permute-start | bytes 786440 | tf_op jit(solution)/shard_map/ppermute | solution.py:594

commit v2 on v1

--- a/solution.py
+++ b/solution.py
@@ -14,9 +14,11 @@
 viscosity = 0.01
 forcing_amplitude = 4.0
 
-TILE = 16
+TILE = 64
+SWEEP = 32
+LEAST = 16
 PAD = 8
-VMEM_BYTES = 52 * 1024 * 1024
+MIB = 1024 * 1024
 
 
 def spacing_of(nx):
@@ -60,8 +62,7 @@
     four = 4.0 * (sines_y[:, None] + sines_x[None, :])
     resting = four == 0.0
     decay = 1.0 / (1.0 + four / 2.0 + np.sqrt(four + four * four / 4.0))
-    green = np.where(resting, 0.0, -decay / np.where(resting, 1.0, 1.0 - decay * decay))
-    return decay, green, resting
+    return decay, resting
 
 
 def split_cat(data, axis):
@@ -82,20 +83,121 @@
     return out[:height] + out[height:]
 
 
-def rate_kernel(tangent, chunk, layers, *refs):
+def power_of(base, exponent):
+    out = None
+    while exponent > 0:
+        if exponent % 2 == 1:
+            out = base if out is None else out * base
+        base = base * base
+        exponent //= 2
+    return out
+
+
+def wrap_rows(ref, index, ny):
+    ref[index + (pl.ds(0, PAD),)] = ref[index + (pl.ds(ny, PAD),)]
+    ref[index + (pl.ds(ny + PAD, PAD),)] = ref[index + (pl.ds(PAD, PAD),)]
+
+
+def halo_pairs(source, fields, near, far, inner, sems, side):
+    out = []
+    for i, (_, ref) in enumerate(fields):
+        out += [
+            pltpu.make_async_copy(
+                source.at[pl.ds(3 * i, 3)], ref.at[:, near, inner], sems.at[side, 2 * i]
+            ),
+            pltpu.make_async_copy(source.at[6 + i], ref.at[2, far, inner], sems.at[side, 2 * i + 1]),
+        ]
+    return out
+
+
+def rate_tile(us, vs, layer, y0, comps):
+    nx = vs.shape[3]
+    space = spacing_of(nx)
+    adv_scale = -time_step / (2.0 * space)
+    lap_scale = viscosity * time_step / (space * space)
+    rows = pl.ds(PAD + y0, TILE)
+    flow = [vs[c, layer, rows] for c in range(3)]
+    drift = flow if us is None else [us[c, layer, rows] for c in range(3)]
+    out = []
+
+    def neighbours(ref, c, centre):
+        return (
+            pltpu.roll(centre, nx - 1, 1),
+            pltpu.roll(centre, 1, 1),
+            ref[c, layer, pl.ds(PAD + y0 + 1, TILE)],
+            ref[c, layer, pl.ds(PAD + y0 - 1, TILE)],
+            ref[c, layer + 1, rows],
+            ref[c, layer - 1, rows],
+        )
+
+    for c in comps:
+        xp, xm, yp, ym, zp, zm = neighbours(vs if us is None else us, c, drift[c])
+        adv = flow[0] * (xp - xm) + flow[1] * (yp - ym) + flow[2] * (zp - zm)
+        lap = ((xp + xm) + (yp + ym)) + ((zp + zm) - 6.0 * drift[c])
+        if us is not None:
+            xp, xm, yp, ym, zp, zm = neighbours(vs, c, flow[c])
+            adv = adv + (drift[0] * (xp - xm) + drift[1] * (yp - ym) + drift[2] * (zp - zm))
+        out.append(adv_scale * adv + lap_scale * lap)
+    return drift, out
+
+
+def z_rate(fns, layer, slot):
+    us, vs, rz = fns[:3]
+    for y0 in range(0, rz.shape[1], TILE):
+        _, (rate,) = rate_tile(us, vs, layer, y0, (2,))
+        rz[slot, pl.ds(y0, TILE)] = rate
+
+
+def layer_rates(fns, layer, i, shift):
+    us, vs, rz, ry, dv, a_out = fns
+    ny, nx = rz.shape[1:]
+    for y0 in range(0, ny, TILE):
+        rows = pl.ds(y0, TILE)
+        drift, (rate_x, rate_y) = rate_tile(us, vs, layer, y0, (0, 1))
+        if shift is not None:
+            rate_x = rate_x + shift
+        a_out[0, i, rows] = drift[0] + rate_x
+        a_out[1, i, rows] = drift[1] + rate_y
+        a_out[2, i, rows] = drift[2] + rz[1, rows]
+        dv[i, rows] = pltpu.roll(rate_x, nx - 1, 1) - pltpu.roll(rate_x, 1, 1)
+        ry[pl.ds(PAD + y0, TILE)] = rate_y
+    z_rate(fns, layer + 1, 2)
+    wrap_rows(ry, (), ny)
+    for y0 in range(0, ny, TILE):
+        rows = pl.ds(y0, TILE)
+        along_y = ry[pl.ds(PAD + y0 + 1, TILE)] - ry[pl.ds(PAD + y0 - 1, TILE)]
+        middle, upper = rz[1, rows], rz[2, rows]
+        along_z = upper - rz[0, rows]
+        dv[i, rows] = dv[i, rows] + (along_y + along_z)
+        rz[0, rows] = middle
+        rz[1, rows] = upper
+
+
+def transform(dv, f_out, basis, chunk):
+    ny, nx = dv.shape[1:]
+    qx, qy = basis.at[pl.ds(0, 2 * nx)], basis.at[pl.ds(2 * nx, 2 * ny)]
+    waves = right_product(dv[...].reshape(chunk * ny, nx), qx[...]).reshape(chunk, ny, nx)
+    waves = left_product(qy[...], jnp.concatenate([waves[i] for i in range(chunk)], axis=1))
+    for i in range(chunk):
+        f_out[i] = waves[:, i * nx : (i + 1) * nx]
+
+
+def rate_kernel(tangent, halos, chunk, layers, *refs):
     if tangent:
-        (place, u_hbm, v_hbm, lo_hbm, hi_hbm, decay, mark, qx, qy) = refs[:9]
-        (a_out, f_out, m_out, us, vs, rz, ry, dv, pw, sems, halo_sems) = refs[9:]
+        (place, u_hbm, v_hbm), refs = refs[:3], refs[3:]
     else:
-        (place, profile, v_hbm, lo_hbm, hi_hbm, decay, mark, qx, qy) = refs[:9]
-        (a_out, f_out, m_out, vs, rz, ry, dv, pw, sems, halo_sems) = refs[9:]
+        (place, profile, v_hbm), refs = refs[:3], refs[3:]
+    if halos:
+        (lo_hbm, hi_hbm), refs = refs[:2], refs[2:]
+    (decay, basis, a_out, f_out, m_out), refs = refs[:5], refs[5:]
+    if tangent:
+        us, refs = refs[0], refs[1:]
+    (vs, rz, ry, dv, pw, sems, halo_sems) = refs
+    if not tangent:
         us = vs
     step = pl.program_id(0)
     steps = layers // chunk
-    ny, nx = f_out.shape[1], f_out.shape[2]
-    space = spacing_of(nx)
-    adv_scale = -time_step / (2.0 * space)
-    lap_scale = viscosity * time_step / (space * space)
+    ny = f_out.shape[1]
     fields = [(v_hbm, vs)]
     if tangent:
         fields.append((u_hbm, us))
@@ -114,171 +216,184 @@
     def halo_copies(side):
         source = (lo_hbm, hi_hbm)[side]
         near, far = ((1, 0), (layers + 2, layers + 3))[side]
-        out = [
-            pltpu.make_async_copy(
-                source.at[pl.ds(0, 3)], vs.at[:, near, inner], halo_sems.at[side, 0]
-            ),
-            pltpu.make_async_copy(source.at[6], vs.at[2, far, inner], halo_sems.at[side, 1]),
-        ]
-        if tangent:
-            out += [
-                pltpu.make_async_copy(
-                    source.at[pl.ds(3, 3)], us.at[:, near, inner], halo_sems.at[side, 2]
-                ),
-                pltpu.make_async_copy(source.at[7], us.at[2, far, inner], halo_sems.at[side, 3]),
-            ]
-        return out
-
-    def wrap_rows(ref, index):
-        ref[index + (pl.ds(0, PAD),)] = ref[index + (pl.ds(ny, PAD),)]
-        ref[index + (pl.ds(ny + PAD, PAD),)] = ref[index + (pl.ds(PAD, PAD),)]
-
-    def wrap_layers(first, count):
+        return halo_pairs(source, fields, near, far, inner, halo_sems, side)
+
+    def wait_chunk(k):
+        for copy in chunk_copies(k):
+            copy.wait()
+
         def body(i, carry):
             for _, ref in fields:
                 for c in range(3):
-                    wrap_rows(ref, (c, first + i))
+                    wrap_rows(ref, (c, k * chunk + 2 + i), ny)
             return carry
 
-        lax.fori_loop(0, count, body, 0)
-
-    def wait_chunk(k):
-        for copy in chunk_copies(k):
-            copy.wait()
-        wrap_layers(k * chunk + 2, chunk)
+        lax.fori_loop(0, chunk, body, 0)
 
     def wait_halo(side):
         for copy in halo_copies(side):
             copy.wait()
         near, far = ((1, 0), (layers + 2, layers + 3))[side]
-        wrap_layers(near, 1)
         for _, ref in fields:
-            wrap_rows(ref, (2, far))
-
-    def rate_tile(layer, y0, comps):
-        rows = pl.ds(PAD + y0, TILE)
-        flow = [vs[c, layer, rows] for c in range(3)]
-        drift = [us[c, layer, rows] for c in range(3)] if tangent else flow
-        out = []
-
-        def neighbours(ref, c, centre):
-            return (
-                pltpu.roll(centre, nx - 1, 1),
-                pltpu.roll(centre, 1, 1),
-                ref[c, layer, pl.ds(PAD + y0 + 1, TILE)],
-                ref[c, layer, pl.ds(PAD + y0 - 1, TILE)],
-                ref[c, layer + 1, rows],
-                ref[c, layer - 1, rows],
-            )
-
-        for c in comps:
-            xp, xm, yp, ym, zp, zm = neighbours(us, c, drift[c])
-            adv = flow[0] * (xp - xm) + flow[1] * (yp - ym) + flow[2] * (zp - zm)
-            lap = ((xp + xm) + (yp + ym)) + ((zp + zm) - 6.0 * drift[c])
-            if tangent:
-                xp, xm, yp, ym, zp, zm = neighbours(vs, c, flow[c])
-                adv = adv + (
-                    drift[0] * (xp - xm) + drift[1] * (yp - ym) + drift[2] * (zp - zm)
-                )
-            out.append(adv_scale * adv + lap_scale * lap)
-        return drift, out
-
-    def z_rate(layer, slot):
-        for y0 in range(0, ny, TILE):
-            _, (rate,) = rate_tile(layer, y0, (2,))
-            rz[slot, pl.ds(y0, TILE)] = rate
+            for c in range(3):
+                wrap_rows(ref, (c, near), ny)
+            wrap_rows(ref, (2, far), ny)
+
+    fns = (us if tangent else None, vs, rz, ry, dv, a_out)
 
     @pl.when(step == 0)
     def _():
-        for copy in halo_copies(0):
-            copy.start()
+        if halos:
+            for copy in halo_copies(0):
+                copy.start()
         for k in range(steps):
             for copy in chunk_copies(k):
                 copy.start()
-        for copy in halo_copies(1):
-            copy.start()
-        wait_halo(0)
+        if halos:
+            for copy in halo_copies(1):
+                copy.start()
+            wait_halo(0)
         wait_chunk(0)
-        if steps == 1:
-            wait_halo(1)
-        z_rate(1, 0)
-        z_rate(2, 1)
+        if halos:
+            if steps == 1:
+                wait_halo(1)
+            z_rate(fns, 1, 0)
+            z_rate(fns, 2, 1)
         m_out[...] = jnp.zeros(m_out.shape, jnp.float32)
         start = (place[0] * (layers // 2)).astype(jnp.float32)
-        pw[...] = jnp.where(mark[...] > 0.0, start, 1.0)
+        pw[...] = jnp.where(decay[...] >= 1.0, start, 1.0)
 
     @pl.when(step + 1 < steps)
     def _():
         wait_chunk(step + 1)
 
-    if steps > 1:
+    if halos and steps > 1:
 
         @pl.when(step + 1 == steps)
         def _():
             wait_halo(1)
 
-    def layer_body(i, carry):
-        layer = step * chunk + i + 2
+    for i in range(chunk):
+        shift = None if tangent else profile[step * chunk + i]
+        layer_rates(fns, step * chunk + i + 2, i, shift)
+    transform(dv, f_out, basis, chunk)
+
+    def moments(first, last):
         for y0 in range(0, ny, TILE):
             rows = pl.ds(y0, TILE)
-            drift, (rate_x, rate_y) = rate_tile(layer, y0, (0, 1))
-            if not tangent:
-                rate_x = rate_x + profile[step * chunk + i]
-            a_out[0, i, rows] = drift[0] + rate_x
-            a_out[1, i, rows] = drift[1] + rate_y
-            a_out[2, i, rows] = drift[2] + rz[1, rows]
-            dv[i, rows] = pltpu.roll(rate_x, nx - 1, 1) - pltpu.roll(rate_x, 1, 1)
-            ry[pl.ds(PAD + y0, TILE)] = rate_y
-        z_rate(layer + 1, 2)
-        wrap_rows(ry, ())
-        for y0 in range(0, ny, TILE):
-            rows = pl.ds(y0, TILE)
-            along_y = ry[pl.ds(PAD + y0 + 1, TILE)] - ry[pl.ds(PAD + y0 - 1, TILE)]
-            middle, upper = rz[1, rows], rz[2, rows]
-            along_z = upper - rz[0, rows]
-            dv[i, rows] = dv[i, rows] + (along_y + along_z)
-            rz[0, rows] = middle
-            rz[1, rows] = upper
-        return carry
-
-    lax.fori_loop(0, chunk, layer_body, 0)
-
-    waves = right_product(dv[...].reshape(chunk * ny, nx), qx[...]).reshape(chunk, ny, nx)
-    waves = left_product(qy[...], jnp.concatenate([waves[i] for i in range(chunk)], axis=1))
-    for i in range(chunk):
-        f_out[i] = waves[:, i * nx : (i + 1) * nx]
-    for y0 in range(0, ny, TILE):
-        rows = pl.ds(y0, TILE)
-        rate = decay[rows]
-        marks = mark[rows]
-        power = pw[rows]
-        right = [m_out[0, rows], m_out[1, rows]]
-        left = [m_out[2, rows], m_out[3, rows]]
-        for i in range(chunk):
-            f = f_out[i, rows]
-            parity = i % 2
-            right[parity] = rate * right[parity] + f
-            left[parity] = left[parity] + power * f
-            if parity == 1:
-                power = rate * power + marks
-        pw[rows] = power
-        m_out[0, rows], m_out[1, rows] = right
-        m_out[2, rows], m_out[3, rows] = left
+            rate = decay[rows]
+            marks = jnp.where(rate >= 1.0, 1.0, 0.0)
+            power = pw[rows]
+            right = [m_out[0, rows], m_out[1, rows]]
+            left = [m_out[2, rows], m_out[3, rows]]
+            for i in range(chunk):
+                parity = i % 2
+                if first <= i < last:
+                    f = f_out[i, rows]
+                    right[parity] = rate * right[parity] + f
+                    left[parity] = left[parity] + power * f
+                if parity == 1:
+                    power = rate * power + marks
+            pw[rows] = power
+            m_out[0, rows], m_out[1, rows] = right
+            m_out[2, rows], m_out[3, rows] = left
+
+    if halos:
+        moments(0, chunk)
+    else:
+        @pl.when(step == 0)
+        def _():
+            moments(2, chunk)
+
+        @pl.when((step > 0) & (step + 1 < steps))
+        def _():
+            moments(0, chunk)
+
+        @pl.when(step + 1 == steps)
+        def _():
+            moments(0, chunk - 2)
+
+
+def edge_kernel(layers, *refs):
+    (place, u_hbm, v_hbm, lo_hbm, hi_hbm, a_in, f_in, m_in, decay, basis) = refs[:10]
+    (a_out, f_out, m_out, us, vs, rz, ry, dv, sems, halo_sems) = refs[10:]
+    step = pl.program_id(0)
+    ny = f_out.shape[1]
+    fields = [(v_hbm, vs), (u_hbm, us)]
+    inner = pl.ds(PAD, ny)
+
+    def copies(side):
+        source = (lo_hbm, hi_hbm)[side]
+        near, far = ((1, 0), (10, 11))[side]
+        first, slot = ((0, 2), (layers - 4, 6))[side]
+        return halo_pairs(source, fields, near, far, inner, halo_sems, side) + [
+            pltpu.make_async_copy(
+                ref.at[:, pl.ds(first, 4)], target.at[:, pl.ds(slot, 4), inner], sems.at[side, i]
+            )
+            for i, (ref, target) in enumerate(fields)
+        ]
+
+    def arrive(side):
+        for copy in copies(side):
+            copy.wait()
+        near, far = ((1, 0), (10, 11))[side]
+        for _, ref in fields:
+            for layer in range(6 * side, 6 * side + 6):
+                for c in range(3):
+                    if layer != far or c == 2:
+                        wrap_rows(ref, (c, layer), ny)
+
+    @pl.when(step == 0)
+    def _():
+        for side in range(2):
+            for copy in copies(side):
+                copy.start()
+        arrive(0)
+
+    @pl.when(step == 1)
+    def _():
+        arrive(1)
+
+    fns = (us, vs, rz, ry, dv, a_out)
+    top = step * 6 + 2
+    z_rate(fns, top - 1, 0)
+    z_rate(fns, top, 1)
+    for i in range(2):
+        layer_rates(fns, top + i, i, None)
+    transform(dv, f_out, basis, 2)
+    half = layers // 2
+    start = place[0] * half
+    last = power_of(decay[...], half - 1)
+
+    @pl.when(step == 0)
+    def _():
+        weight = jnp.where(decay[...] >= 1.0, start.astype(jnp.float32), 1.0)
+        for p in range(2):
+            m_out[p] = decay[...] * m_in[p] + last * f_out[p]
+            m_out[2 + p] = m_in[2 + p] + weight * f_out[p]
+
+    @pl.when(step == 1)
+    def _():
+        weight = jnp.where(decay[...] >= 1.0, (start + half - 1).astype(jnp.float32), last)
+        for p in range(2):
+            m_out[p] = m_out[p] + f_out[p]
+            m_out[2 + p] = m_out[2 + p] + weight * f_out[p]
 
 
 def solve_kernel(chunk, layers, period, rows_out, *refs):
-    (place, f_in, sides, totals, wrap_l, wrap_r, decay, green, mark, qy, qx, a_in) = refs[:12]
-    (v_out, qm, hat, phi) = refs[12:]
+    (place, f_in, sides, totals, wrap_l, wrap_r, decay, basis, a_in) = refs[:9]
+    (v_out, qm, hat, phi) = refs[9:]
     step = pl.program_id(0)
     ny, nx = f_in.shape[1], f_in.shape[2]
     tall = rows_out + 2 * PAD
     half = layers // 2
-
-    def sweep(y0, resting):
-        size = PAD if resting else TILE
-        rows = pl.ds(y0, size)
+    qx, qy = basis.at[pl.ds(0, 2 * nx)], basis.at[pl.ds(2 * nx, 2 * tall)]
+
+    def sweep(y0):
+        rows = pl.ds(y0, SWEEP)
         rate = decay[rows]
-        factor = green[rows]
+        resting = rate >= 1.0
+        factor = jnp.where(resting, 0.0, -rate / jnp.where(resting, 1.0, 1.0 - rate * rate))
         left = [sides[p, rows] + wrap_l[rows] * totals[p, rows] for p in range(2)]
         right = [sides[2 + p, rows] + wrap_r[rows] * totals[2 + p, rows] for p in range(2)]
         back = list(right)
@@ -296,7 +411,7 @@
 
     def resting_columns():
         rows = pl.ds(0, PAD)
-        marked = mark[rows] > 0.0
+        marked = decay[rows] >= 1.0
         start = place[0] * half
         for p in range(2):
             own0 = jnp.zeros((PAD, nx), jnp.float32)
@@ -336,28 +451,29 @@
     @pl.when(step == 0)
     def _():
         def body(i, carry):
-            sweep(pl.multiple_of(i * TILE, TILE), False)
+            sweep(pl.multiple_of(i * SWEEP, SWEEP))
             return carry
 
-        lax.fori_loop(0, ny // TILE, body, 0)
+        lax.fori_loop(0, ny // SWEEP, body, 0)
         resting_columns()
         invert(0, 2, 0)
 
     invert(step * chunk + 2, chunk, 2)
 
     for i in range(chunk):
-        for y0 in range(0, rows_out, TILE):
-            rows = pl.ds(y0, TILE)
+        size = min(TILE, rows_out)
+        for y0 in range(0, rows_out, size):
+            rows = pl.ds(y0, size)
             layer = i + 1
-            here = phi[layer, pl.ds(PAD + y0, TILE)]
+            here = phi[layer, pl.ds(PAD + y0, size)]
             v_out[0, i, rows] = a_in[0, i, rows] - (
                 pltpu.roll(here, nx - 1, 1) - pltpu.roll(here, 1, 1)
             )
             v_out[1, i, rows] = a_in[1, i, rows] - (
-                phi[layer, pl.ds(PAD + y0 + 1, TILE)] - phi[layer, pl.ds(PAD + y0 - 1, TILE)]
+                phi[layer, pl.ds(PAD + y0 + 1, size)] - phi[layer, pl.ds(PAD + y0 - 1, size)]
             )
             v_out[2, i, rows] = a_in[2, i, rows] - (
-                phi[layer + 1, pl.ds(PAD + y0, TILE)] - phi[layer - 1, pl.ds(PAD + y0, TILE)]
+                phi[layer + 1, pl.ds(PAD + y0, size)] - phi[layer - 1, pl.ds(PAD + y0, size)]
             )
     for i in range(2):
         phi[i] = phi[chunk + i]
@@ -392,7 +508,7 @@
                 tile = {i: x_ref[i, part] for i in needed}
                 return tuple(s + tile[i] * tile[j] for s, (i, j) in zip(sums, pairs))
 
-            sums = lax.fori_loop(0, rows // 8, body, tuple(acc[s] for s in slots))
+            sums = lax.fori_loop(0, rows // 8, body, tuple(acc[s] for s in slots), unroll=4)
             for s, value in zip(slots, sums):
                 acc[s] = value
 
@@ -404,8 +520,8 @@
         out = jnp.zeros(shape, jnp.float32)
         for s, (i, j) in enumerate(pairs_of(count)):
             total = jnp.sum(jnp.sum(acc[s], axis=0, keepdims=True), axis=1, keepdims=True)
-            hit = ((row == i) & (lane == j)) | ((row == j) & (lane == i))
-            out = jnp.where(hit, total, out)
+            for at in {i * count + j, j * count + i}:
+                out = jnp.where((row == at // shape[1]) & (lane == at % shape[1]), total, out)
         out_ref[...] = out
 
 
@@ -415,11 +531,18 @@
 
     @pl.when(step == 0)
     def _():
-        shape = parts_ref.shape[1:]
+        nx = x_ref.shape[2]
+        shape = (max(8, count), nx)
         row = lax.broadcasted_iota(jnp.int32, shape, 0)
         lane = lax.broadcasted_iota(jnp.int32, shape, 1)
-        work = jnp.sum(parts_ref[...], axis=0) / cells
-        work = jnp.where(lane == row + count, 1.0, work)
+        flat = jnp.sum(parts_ref[...], axis=0) / cells
+        work = jnp.where(lane == row + count, 1.0, 0.0)
+        for i in range(count):
+            at, shift = i * count // nx, i * count % nx
+            line = flat[at : at + 1]
+            if shift > 0:
+                line = pltpu.roll(line, nx - shift, 1)
+            work = jnp.where((row == i) & (lane < count), line, work)
         for k in range(count - 1):
             pivot = work[k : k + 1, k : k + 1]
             scale = jnp.where(row[:, :1] > k, work[:, k : k + 1] / pivot, 0.0)
@@ -444,11 +567,11 @@
             out_ref[i, part] = total
         return carry
 
-    lax.fori_loop(0, rows // 16, body, 0)
-
-
-def params(limit=VMEM_BYTES):
-    return pltpu.CompilerParams(vmem_limit_bytes=limit)
+    lax.fori_loop(0, rows // 16, body, 0, unroll=2)
+
+
+def params(limit):
+    return pltpu.CompilerParams(vmem_limit_bytes=limit * MIB)
 
 
 def whole(shape):
@@ -459,7 +582,7 @@
 SMEM = pl.BlockSpec(memory_space=pltpu.SMEM)
 
 
-def rates(place, extra, velocity, lo, hi, tables):
+def rates(place, extra, velocity, halos, tables):
     _, layers, ny, nx = velocity.shape
     tangent = extra.ndim == 4
     chunk = 4 if layers % 4 == 0 else 2
@@ -475,9 +598,10 @@
     ]
     size = velocity.size
     return pl.pallas_call(
-        functools.partial(rate_kernel, tangent, chunk, layers),
+        functools.partial(rate_kernel, tangent, len(halos) > 0, chunk, layers),
         grid=(layers // chunk,),
-        in_specs=[SMEM, ANY if tangent else SMEM, ANY, ANY, ANY]
+        in_specs=[SMEM, ANY if tangent else SMEM, ANY]
+        + [ANY for _ in halos]
         + [whole(t.shape) for t in tables],
         out_specs=[
             pl.BlockSpec((3, chunk, ny, nx), lambda g: (0, g, 0, 0)),
@@ -490,12 +614,48 @@
             jax.ShapeDtypeStruct((4, ny, nx), jnp.float32),
         ],
         scratch_shapes=scratch,
-        compiler_params=params(),
+        compiler_params=params(52),
         cost_estimate=pl.CostEstimate(
             flops=60 * size, bytes_accessed=16 * size, transcendentals=0
         ),
         name="tangent_rates" if tangent else "base_rates",
-    )(place, extra, velocity, lo, hi, *tables)
+    )(place, extra, velocity, *halos, *tables)
+
+
+def edge_rates(place, tangent, velocity, halos, a, f, moments, tables):
+    _, layers, ny, nx = velocity.shape
+    field = pltpu.VMEM((3, 12, ny + 2 * PAD, nx), jnp.float32)
+    ends = layers // 2 - 1
+    return pl.pallas_call(
+        functools.partial(edge_kernel, layers),
+        grid=(2,),
+        in_specs=[SMEM] + [ANY] * 6 + [whole(t.shape) for t in (moments, *tables)],
+        out_specs=[
+            pl.BlockSpec((3, 2, ny, nx), lambda g: (0, g * ends, 0, 0)),
+            pl.BlockSpec((2, ny, nx), lambda g: (g * ends, 0, 0)),
+            whole((4, ny, nx)),
+        ],
+        out_shape=[
+            jax.ShapeDtypeStruct(a.shape, jnp.float32),
+            jax.ShapeDtypeStruct(f.shape, jnp.float32),
+            jax.ShapeDtypeStruct(moments.shape, jnp.float32),
+        ],
+        scratch_shapes=[
+            field,
+            field,
+            pltpu.VMEM((3, ny, nx), jnp.float32),
+            pltpu.VMEM((ny + 2 * PAD, nx), jnp.float32),
+            pltpu.VMEM((2, ny, nx), jnp.float32),
+            pltpu.SemaphoreType.DMA((2, 2)),
+            pltpu.SemaphoreType.DMA((2, 4)),
+        ],
+        input_output_aliases={5: 0, 6: 1},
+        compiler_params=params(52),
+        cost_estimate=pl.CostEstimate(
+            flops=60 * 12 * ny * nx, bytes_accessed=160 * ny * nx, transcendentals=0
+        ),
+        name="tangent_edges",
+    )(place, tangent, velocity, *halos, a, f, moments, *tables)
 
 
 def solve(place, f, sides, totals, wraps, tables, a, rows_out, period, block):
@@ -519,7 +679,7 @@
             ],
         ),
         out_shape=jax.ShapeDtypeStruct((3, layers, rows_out, nx), jnp.float32),
-        compiler_params=params(),
+        compiler_params=params(52),
         cost_estimate=pl.CostEstimate(
             flops=40 * a.size, bytes_accessed=12 * a.size, transcendentals=0
         ),
@@ -529,7 +689,7 @@
 
 def row_chunk(rows):
     best = 16
-    for size in range(16, 200, 16):
+    for size in range(16, 800, 16):
         if rows % size == 0:
             best = size
     return best
@@ -538,7 +698,7 @@
 def gram(cells):
     count, rows, nx = cells.shape
     size = row_chunk(rows)
-    tall = max(8, count)
+    tall = -(-count * count // nx)
     return pl.pallas_call(
         functools.partial(gram_kernel, count),
         grid=(rows // size,),
@@ -546,7 +706,7 @@
         out_specs=whole((tall, nx)),
         out_shape=jax.ShapeDtypeStruct((tall, nx), jnp.float32),
         scratch_shapes=[pltpu.VMEM((count * (count + 1) // 2, 8, nx), jnp.float32)],
-        compiler_params=params(),
+        compiler_params=params(12),
         cost_estimate=pl.CostEstimate(
             flops=count * cells.size, bytes_accessed=4 * cells.size, transcendentals=0
         ),
@@ -563,14 +723,14 @@
         in_specs=[whole(parts.shape), pl.BlockSpec((count, size, nx), lambda g: (0, g, 0))],
         out_specs=[
             pl.BlockSpec((count, size, nx), lambda g: (0, g, 0)),
-            whole(parts.shape[1:]),
+            whole((max(8, count), nx)),
         ],
         out_shape=[
             jax.ShapeDtypeStruct(cells.shape, jnp.float32),
-            jax.ShapeDtypeStruct(parts.shape[1:], jnp.float32),
+            jax.ShapeDtypeStruct((max(8, count), nx), jnp.float32),
         ],
         scratch_shapes=[pltpu.VMEM((count * (count + 1) // 2, 8, nx), jnp.float32)],
-        compiler_params=params(),
+        compiler_params=params(20),
         cost_estimate=pl.CostEstimate(
             flops=count * cells.size, bytes_accessed=8 * cells.size, transcendentals=0
         ),
@@ -620,10 +780,8 @@
 
     basis_x, sines_x = real_basis(nx)
     basis_y, sines_y = real_basis(ny)
-    decay64, green64, resting = column_tables(sines_y, sines_x)
+    decay64, resting = column_tables(sines_y, sines_x)
     decay = jnp.asarray(decay64, jnp.float32)
-    green = jnp.asarray(green64, jnp.float32)
-    mark = jnp.asarray(resting, jnp.float32)
     slab_log = jnp.asarray((layers // 2) * np.log(decay64), jnp.float32)
     closing = jnp.asarray(
         np.where(resting, 0.0, 1.0 / np.where(resting, 1.0, 1.0 - decay64**period)), jnp.float32
@@ -633,18 +791,17 @@
         return jnp.exp(jnp.asarray(exponent).astype(jnp.float32) * slab_log)
 
     wraps = (closing * slab_power(here), closing * slab_power(slabs - 1 - here))
-    qx_forward = jnp.asarray(right_table(basis_x))
-    qy_forward = jnp.asarray(left_table(basis_y.T))
+    forward = jnp.asarray(np.concatenate([right_table(basis_x), left_table(basis_y.T)], axis=0))
     qx_inverse = jnp.asarray(right_table(basis_x.T))
     rows_out = ny // vectors
 
-    def rows_table(first, count):
+    def inverse_tables(first, count):
         high, low = halves(np.concatenate([basis_y, basis_y, basis_y], axis=0))
-        both = []
+        both = [qx_inverse]
         for part in (high, low):
             part = lax.dynamic_slice_in_dim(jnp.asarray(part), ny + first - PAD, count + 2 * PAD, 0)
             both.append(jnp.concatenate([part, part], axis=1))
-        return jnp.concatenate(both, axis=0)
+        return (decay, jnp.concatenate(both, axis=0))
 
     def edge(near, far):
         return jnp.concatenate(
@@ -654,14 +811,16 @@
     lo = ring_shift(edge(layers - 1, layers - 2), 1)
     hi = ring_shift(edge(0, 1), -1)
 
-    rows_run = max(rows_out, TILE)
+    rows_run = max(rows_out, LEAST)
     block = mine * rows_out // rows_run
     place = jnp.stack([here, block]).astype(jnp.int32)
-    rate_tables = (decay, mark, qx_forward, qy_forward)
-    a, f, moments = rates(place, tangent, base_flow, lo, hi, rate_tables)
+    rate_tables = (decay, forward)
+    a, f, moments = rates(place, tangent, base_flow, (), rate_tables)
+    a, f, moments = edge_rates(place, tangent, base_flow, (lo, hi), a, f, moments, rate_tables)
     sides, totals = side_sums(moments, slab_power)
-    tables = (decay, green, mark, rows_table(0, ny), qx_inverse)
+    tables = inverse_tables(0, ny)
     advanced = solve(place, f, sides, totals, wraps, tables, a, ny, period, 0)
+    advanced, base_lo, base_hi = lax.optimization_barrier((advanced, lo, hi))
 
     piece_rows = 3 * layers * ny // vectors
     cells = lax.all_to_all(
@@ -671,9 +830,9 @@
     positions = (here * layers + jnp.arange(layers, dtype=jnp.int32)) % nz
     angles = 2.0 * math.pi / nz * (shells[:, None] * positions[None, :] % nz).astype(jnp.float32)
     profile = time_step * forcing_amplitude * jnp.sum(jnp.sin(angles), axis=0)
-    base_a, base_f, base_moments = rates(place, profile, base_flow, lo, hi, rate_tables)
+    base_a, base_f, base_moments = rates(place, profile, base_flow, (base_lo, base_hi), rate_tables)
     base_sides, base_totals = side_sums(base_moments, slab_power)
-    tables = (decay, green, mark, rows_table(block * rows_run, rows_run), qx_inverse)
+    tables = inverse_tables(block * rows_run, rows_run)
     base_rows = solve(
         place, base_f, base_sides, base_totals, wraps, tables, base_a, rows_run, period, 1
     )
@@ -682,6 +841,7 @@
             base_rows, mine * rows_out - block * rows_run, rows_out, 2
         )
 
+    cells, base_rows = lax.optimization_barrier((cells, base_rows))
     part = gram(cells)
     devices = slabs * vectors
     if devices <= 64:
@@ -695,8 +855,9 @@
     else:
         parts = lax.psum(part, ("vec", "gz"))[None]
     ortho_cells, growth = ortho(parts, cells, 3.0 * nz * ny * nx)
+    ortho_cells, growth = lax.optimization_barrier((ortho_cells, growth[:vectors, 0]))
     returned = lax.all_to_all(ortho_cells, "vec", split_axis=0, concat_axis=0, tiled=True)
-    return (base_rows, returned.reshape(tangents.shape), growth[:vectors, 0])
+    return (base_rows, returned.reshape(tangents.shape), growth)
 
 
 def solution(mesh):

time: 413 us -> 363 us (0.88)
  waiting for transfers between devices: 147 us -> 121 us
  Pallas kernels: 82.6 us -> 67.8 us
  local copies, waits for them, and re-layouts: 13.4 us -> 8.14 us
    all_to_all x1, waiting for transfers between devices: 121 us -> 105 us  [per_device(): lax.all_to_all(advanced.reshape(vectors, piece_rows, nx), 'vec', split_ax...]
    ppermute x2, waiting for transfers between devices: 11.3 us -> 0.01 us  [ring_shift(): lax.ppermute(block, 'gz', [(i, (i + shift) % count) for i in range(count)])]
    pallas_call x2 -> x3, Pallas kernels: 45.2 us -> 37.7 us  [the longest x2 32.2 us: rates(): pl.pallas_call(functools.partial(rate_kernel, tangent, len(halos) > 0, ch...]
    unnamed x27 -> x23, local copies, waits for them, and re-layouts: 9.83 us -> 4.54 us
    pallas_call x1, Pallas kernels: 9.68 us -> 5.32 us  [ortho(): pl.pallas_call(functools.partial(ortho_kernel, count, total_cells), grid=...]
  transfers between devices with their start and end apart: 7 -> 7, of which waited for: 6 -> 5; matrix products, arithmetic and copies ran while one was open for 1% -> 0% of each run, Pallas kernels for 6% -> 11%
where the time goes in v2:
time: 363 us; the launch traced here: 362 us
  blocking collectives  151 us (42%)
  waiting for transfers between devices  121 us (33%)
  Pallas kernels  67.8 us (19%)
  starting transfers between devices  12.3 us (3%)
  local copies, waits for them, and re-layouts  8.14 us (2%)
    all_to_all x1, blocking collectives, per_device(): lax.all_to_all(ortho_cells, 'vec', split_axis=0, concat_axis=0, tiled=True)  141 us
    all_to_all x1, waiting for transfers between devices, per_device(): lax.all_to_all(advanced.reshape(vectors, piece_rows, nx), 'vec', split_ax...  105 us
    pallas_call x2, Pallas kernels, rates(): pl.pallas_call(functools.partial(rate_kernel, tangent, len(halos) > 0, ch...  32.2 us
    pallas_call x2, Pallas kernels, solve(): pl.pallas_call(functools.partial(solve_kernel, chunk, layers, period, row...  20.3 us
    ppermute x4, waiting for transfers between devices, side_sums(): lax.ppermute(jnp.concatenate([right, left], axis=0), 'gz', [(i, i ^ span)...  15.9 us
    all_to_all x1, blocking collectives, per_device(): lax.all_to_all(jnp.broadcast_to(part[None], (devices,) + part.shape), ('v...  10.6 us
  transfers between devices with their start and end apart: 7, of which 5 were waited for; matrix products, arithmetic and copies ran while one was open for 0% of the time, Pallas kernels for 11%

profile of v2, /device:TPU:0, one launch (start us, length us, event | category | flops | bytes accessed | tf_op | source)
XLA Modules:
  0.0 362.3 jit_solution(6378695149444831271)
XLA Ops:
  0.6 1.3 slice_bitcast_fusion
  1.9 1.0 slice_bitcast_fusion.4
  2.9 2.4 collective-permute-start.1
  5.4 0.1 collective-permute-start
  5.5 0.1 pad_add_fusion.refs_0_
  5.5 0.0 copy-start
  5.5 0.9 copy-done
  6.5 0.0 copy-start.2
  6.5 0.8 copy-done.2
  7.3 0.0 copy-start.1
  7.3 18.5 %tangent_rates.1 = (f32[3,32,128,128]{3,2,1,0:T(8,128)}, f32[32,128,128]{2,1,0:T(8,128)}, f32[4,128,128]{2,1,0:T(8,128)S(1)}) custom-call(s32[2]{0:T(128)S(1)} %pad_add_fusion.refs_0_, f32[3,32,128,128]{3,2,1,0:T(8,128)} %bitcast.29, f32[3,32,128,128]{3,2,1,0:T(8,128)} %refs_2_.5, f32[128,128]{1,0:T(8,128)S(1)} %copy-done.2, bf16[512,256]{1,0:T(8,128)(2,1)S(1)} %copy-done), custom_call_target="tpu_custom_call" | custom-call | flops 94371840 | bytes 25165824 | tf_op jit(solution)/shard_map/tangent_rates/pallas_call | solution.py:600
  25.8 0.0 collective-permute-done.1.refs_4_
  25.8 0.0 collective-permute-done.refs_3_
  25.8 0.0 copy-done.1
  25.8 0.0 copy-start.6
  25.8 0.0 copy-start.8
  25.9 0.0 copy-start.9
  25.9 0.0 copy-start.5
  25.9 0.0 copy-start.3
  25.9 0.0 copy-start.4
  25.9 5.6 %tangent_edges.1 = (f32[3,32,128,128]{3,2,1,0:T(8,128)}, f32[32,128,128]{2,1,0:T(8,128)}, f32[4,128,128]{2,1,0:T(8,128)S(1)}) custom-call(s32[2]{0:T(128)S(1)} %pad_add_fusion.refs_0_, f32[3,32,128,128]{3,2,1,0:T(8,128)} %bitcast.30, f32[3,32,128,128]{3,2,1,0:T(8,128)} %refs_2_.5, ...), custom_call_target="tpu_custom_call", output_to_operand_aliasing={{0}: (5, {}), {1}: (6, {})} | custom-call | flops 11796480 | bytes 2621440 | tf_op jit(solution)/shard_map/tangent_edges/pallas_call | solution.py:629
  31.5 0.7 collective-permute-start.2
  32.2 1.2 collective-permute-done.2
  33.4 0.0 copy-done.6
  33.5 1.5 collective-permute-start.3
  35.0 0.0 copy-done.8
  35.0 0.0 copy-done.9
  35.0 7.1 %collective-permute-done.3 = f32[4,128,128]{2,1,0:T(8,128)S(1)} collective-permute-done((f32[4,128,128]{2,1,0:T(8,128)S(1)}, f32[4,128,128]{2,1,0:T(8,128)S(1)}, u32[]{:S(2)}, u32[]{:S(2)}) %collective-permute-start.3) | collective-permute-done | bytes 262176 | tf_op jit(solution)/shard_map/ppermute | solution.py:754
  42.1 0.0 copy-done.5
  42.1 0.1 add_select_fusion.9
  42.3 0.0 copy-done.3
  42.3 0.0 copy-done.4
  42.3 11.5 %tangent_solve.1 = f32[3,32,128,128]{3,2,1,0:T(8,128)} custom-call(s32[2]{0:T(128)S(1)} %pad_add_fusion.refs_0_, f32[32,128,128]{2,1,0:T(8,128)} %get-tuple-element.24.refs_1_, f32[4,128,128]{2,1,0:T(8,128)S(1)} %pad_maximum_fusion.3.refs_2_, f32[4,128,128]{2,1,0:T(8,128)S(1)} %pad_maximum_fusion.4.refs_3_, f32[128,128]{1,0:T(8,128)S(1)} %get-tuple-element.64.refs_4_, ...), custom_call_target="tpu_custom_call" | custom-call | flops 62914560 | bytes 18874368 | tf_op jit(solution)/shard_map/tangent_solve/pallas_call | solution.py:666
  53.8 0.0 copy-start.10
  53.8 6.0 %all-to-all-start = ((f32[8,1536,128]{2,1,0:T(8,128)}), f32[8,1536,128]{2,1,0:T(8,128)}, u32[]{:S(2)}, u32[]{:S(2)}) async-start(f32[8,1536,128]{2,1,0:T(8,128)} %bitcast.32), calls=%async_computation | async-start | bytes 12582912 | tf_op jit(solution)/shard_map/all_to_all | solution.py:826
  59.7 0.0 copy-start.7
  59.8 0.0 copy-done.10
  59.8 0.1 fusion.3
  59.9 13.7 %base_rates.1 = (f32[3,32,128,128]{3,2,1,0:T(8,128)}, f32[32,128,128]{2,1,0:T(8,128)}, f32[4,128,128]{2,1,0:T(8,128)S(1)}) custom-call(s32[2]{0:T(128)S(1)} %pad_add_fusion.refs_0_, f32[32]{0:T(128)S(1)} %broadcast_multiply_fusion.refs_1_, f32[3,32,128,128]{3,2,1,0:T(8,128)} %refs_2_.5, f32[8,128,128]{2,1,0:T(8,128)S(1)} %collective-permute-done.refs_3_, ...), custom_call_target="tpu_custom_call" | custom-call | flops 94371840 | bytes 25165824 | tf_op jit(solution)/shard_map/base_rates/pallas_call | solution.py:600
  73.6 0.1 collective-permute-start.4
  73.7 1.5 collective-permute-done.4
  75.2 0.1 add_select_fusion.7
  75.3 1.5 collective-permute-start.5
  76.8 0.7 constant_dynamic-slice_fusion
  77.5 0.0 copy-done.7
  77.6 6.2 %collective-permute-done.5 = f32[4,128,128]{2,1,0:T(8,128)S(1)} collective-permute-done((f32[4,128,128]{2,1,0:T(8,128)S(1)}, f32[4,128,128]{2,1,0:T(8,128)S(1)}, u32[]{:S(2)}, u32[]{:S(2)}) %collective-permute-start.5) | collective-permute-done | bytes 262176 | tf_op jit(solution)/shard_map/ppermute | solution.py:754
  83.7 0.1 add_select_fusion.5
  83.9 8.8 %base_solve.1 = f32[3,32,16,128]{3,2,1,0:T(8,128)} custom-call(s32[2]{0:T(128)S(1)} %pad_add_fusion.refs_0_, f32[32,128,128]{2,1,0:T(8,128)} %get-tuple-element.30.refs_1_, f32[4,128,128]{2,1,0:T(8,128)S(1)} %pad_maximum_fusion.6.refs_2_, f32[4,128,128]{2,1,0:T(8,128)S(1)} %pad_maximum_fusion.7.refs_3_, f32[128,128]{1,0:T(8,128)S(1)} %get-tuple-element.64.refs_4_, ...), custom_call_target="tpu_custom_call" | custom-call | flops 62914560 | bytes 18874368 | tf_op jit(solution)/shard_map/base_solve/pallas_call | solution.py:666
  92.7 105.0 %all-to-all-done.x_ref = f32[8,1536,128]{2,1,0:T(8,128)} async-done(((f32[8,1536,128]{2,1,0:T(8,128)}), f32[8,1536,128]{2,1,0:T(8,128)}, u32[]{:S(2)}, u32[]{:S(2)}) %all-to-all-start) | async-done | bytes 6291488 | tf_op jit(solution)/shard_map/all_to_all | solution.py:826
  197.7 4.5 %gram_parts.1 = f32[1,128]{1,0:T(1,128)S(1)} custom-call(f32[8,1536,128]{2,1,0:T(8,128)} %all-to-all-done.x_ref), custom_call_target="tpu_custom_call" | custom-call | flops 12582912 | bytes 6291456 | tf_op jit(solution)/shard_map/gram_parts/pallas_call | solution.py:702
  202.2 10.6 %all_to_all.15.parts_ref = f32[32,1,128]{2,1,0:T(1,128)S(1)} all-to-all(f32[32,1,128]{2,1,0:T(1,128)S(1)} %broadcast_in_dim.5), channel_id=1, replica_groups=mesh['vec'=8,'gz'=4] {'vec','gz'}, dimensions={0} | all-to-all | bytes 32768 | tf_op jit(solution)/shard_map/all_to_all | solution.py:848
  212.7 5.3 %ortho_rows.1 = (f32[8,1536,128]{2,1,0:T(8,128)S(1)}, f32[8,128]{1,0:T(8,128)S(1)}) custom-call(f32[32,1,128]{2,1,0:T(1,128)S(1)} %all_to_all.15.parts_ref, f32[8,1536,128]{2,1,0:T(8,128)} %all-to-all-done.x_ref), custom_call_target="tpu_custom_call" | custom-call | flops 12582912 | bytes 12582912 | tf_op jit(solution)/shard_map/ortho_rows/pallas_call | solution.py:720
  218.1 0.6 slice_reduce_fusion
  218.7 140.9 %all_to_all.16 = f32[8,1536,128]{2,1,0:T(8,128)S(1)} all-to-all(f32[8,1536,128]{2,1,0:T(8,128)S(1)} %get-tuple-element.37), channel_id=1, replica_groups=mesh['vec'=8,'gz'=4] {'vec'}, dimensions={0} | all-to-all | bytes 12582912 | tf_op jit(solution)/shard_map/all_to_all | solution.py:859
  359.6 2.7 copy.28
  (14 shorter events, 0.3 us)
Async XLA Ops:
  2.9 22.9 %collective-permute-start.1 = (f32[8,128,128]{2,1,0:T(8,128)S(1)}, f32[8,128,128]{2,1,0:T(8,128)S(1)}, u32[]{:S(2)}, u32[]{:S(2)}) collective-permute-start(f32[8,128,128]{2,1,0:T(8,128)S(1)} %pad_maximum_fusion.1), channel_id=1, source_target_pairs={{0,3},{1,0},{2,1},{3,2},{4,7},{5,4},{6,5},{7,6},{8,11},{9,8},{10,9... | collective-permute-start | bytes 1572872 | tf_op jit(solution)/shard_map/ppermute | solution.py:743
  5.4 20.4 %collective-permute-start = (f32[8,128,128]{2,1,0:T(8,128)S(1)}, f32[8,128,128]{2,1,0:T(8,128)S(1)}, u32[]{:S(2)}, u32[]{:S(2)}) collective-permute-start(f32[8,128,128]{2,1,0:T(8,128)S(1)} %pad_maximum_fusion), channel_id=1, source_target_pairs={{0,1},{1,2},{2,3},{3,0},{4,5},{5,6},{6,7},{7,4},{8,9},{9,10},{10,1... | collective-permute-start | bytes 1572872 | tf_op jit(solution)/shard_map/ppermute | solution.py:743
  5.5 1.0 copy-start
  6.5 0.8 copy-start.2
  7.3 18.5 %copy-start.1 = (bf16[512,256]{1,0:T(8,128)(2,1)S(1)}, bf16[512,256]{1,0:T(8,128)(2,1)}, u32[]{:S(2)}) copy-start(bf16[512,256]{1,0:T(8,128)(2,1)} %constant.144.clone.refs_4_.refs_9_.refs_6_) | copy-start | bytes 786436
  25.8 7.5 %copy-start.6 = (f32[128,128]{1,0:T(8,128)S(1)}, f32[128,128]{1,0:T(8,128)}, u32[]{:S(2)}) copy-start(f32[128,128]{1,0:T(8,128)} %constant.151) | copy-start | bytes 196612
  25.8 9.1 %copy-start.8 = (f32[128,128]{1,0:T(8,128)S(1)}, f32[128,128]{1,0:T(8,128)}, u32[]{:S(2)}) copy-start(f32[128,128]{1,0:T(8,128)} %constant.142.clone) | copy-start | bytes 196612
  25.9 9.1 %copy-start.9 = (f32[128,128]{1,0:T(8,128)S(1)}, f32[128,128]{1,0:T(8,128)}, u32[]{:S(2)}) copy-start(f32[128,128]{1,0:T(8,128)} %constant.143.clone) | copy-start | bytes 196612
  25.9 16.2 %copy-start.5 = (f32[128,128]{1,0:T(8,128)S(1)}, f32[128,128]{1,0:T(8,128)}, u32[]{:S(2)}) copy-start(f32[128,128]{1,0:T(8,128)} %constant.153) | copy-start | bytes 196612
  25.9 16.4 %copy-start.3 = (f32[128,128]{1,0:T(8,128)S(1)}, f32[128,128]{1,0:T(8,128)}, u32[]{:S(2)}) copy-start(f32[128,128]{1,0:T(8,128)} %constant.141.clone.refs_3_.refs_8_.refs_6_.refs_5_) | copy-start | bytes 196612
  25.9 16.4 %copy-start.4 = (bf16[544,256]{1,0:T(8,128)(2,1)S(1)}, bf16[544,256]{1,0:T(8,128)(2,1)}, u32[]{:S(2)}) copy-start(bf16[544,256]{1,0:T(8,128)(2,1)} %constant.158.refs_7_) | copy-start | bytes 835588
  31.5 1.9 collective-permute-start.2
  33.5 8.7 %collective-permute-start.3 = (f32[4,128,128]{2,1,0:T(8,128)S(1)}, f32[4,128,128]{2,1,0:T(8,128)S(1)}, u32[]{:S(2)}, u32[]{:S(2)}) collective-permute-start(f32[4,128,128]{2,1,0:T(8,128)S(1)} %pad_maximum_fusion.2), channel_id=1, source_target_pairs={{0,2},{1,3},{2,0},{3,1},{4,6},{5,7},{6,4},{7,5},{8,10},{9,11},{10,... | collective-permute-start | bytes 786440 | tf_op jit(solution)/shard_map/ppermute | solution.py:754
  53.8 6.0 %copy-start.10 = (s32[4]{0:T(128)S(1)}, s32[4]{0:T(128)}, u32[]{:S(2)}) copy-start(s32[4]{0:T(128)} %param.14) | copy-start | bytes 52
  53.8 143.9 %all-to-all-start = ((f32[8,1536,128]{2,1,0:T(8,128)}), f32[8,1536,128]{2,1,0:T(8,128)}, u32[]{:S(2)}, u32[]{:S(2)}) async-start(f32[8,1536,128]{2,1,0:T(8,128)} %bitcast.32), calls=%async_computation | async-start | bytes 12582912 | tf_op jit(solution)/shard_map/all_to_all | solution.py:826
  59.7 17.8 %copy-start.7 = (bf16[256,256]{1,0:T(8,128)(2,1)S(1)}, bf16[256,256]{1,0:T(8,128)(2,1)}, u32[]{:S(2)}) copy-start(bf16[256,256]{1,0:T(8,128)(2,1)} %constant.145.clone) | copy-start | bytes 393220
  73.6 1.6 collective-permute-start.4
  75.3 8.4 %collective-permute-start.5 = (f32[4,128,128]{2,1,0:T(8,128)S(1)}, f32[4,128,128]{2,1,0:T(8,128)S(1)}, u32[]{:S(2)}, u32[]{:S(2)}) collective-permute-start(f32[4,128,128]{2,1,0:T(8,128)S(1)} %pad_maximum_fusion.5), channel_id=1, source_target_pairs={{0,2},{1,3},{2,0},{3,1},{4,6},{5,7},{6,4},{7,5},{8,10},{9,11},{10,... | collective-permute-start | bytes 786440 | tf_op jit(solution)/shard_map/ppermute | solution.py:754

commit v3 on v2

--- a/solution.py
+++ b/solution.py
@@ -14,7 +14,7 @@
 viscosity = 0.01
 forcing_amplitude = 4.0
 
-TILE = 64
+TILE = 128
 SWEEP = 32
 LEAST = 16
 PAD = 8
@@ -148,7 +148,7 @@
         rz[slot, pl.ds(y0, TILE)] = rate
 
 
-def layer_rates(fns, layer, i, shift):
+def layer_rates(fns, layer, i, slot, shift):
     us, vs, rz, ry, dv, a_out = fns
     ny, nx = rz.shape[1:]
     for y0 in range(0, ny, TILE):
@@ -156,9 +156,9 @@
         drift, (rate_x, rate_y) = rate_tile(us, vs, layer, y0, (0, 1))
         if shift is not None:
             rate_x = rate_x + shift
-        a_out[0, i, rows] = drift[0] + rate_x
-        a_out[1, i, rows] = drift[1] + rate_y
-        a_out[2, i, rows] = drift[2] + rz[1, rows]
+        a_out[0, slot, rows] = drift[0] + rate_x
+        a_out[1, slot, rows] = drift[1] + rate_y
+        a_out[2, slot, rows] = drift[2] + rz[1, rows]
         dv[i, rows] = pltpu.roll(rate_x, nx - 1, 1) - pltpu.roll(rate_x, 1, 1)
         ry[pl.ds(PAD + y0, TILE)] = rate_y
     z_rate(fns, layer + 1, 2)
@@ -189,10 +189,11 @@
         (place, profile, v_hbm), refs = refs[:3], refs[3:]
     if halos:
         (lo_hbm, hi_hbm), refs = refs[:2], refs[2:]
-    (decay, basis, a_out, f_out, m_out), refs = refs[:5], refs[5:]
+    (decay_hbm, basis_hbm, a_hbm, f_hbm, m_out), refs = refs[:5], refs[5:]
     if tangent:
         us, refs = refs[0], refs[1:]
-    (vs, rz, ry, dv, pw, sems, halo_sems) = refs
+    (vs, rz, ry, dv, pw, a_out, f_out, f_all, decay, basis) = refs[:10]
+    (sems, halo_sems, out_sems, table_sems) = refs[10:]
     if not tangent:
         us = vs
     step = pl.program_id(0)
@@ -218,6 +219,19 @@
         near, far = ((1, 0), (layers + 2, layers + 3))[side]
         return halo_pairs(source, fields, near, far, inner, halo_sems, side)
 
+    def table_copies():
+        return [
+            pltpu.make_async_copy(decay_hbm, decay, table_sems.at[0]),
+            pltpu.make_async_copy(basis_hbm, basis, table_sems.at[1]),
+        ]
+
+    def out_copies(k):
+        part = pl.ds(k * chunk, chunk)
+        return [
+            pltpu.make_async_copy(a_out.at[:, part], a_hbm.at[:, part], out_sems.at[k, 0]),
+            pltpu.make_async_copy(f_all.at[part], f_hbm.at[part], out_sems.at[k, 1]),
+        ]
+
     def wait_chunk(k):
         for copy in chunk_copies(k):
             copy.wait()
@@ -249,6 +263,9 @@
         for k in range(steps):
             for copy in chunk_copies(k):
                 copy.start()
+            if k == 0:
+                for copy in table_copies():
+                    copy.start()
         if halos:
             for copy in halo_copies(1):
                 copy.start()
@@ -259,6 +276,8 @@
                 wait_halo(1)
             z_rate(fns, 1, 0)
             z_rate(fns, 2, 1)
+        for copy in table_copies():
+            copy.wait()
         m_out[...] = jnp.zeros(m_out.shape, jnp.float32)
         start = (place[0] * (layers // 2)).astype(jnp.float32)
         pw[...] = jnp.where(decay[...] >= 1.0, start, 1.0)
@@ -275,8 +294,12 @@
 
     for i in range(chunk):
         shift = None if tangent else profile[step * chunk + i]
-        layer_rates(fns, step * chunk + i + 2, i, shift)
+        layer_rates(fns, step * chunk + i + 2, i, step * chunk + i, shift)
     transform(dv, f_out, basis, chunk)
+    for i in range(chunk):
+        f_all[step * chunk + i] = f_out[i]
+    for copy in out_copies(step):
+        copy.start()
 
     def moments(first, last):
         for y0 in range(0, ny, TILE):
@@ -313,10 +336,17 @@
         def _():
             moments(0, chunk - 2)
 
+    @pl.when(step + 1 == steps)
+    def _():
+        for k in range(steps):
+            for copy in out_copies(k):
+                copy.wait()
+
 
 def edge_kernel(layers, *refs):
-    (place, u_hbm, v_hbm, lo_hbm, hi_hbm, a_in, f_in, m_in, decay, basis) = refs[:10]
-    (a_out, f_out, m_out, us, vs, rz, ry, dv, sems, halo_sems) = refs[10:]
+    (place, u_hbm, v_hbm, lo_hbm, hi_hbm, a_in, f_in, m_in, decay_hbm, basis_hbm) = refs[:10]
+    (a_out, f_out, m_out, us, vs, rz, ry, dv, decay, basis) = refs[10:20]
+    (sems, halo_sems, table_sems) = refs[20:]
     step = pl.program_id(0)
     ny = f_out.shape[1]
     fields = [(v_hbm, vs), (u_hbm, us)]
@@ -343,12 +373,18 @@
                     if layer != far or c == 2:
                         wrap_rows(ref, (c, layer), ny)
 
+    tables = [
+        pltpu.make_async_copy(decay_hbm, decay, table_sems.at[0]),
+        pltpu.make_async_copy(basis_hbm, basis, table_sems.at[1]),
+    ]
+
     @pl.when(step == 0)
     def _():
-        for side in range(2):
-            for copy in copies(side):
-                copy.start()
+        for copy in copies(0) + tables + copies(1):
+            copy.start()
         arrive(0)
+        for copy in tables:
+            copy.wait()
 
     @pl.when(step == 1)
     def _():
@@ -359,7 +395,7 @@
     z_rate(fns, top - 1, 0)
     z_rate(fns, top, 1)
     for i in range(2):
-        layer_rates(fns, top + i, i, None)
+        layer_rates(fns, top + i, i, i, None)
     transform(dv, f_out, basis, 2)
     half = layers // 2
     start = place[0] * half
@@ -381,13 +417,28 @@
 
 
 def solve_kernel(chunk, layers, period, rows_out, *refs):
-    (place, f_in, sides, totals, wrap_l, wrap_r, decay, basis, a_in) = refs[:9]
-    (v_out, qm, hat, phi) = refs[9:]
+    (place, f_hbm, sides, totals, wrap_l, wrap_r, decay, basis, a_hbm) = refs[:9]
+    (v_hbm, f_in, av, qm, hat, phi, f_sem, a_sems, v_sems) = refs[9:]
     step = pl.program_id(0)
+    steps = layers // chunk
     ny, nx = f_in.shape[1], f_in.shape[2]
     tall = rows_out + 2 * PAD
     half = layers // 2
     qx, qy = basis.at[pl.ds(0, 2 * nx)], basis.at[pl.ds(2 * nx, 2 * tall)]
+
+    def f_copy():
+        return pltpu.make_async_copy(f_hbm, f_in, f_sem)
+
+    def a_copy(k):
+        part = pl.ds(k * chunk, chunk)
+        rows = pl.ds(0, rows_out)
+        if rows_out < ny:
+            rows = pl.ds(pl.multiple_of(place[1] * rows_out, rows_out), rows_out)
+        return pltpu.make_async_copy(a_hbm.at[:, part, rows], av.at[:, part], a_sems.at[k])
+
+    def v_copy(k):
+        part = pl.ds(k * chunk, chunk)
+        return pltpu.make_async_copy(av.at[:, part], v_hbm.at[:, part], v_sems.at[k])
 
     def sweep(y0):
         rows = pl.ds(y0, SWEEP)
@@ -450,6 +501,11 @@
 
     @pl.when(step == 0)
     def _():
+        f_copy().start()
+        for k in range(steps):
+            a_copy(k).start()
+        f_copy().wait()
+
         def body(i, carry):
             sweep(pl.multiple_of(i * SWEEP, SWEEP))
             return carry
@@ -459,24 +515,32 @@
         invert(0, 2, 0)
 
     invert(step * chunk + 2, chunk, 2)
+    a_copy(step).wait()
 
     for i in range(chunk):
+        at = step * chunk + i
         size = min(TILE, rows_out)
         for y0 in range(0, rows_out, size):
             rows = pl.ds(y0, size)
             layer = i + 1
             here = phi[layer, pl.ds(PAD + y0, size)]
-            v_out[0, i, rows] = a_in[0, i, rows] - (
+            av[0, at, rows] = av[0, at, rows] - (
                 pltpu.roll(here, nx - 1, 1) - pltpu.roll(here, 1, 1)
             )
-            v_out[1, i, rows] = a_in[1, i, rows] - (
+            av[1, at, rows] = av[1, at, rows] - (
                 phi[layer, pl.ds(PAD + y0 + 1, size)] - phi[layer, pl.ds(PAD + y0 - 1, size)]
             )
-            v_out[2, i, rows] = a_in[2, i, rows] - (
+            av[2, at, rows] = av[2, at, rows] - (
                 phi[layer + 1, pl.ds(PAD + y0, size)] - phi[layer - 1, pl.ds(PAD + y0, size)]
             )
     for i in range(2):
         phi[i] = phi[chunk + i]
+    v_copy(step).start()
+
+    @pl.when(step + 1 == steps)
+    def _():
+        for k in range(steps):
+            v_copy(k).wait()
 
 
 def pairs_of(count):
@@ -574,11 +638,12 @@
     return pltpu.CompilerParams(vmem_limit_bytes=limit * MIB)
 
 
-def whole(shape):
-    return pl.BlockSpec(shape, lambda *_: (0,) * len(shape))
+def whole(_):
+    return pl.BlockSpec(memory_space=pltpu.VMEM)
 
 
 ANY = pl.BlockSpec(memory_space=pl.ANY)
+HBM = pl.BlockSpec(memory_space=pltpu.HBM)
 SMEM = pl.BlockSpec(memory_space=pltpu.SMEM)
 
 
@@ -593,8 +658,14 @@
         pltpu.VMEM((ny + 2 * PAD, nx), jnp.float32),
         pltpu.VMEM((chunk, ny, nx), jnp.float32),
         pltpu.VMEM((ny, nx), jnp.float32),
+        pltpu.VMEM(velocity.shape, jnp.float32),
+        pltpu.VMEM((chunk, ny, nx), jnp.float32),
+        pltpu.VMEM((layers, ny, nx), jnp.float32),
+        *[pltpu.VMEM(t.shape, t.dtype) for t in tables],
         pltpu.SemaphoreType.DMA((layers // chunk, 2)),
         pltpu.SemaphoreType.DMA((2, 4)),
+        pltpu.SemaphoreType.DMA((layers // chunk, 2)),
+        pltpu.SemaphoreType.DMA((2,)),
     ]
     size = velocity.size
     return pl.pallas_call(
@@ -602,19 +673,15 @@
         grid=(layers // chunk,),
         in_specs=[SMEM, ANY if tangent else SMEM, ANY]
         + [ANY for _ in halos]
-        + [whole(t.shape) for t in tables],
-        out_specs=[
-            pl.BlockSpec((3, chunk, ny, nx), lambda g: (0, g, 0, 0)),
-            pl.BlockSpec((chunk, ny, nx), lambda g: (g, 0, 0)),
-            whole((4, ny, nx)),
-        ],
+        + [HBM for _ in tables],
+        out_specs=[ANY, ANY, whole((4, ny, nx))],
         out_shape=[
             jax.ShapeDtypeStruct(velocity.shape, jnp.float32),
             jax.ShapeDtypeStruct((layers, ny, nx), jnp.float32),
             jax.ShapeDtypeStruct((4, ny, nx), jnp.float32),
         ],
         scratch_shapes=scratch,
-        compiler_params=params(52),
+        compiler_params=params(52 if tangent else 28),
         cost_estimate=pl.CostEstimate(
             flops=60 * size, bytes_accessed=16 * size, transcendentals=0
         ),
@@ -629,7 +696,7 @@
     return pl.pallas_call(
         functools.partial(edge_kernel, layers),
         grid=(2,),
-        in_specs=[SMEM] + [ANY] * 6 + [whole(t.shape) for t in (moments, *tables)],
+        in_specs=[SMEM] + [ANY] * 6 + [whole(moments.shape)] + [HBM for _ in tables],
         out_specs=[
             pl.BlockSpec((3, 2, ny, nx), lambda g: (0, g * ends, 0, 0)),
             pl.BlockSpec((2, ny, nx), lambda g: (g * ends, 0, 0)),
@@ -646,8 +713,10 @@
             pltpu.VMEM((3, ny, nx), jnp.float32),
             pltpu.VMEM((ny + 2 * PAD, nx), jnp.float32),
             pltpu.VMEM((2, ny, nx), jnp.float32),
+            *[pltpu.VMEM(t.shape, t.dtype) for t in tables],
             pltpu.SemaphoreType.DMA((2, 2)),
             pltpu.SemaphoreType.DMA((2, 4)),
+            pltpu.SemaphoreType.DMA((2,)),
         ],
         input_output_aliases={5: 0, 6: 1},
         compiler_params=params(52),
@@ -658,9 +727,9 @@
     )(place, tangent, velocity, *halos, a, f, moments, *tables)
 
 
-def solve(place, f, sides, totals, wraps, tables, a, rows_out, period, block):
+def solve(place, f, sides, totals, wraps, tables, a, rows_out, period):
     layers, ny, nx = f.shape
-    chunk = 4 if layers % 4 == 0 else 2
+    chunk = 8 if layers % 8 == 0 else 2
     tall = rows_out + 2 * PAD
     moments = whole((4, ny, nx))
     return pl.pallas_call(
@@ -668,18 +737,23 @@
         grid_spec=pltpu.PrefetchScalarGridSpec(
             num_scalar_prefetch=1,
             grid=(layers // chunk,),
-            in_specs=[whole(f.shape), moments, moments, whole((ny, nx)), whole((ny, nx))]
+            in_specs=[ANY, moments, moments, whole((ny, nx)), whole((ny, nx))]
             + [whole(t.shape) for t in tables]
-            + [pl.BlockSpec((3, chunk, rows_out, nx), lambda g, p: (0, g, p[1] * block, 0))],
-            out_specs=pl.BlockSpec((3, chunk, rows_out, nx), lambda g, p: (0, g, 0, 0)),
+            + [ANY],
+            out_specs=ANY,
             scratch_shapes=[
+                pltpu.VMEM((layers, ny, nx), jnp.float32),
+                pltpu.VMEM((3, layers, rows_out, nx), jnp.float32),
                 pltpu.VMEM((layers, ny, nx), jnp.float32),
                 pltpu.VMEM((layers + 2, ny, nx), jnp.float32),
                 pltpu.VMEM((chunk + 2, tall, nx), jnp.float32),
+                pltpu.SemaphoreType.DMA,
+                pltpu.SemaphoreType.DMA((layers // chunk,)),
+                pltpu.SemaphoreType.DMA((layers // chunk,)),
             ],
         ),
         out_shape=jax.ShapeDtypeStruct((3, layers, rows_out, nx), jnp.float32),
-        compiler_params=params(52),
+        compiler_params=params(52 if rows_out == ny else 16),
         cost_estimate=pl.CostEstimate(
             flops=40 * a.size, bytes_accessed=12 * a.size, transcendentals=0
         ),
@@ -819,7 +893,7 @@
     a, f, moments = edge_rates(place, tangent, base_flow, (lo, hi), a, f, moments, rate_tables)
     sides, totals = side_sums(moments, slab_power)
     tables = inverse_tables(0, ny)
-    advanced = solve(place, f, sides, totals, wraps, tables, a, ny, period, 0)
+    advanced = solve(place, f, sides, totals, wraps, tables, a, ny, period)
     advanced, base_lo, base_hi = lax.optimization_barrier((advanced, lo, hi))
 
     piece_rows = 3 * layers * ny // vectors
@@ -834,7 +908,7 @@
     base_sides, base_totals = side_sums(base_moments, slab_power)
     tables = inverse_tables(block * rows_run, rows_run)
     base_rows = solve(
-        place, base_f, base_sides, base_totals, wraps, tables, base_a, rows_run, period, 1
+        place, base_f, base_sides, base_totals, wraps, tables, base_a, rows_run, period
     )
     if rows_run != rows_out:
         base_rows = lax.dynamic_slice_in_dim(

time: 363 us -> 359 us (0.989)
  Pallas kernels: 67.8 us -> 58.7 us
  local copies, waits for them, and re-layouts: 8.14 us -> 17.2 us
  waiting for transfers between devices: 121 us -> 114 us
    unnamed x23 -> x35, local copies, waits for them, and re-layouts: 4.54 us -> 13.7 us
    pallas_call x2, Pallas kernels: 20.3 us -> 14.1 us  [solve(): pl.pallas_call(functools.partial(solve_kernel, chunk, layers, period, row...]
    all_to_all x1, waiting for transfers between devices: 105 us -> 99.4 us  [per_device(): lax.all_to_all(advanced.reshape(vectors, piece_rows, nx), 'vec', split_ax...]
  transfers between devices with their start and end apart: 7 -> 7, of which waited for: 5 -> 5; matrix products, arithmetic and copies ran while one was open for 0% -> 1% of each run, Pallas kernels for 11% -> 9%
where the time goes in v3:
time: 359 us; the launch traced here: 358 us
  blocking collectives  151 us (42%)
  waiting for transfers between devices  114 us (32%)
  Pallas kernels  58.7 us (16%)
  local copies, waits for them, and re-layouts  17.2 us (5%)
  starting transfers between devices  12.1 us (3%)
    all_to_all x1, blocking collectives, per_device(): lax.all_to_all(ortho_cells, 'vec', split_axis=0, concat_axis=0, tiled=True)  141 us
    all_to_all x1, waiting for transfers between devices, per_device(): lax.all_to_all(advanced.reshape(vectors, piece_rows, nx), 'vec', split_ax...  99.4 us
    pallas_call x2, Pallas kernels, rates(): pl.pallas_call(functools.partial(rate_kernel, tangent, len(halos) > 0, ch...  29.4 us
    ppermute x4, waiting for transfers between devices, side_sums(): lax.ppermute(jnp.concatenate([right, left], axis=0), 'gz', [(i, i ^ span)...  15.1 us
    pallas_call x2, Pallas kernels, solve(): pl.pallas_call(functools.partial(solve_kernel, chunk, layers, period, row...  14.1 us
    unnamed x35, local copies, waits for them, and re-layouts  13.7 us
    all_to_all x1, blocking collectives, per_device(): lax.all_to_all(jnp.broadcast_to(part[None], (devices,) + part.shape), ('v...  10.6 us
  transfers between devices with their start and end apart: 7, of which 5 were waited for; matrix products, arithmetic and copies ran while one was open for 1% of the time, Pallas kernels for 9%

profile of v3, /device:TPU:0, one launch (start us, length us, event | category | flops | bytes accessed | tf_op | source)
XLA Modules:
  0.0 358.5 jit_solution(15819634915839132727)
XLA Ops:
  0.6 1.3 slice_bitcast_fusion
  1.9 1.0 slice_bitcast_fusion.4
  2.9 2.4 collective-permute-start.1
  5.4 0.1 collective-permute-start
  5.5 0.1 pad_add_fusion.refs_0_
  5.6 0.9 copy-done.3
  6.5 0.8 copy-done.5
  7.3 16.6 %tangent_rates.1 = (f32[3,32,128,128]{3,2,1,0:T(8,128)}, f32[32,128,128]{2,1,0:T(8,128)}, f32[4,128,128]{2,1,0:T(8,128)S(1)}) custom-call(s32[2]{0:T(128)S(1)} %pad_add_fusion.refs_0_, f32[3,32,128,128]{3,2,1,0:T(8,128)} %bitcast.29, f32[3,32,128,128]{3,2,1,0:T(8,128)} %refs_2_.5, f32[128,128]{1,0:T(8,128)S(1)} %copy-done.5, bf16[512,256]{1,0:T(8,128)(2,1)S(1)} %copy-done.3), custom_call_target="tpu_custom_call" | custom-call | flops 94371840 | bytes 25165824 | tf_op jit(solution)/shard_map/tangent_rates/pallas_call | solution.py:671
  24.0 0.0 collective-permute-done.1.refs_4_
  24.0 0.0 collective-permute-done.refs_3_
  24.0 0.0 copy-done.4
  24.0 0.0 copy-start.13
  24.0 0.0 copy-start.14
  24.0 0.0 copy-start.15
  24.1 0.0 copy-start.12
  24.1 0.0 copy-start.6
  24.1 0.0 copy-start.9
  24.1 5.5 %tangent_edges.1 = (f32[3,32,128,128]{3,2,1,0:T(8,128)}, f32[32,128,128]{2,1,0:T(8,128)}, f32[4,128,128]{2,1,0:T(8,128)S(1)}) custom-call(s32[2]{0:T(128)S(1)} %pad_add_fusion.refs_0_, f32[3,32,128,128]{3,2,1,0:T(8,128)} %bitcast.30, f32[3,32,128,128]{3,2,1,0:T(8,128)} %refs_2_.5, ...), custom_call_target="tpu_custom_call", output_to_operand_aliasing={{0}: (5, {}), {1}: (6, {})} | custom-call | flops 11796480 | bytes 2621440 | tf_op jit(solution)/shard_map/tangent_edges/pallas_call | solution.py:696
  29.6 0.7 collective-permute-start.2
  30.4 1.2 collective-permute-done.2
  31.5 0.0 copy-done.13
  31.6 1.5 collective-permute-start.3
  33.1 0.0 copy-done.14
  33.1 0.0 copy-done.15
  33.2 0.0 copy-start.7
  33.2 0.0 copy-start.10
  33.2 0.0 copy-start.11
  33.2 7.0 %collective-permute-done.3 = f32[4,128,128]{2,1,0:T(8,128)S(1)} collective-permute-done((f32[4,128,128]{2,1,0:T(8,128)S(1)}, f32[4,128,128]{2,1,0:T(8,128)S(1)}, u32[]{:S(2)}, u32[]{:S(2)}) %collective-permute-start.3) | collective-permute-done | bytes 262176 | tf_op jit(solution)/shard_map/ppermute | solution.py:828
  40.3 0.0 copy-done.12
  40.3 0.1 add_select_fusion.9
  40.4 0.0 copy-done.6
  40.4 0.0 copy-done.9
  40.4 9.7 %tangent_solve.1 = f32[3,32,128,128]{3,2,1,0:T(8,128)} custom-call(s32[2]{0:T(128)S(1)} %pad_add_fusion.refs_0_, f32[32,128,128]{2,1,0:T(8,128)} %get-tuple-element.24.refs_1_, f32[4,128,128]{2,1,0:T(8,128)S(1)} %pad_maximum_fusion.3.refs_2_, f32[4,128,128]{2,1,0:T(8,128)S(1)} %pad_maximum_fusion.4.refs_3_, f32[128,128]{1,0:T(8,128)S(1)} %get-tuple-element.64.refs_4_, ...), custom_call_target="tpu_custom_call" | custom-call | flops 62914560 | bytes 18874368 | tf_op jit(solution)/shard_map/tangent_solve/pallas_call | solution.py:735
  50.1 0.0 copy-done.7
  50.1 0.0 copy-start.16
  50.1 5.8 %all-to-all-start = ((f32[8,1536,128]{2,1,0:T(8,128)}), f32[8,1536,128]{2,1,0:T(8,128)}, u32[]{:S(2)}, u32[]{:S(2)}) async-start(f32[8,1536,128]{2,1,0:T(8,128)} %bitcast.32), calls=%async_computation | async-start | bytes 12582912 | tf_op jit(solution)/shard_map/all_to_all | solution.py:900
  56.0 0.0 copy-done.16
  56.0 0.1 fusion.3
  56.1 0.0 copy-done.10
  56.1 0.0 copy-done.11
  56.2 0.0 copy-start
  56.2 2.8 copy-done
  59.0 12.7 %base_rates.1 = (f32[3,32,128,128]{3,2,1,0:T(8,128)S(1)}, f32[32,128,128]{2,1,0:T(8,128)S(1)}, f32[4,128,128]{2,1,0:T(8,128)S(1)}) custom-call(s32[2]{0:T(128)S(1)} %pad_add_fusion.refs_0_, f32[32]{0:T(128)S(1)} %broadcast_multiply_fusion.refs_1_, f32[3,32,128,128]{3,2,1,0:T(8,128)S(1)} %copy-done, f32[8,128,128]{2,1,0:T(8,128)S(1)} %collective-permute-done.refs_3_, ...), custom_call_target="tpu_custom_call" | custom-call | flops 94371840 | bytes 25165824 | tf_op jit(solution)/shard_map/base_rates/pallas_call | solution.py:671
  71.7 0.0 copy-start.1
  71.7 2.7 copy-done.1
  74.4 0.0 collective-permute-start.4
  74.4 1.5 collective-permute-done.4
  75.9 0.9 add_select_fusion.7
  76.8 1.5 collective-permute-start.5
  78.4 0.7 constant_dynamic-slice_fusion
  79.1 0.9 maximum_maximum_fusion.refs_7_
  80.0 5.4 %collective-permute-done.5 = f32[4,128,128]{2,1,0:T(8,128)} collective-permute-done((f32[4,128,128]{2,1,0:T(8,128)S(1)}, f32[4,128,128]{2,1,0:T(8,128)}, u32[]{:S(2)}, u32[]{:S(2)}) %collective-permute-start.5) | collective-permute-done | bytes 262176 | tf_op jit(solution)/shard_map/ppermute | solution.py:828
  85.4 1.1 add_select_fusion.5
  86.5 0.0 copy-start.2
  86.5 2.8 copy-done.2
  89.3 0.8 copy-done.8
  90.2 4.4 %base_solve.1 = f32[3,32,16,128]{3,2,1,0:T(8,128)} custom-call(s32[2]{0:T(128)S(1)} %pad_add_fusion.refs_0_, f32[32,128,128]{2,1,0:T(8,128)S(1)} %get-tuple-element.30.refs_1_, f32[4,128,128]{2,1,0:T(8,128)S(1)} %pad_maximum_fusion.6.refs_2_, f32[4,128,128]{2,1,0:T(8,128)S(1)} %pad_maximum_fusion.7.refs_3_, f32[128,128]{1,0:T(8,128)S(1)} %copy-done.8, ...), custom_call_target="tpu_custom_call" | custom-call | flops 62914560 | bytes 18874368 | tf_op jit(solution)/shard_map/base_solve/pallas_call | solution.py:735
  94.6 99.4 %all-to-all-done.x_ref = f32[8,1536,128]{2,1,0:T(8,128)} async-done(((f32[8,1536,128]{2,1,0:T(8,128)}), f32[8,1536,128]{2,1,0:T(8,128)}, u32[]{:S(2)}, u32[]{:S(2)}) %all-to-all-start) | async-done | bytes 6291488 | tf_op jit(solution)/shard_map/all_to_all | solution.py:900
  193.9 4.5 %gram_parts.1 = f32[1,128]{1,0:T(1,128)S(1)} custom-call(f32[8,1536,128]{2,1,0:T(8,128)} %all-to-all-done.x_ref), custom_call_target="tpu_custom_call" | custom-call | flops 12582912 | bytes 6291456 | tf_op jit(solution)/shard_map/gram_parts/pallas_call | solution.py:776
  198.4 10.6 %all_to_all.15.parts_ref = f32[32,1,128]{2,1,0:T(1,128)S(1)} all-to-all(f32[32,1,128]{2,1,0:T(1,128)S(1)} %broadcast_in_dim.5), channel_id=1, replica_groups=mesh['vec'=8,'gz'=4] {'vec','gz'}, dimensions={0} | all-to-all | bytes 32768 | tf_op jit(solution)/shard_map/all_to_all | solution.py:922
  209.0 5.3 %ortho_rows.1 = (f32[8,1536,128]{2,1,0:T(8,128)S(1)}, f32[8,128]{1,0:T(8,128)S(1)}) custom-call(f32[32,1,128]{2,1,0:T(1,128)S(1)} %all_to_all.15.parts_ref, f32[8,1536,128]{2,1,0:T(8,128)} %all-to-all-done.x_ref), custom_call_target="tpu_custom_call" | custom-call | flops 12582912 | bytes 12582912 | tf_op jit(solution)/shard_map/ortho_rows/pallas_call | solution.py:794
  214.2 0.6 slice_reduce_fusion
  214.9 140.9 %all_to_all.16 = f32[8,1536,128]{2,1,0:T(8,128)S(1)} all-to-all(f32[8,1536,128]{2,1,0:T(8,128)S(1)} %get-tuple-element.37), channel_id=1, replica_groups=mesh['vec'=8,'gz'=4] {'vec'}, dimensions={0} | all-to-all | bytes 12582912 | tf_op jit(solution)/shard_map/all_to_all | solution.py:933
  355.8 2.7 copy.28
  (17 shorter events, 0.3 us)
Async XLA Ops:
  2.9 21.1 %collective-permute-start.1 = (f32[8,128,128]{2,1,0:T(8,128)S(1)}, f32[8,128,128]{2,1,0:T(8,128)S(1)}, u32[]{:S(2)}, u32[]{:S(2)}) collective-permute-start(f32[8,128,128]{2,1,0:T(8,128)S(1)} %pad_maximum_fusion.1), channel_id=1, source_target_pairs={{0,3},{1,0},{2,1},{3,2},{4,7},{5,4},{6,5},{7,6},{8,11},{9,8},{10,9... | collective-permute-start | bytes 1572872 | tf_op jit(solution)/shard_map/ppermute | solution.py:817
  5.4 18.6 %collective-permute-start = (f32[8,128,128]{2,1,0:T(8,128)S(1)}, f32[8,128,128]{2,1,0:T(8,128)S(1)}, u32[]{:S(2)}, u32[]{:S(2)}) collective-permute-start(f32[8,128,128]{2,1,0:T(8,128)S(1)} %pad_maximum_fusion), channel_id=1, source_target_pairs={{0,1},{1,2},{2,3},{3,0},{4,5},{5,6},{6,7},{7,4},{8,9},{9,10},{10,1... | collective-permute-start | bytes 1572872 | tf_op jit(solution)/shard_map/ppermute | solution.py:817
  5.5 1.0 copy-start.3
  6.5 0.8 copy-start.5
  7.3 16.7 %copy-start.4 = (bf16[512,256]{1,0:T(8,128)(2,1)S(1)}, bf16[512,256]{1,0:T(8,128)(2,1)}, u32[]{:S(2)}) copy-start(bf16[512,256]{1,0:T(8,128)(2,1)} %constant.144.clone.refs_4_.refs_9_.refs_6_) | copy-start | bytes 786436
  24.0 7.5 %copy-start.13 = (f32[128,128]{1,0:T(8,128)S(1)}, f32[128,128]{1,0:T(8,128)}, u32[]{:S(2)}) copy-start(f32[128,128]{1,0:T(8,128)} %constant.151) | copy-start | bytes 196612
  24.0 9.1 %copy-start.14 = (f32[128,128]{1,0:T(8,128)S(1)}, f32[128,128]{1,0:T(8,128)}, u32[]{:S(2)}) copy-start(f32[128,128]{1,0:T(8,128)} %constant.142.clone) | copy-start | bytes 196612
  24.0 9.1 %copy-start.15 = (f32[128,128]{1,0:T(8,128)S(1)}, f32[128,128]{1,0:T(8,128)}, u32[]{:S(2)}) copy-start(f32[128,128]{1,0:T(8,128)} %constant.143.clone) | copy-start | bytes 196612
  24.1 16.2 %copy-start.12 = (f32[128,128]{1,0:T(8,128)S(1)}, f32[128,128]{1,0:T(8,128)}, u32[]{:S(2)}) copy-start(f32[128,128]{1,0:T(8,128)} %constant.153) | copy-start | bytes 196612
  24.1 16.3 %copy-start.6 = (f32[128,128]{1,0:T(8,128)S(1)}, f32[128,128]{1,0:T(8,128)}, u32[]{:S(2)}) copy-start(f32[128,128]{1,0:T(8,128)} %constant.141.clone.refs_3_.refs_8_.refs_6_.refs_5_) | copy-start | bytes 196612
  24.1 16.3 %copy-start.9 = (bf16[544,256]{1,0:T(8,128)(2,1)S(1)}, bf16[544,256]{1,0:T(8,128)(2,1)}, u32[]{:S(2)}) copy-start(bf16[544,256]{1,0:T(8,128)(2,1)} %constant.158.refs_7_) | copy-start | bytes 835588
  29.6 1.9 collective-permute-start.2
  31.6 8.7 %collective-permute-start.3 = (f32[4,128,128]{2,1,0:T(8,128)S(1)}, f32[4,128,128]{2,1,0:T(8,128)S(1)}, u32[]{:S(2)}, u32[]{:S(2)}) collective-permute-start(f32[4,128,128]{2,1,0:T(8,128)S(1)} %pad_maximum_fusion.2), channel_id=1, source_target_pairs={{0,2},{1,3},{2,0},{3,1},{4,6},{5,7},{6,4},{7,5},{8,10},{9,11},{10,... | collective-permute-start | bytes 786440 | tf_op jit(solution)/shard_map/ppermute | solution.py:828
  33.2 16.9 %copy-start.7 = (f32[128,128]{1,0:T(8,128)}, f32[128,128]{1,0:T(8,128)S(1)}, u32[]{:S(2)}) copy-start(f32[128,128]{1,0:T(8,128)S(1)} %get-tuple-element.64.refs_4_) | copy-start | bytes 196612
  33.2 22.9 %copy-start.10 = (f32[128,128]{1,0:T(8,128)}, f32[128,128]{1,0:T(8,128)S(1)}, u32[]{:S(2)}) copy-start(f32[128,128]{1,0:T(8,128)S(1)} %get-tuple-element.65) | copy-start | bytes 196612
  33.2 22.9 %copy-start.11 = (f32[128,128]{1,0:T(8,128)}, f32[128,128]{1,0:T(8,128)S(1)}, u32[]{:S(2)}) copy-start(f32[128,128]{1,0:T(8,128)S(1)} %get-tuple-element.66) | copy-start | bytes 196612
  50.1 5.9 %copy-start.16 = (s32[4]{0:T(128)S(1)}, s32[4]{0:T(128)}, u32[]{:S(2)}) copy-start(s32[4]{0:T(128)} %param.14) | copy-start | bytes 52
  50.1 143.8 %all-to-all-start = ((f32[8,1536,128]{2,1,0:T(8,128)}), f32[8,1536,128]{2,1,0:T(8,128)}, u32[]{:S(2)}, u32[]{:S(2)}) async-start(f32[8,1536,128]{2,1,0:T(8,128)} %bitcast.32), calls=%async_computation | async-start | bytes 12582912 | tf_op jit(solution)/shard_map/all_to_all | solution.py:900
  56.2 2.8 copy-start
  71.7 2.7 copy-start.1
  74.4 1.5 collective-permute-start.4
  76.8 8.5 %collective-permute-start.5 = (f32[4,128,128]{2,1,0:T(8,128)S(1)}, f32[4,128,128]{2,1,0:T(8,128)}, u32[]{:S(2)}, u32[]{:S(2)}) collective-permute-start(f32[4,128,128]{2,1,0:T(8,128)S(1)} %pad_maximum_fusion.5), channel_id=1, source_target_pairs={{0,2},{1,3},{2,0},{3,1},{4,6},{5,7},{6,4},{7,5},{8,10},{9,11},{10,... | collective-permute-start | bytes 786440 | tf_op jit(solution)/shard_map/ppermute | solution.py:828
  86.5 2.8 copy-start.2
  89.3 0.8 copy-start.8

commit v4 on v3

--- a/solution.py
+++ b/solution.py
@@ -301,40 +301,31 @@
     for copy in out_copies(step):
         copy.start()
 
-    def moments(first, last):
-        for y0 in range(0, ny, TILE):
-            rows = pl.ds(y0, TILE)
-            rate = decay[rows]
-            marks = jnp.where(rate >= 1.0, 1.0, 0.0)
-            power = pw[rows]
-            right = [m_out[0, rows], m_out[1, rows]]
-            left = [m_out[2, rows], m_out[3, rows]]
-            for i in range(chunk):
-                parity = i % 2
-                if first <= i < last:
-                    f = f_out[i, rows]
-                    right[parity] = rate * right[parity] + f
-                    left[parity] = left[parity] + power * f
-                if parity == 1:
-                    power = rate * power + marks
-            pw[rows] = power
-            m_out[0, rows], m_out[1, rows] = right
-            m_out[2, rows], m_out[3, rows] = left
-
-    if halos:
-        moments(0, chunk)
-    else:
-        @pl.when(step == 0)
-        def _():
-            moments(2, chunk)
-
-        @pl.when((step > 0) & (step + 1 < steps))
-        def _():
-            moments(0, chunk)
-
-        @pl.when(step + 1 == steps)
-        def _():
-            moments(0, chunk - 2)
+    for y0 in range(0, ny, TILE):
+        rows = pl.ds(y0, TILE)
+        rate = decay[rows]
+        marks = jnp.where(rate >= 1.0, 1.0, 0.0)
+        power = pw[rows]
+        right = [m_out[0, rows], m_out[1, rows]]
+        left = [m_out[2, rows], m_out[3, rows]]
+        for i in range(chunk):
+            parity = i % 2
+            f = f_out[i, rows]
+            ahead = rate * right[parity] + f
+            if not halos:
+                if i < 2:
+                    f = jnp.where(step > 0, f, 0.0)
+                    ahead = rate * right[parity] + f
+                if i >= chunk - 2:
+                    f = jnp.where(step + 1 < steps, f, 0.0)
+                    ahead = jnp.where(step + 1 < steps, ahead, right[parity])
+            right[parity] = ahead
+            left[parity] = left[parity] + power * f
+            if parity == 1:
+                power = rate * power + marks
+        pw[rows] = power
+        m_out[0, rows], m_out[1, rows] = right
+        m_out[2, rows], m_out[3, rows] = left
 
     @pl.when(step + 1 == steps)
     def _():
@@ -547,13 +538,27 @@
     return [(i, j) for i in range(count) for j in range(i + 1)]
 
 
-def gram_kernel(count, x_ref, out_ref, acc):
+def piece_copies(x_hbm, x_ref, rows, sems):
+    return [
+        pltpu.make_async_copy(
+            x_hbm.at[:, pl.ds(k * rows, rows)], x_ref.at[:, pl.ds(k * rows, rows)], sems.at[k]
+        )
+        for k in range(x_ref.shape[1] // rows)
+    ]
+
+
+def gram_kernel(count, rows, x_hbm, out_ref, x_ref, acc, sems):
     step = pl.program_id(0)
-    rows = x_ref.shape[1]
+    copies = piece_copies(x_hbm, x_ref, rows, sems)
 
     @pl.when(step == 0)
     def _():
+        for copy in copies:
+            copy.start()
         acc[...] = jnp.zeros(acc.shape, jnp.float32)
+
+    for k, copy in enumerate(copies):
+        pl.when(step == k)(copy.wait)
 
     group = 8
     for bi in range(0, count, group):
@@ -567,7 +572,7 @@
             slots = [i * (i + 1) // 2 + j for i, j in pairs]
 
             def body(t, sums):
-                part = pl.ds(pl.multiple_of(t * 8, 8), 8)
+                part = pl.ds(pl.multiple_of(step * rows + t * 8, 8), 8)
                 needed = sorted({i for i, _ in pairs} | {j for _, j in pairs})
                 tile = {i: x_ref[i, part] for i in needed}
                 return tuple(s + tile[i] * tile[j] for s, (i, j) in zip(sums, pairs))
@@ -589,12 +594,14 @@
         out_ref[...] = out
 
 
-def ortho_kernel(count, cells, parts_ref, x_ref, out_ref, growth_ref, coef):
+def ortho_kernel(count, rows, cells, parts_ref, x_hbm, out_ref, growth_ref, x_ref, coef, sems):
     step = pl.program_id(0)
-    rows = x_ref.shape[1]
+    copies = piece_copies(x_hbm, x_ref, rows, sems)
 
     @pl.when(step == 0)
     def _():
+        for copy in copies:
+            copy.start()
         nx = x_ref.shape[2]
         shape = (max(8, count), nx)
         row = lax.broadcasted_iota(jnp.int32, shape, 0)
@@ -612,15 +619,19 @@
             scale = jnp.where(row[:, :1] > k, work[:, k : k + 1] / pivot, 0.0)
             work = work - scale * work[k : k + 1, :]
         diagonal = jnp.sum(jnp.where(lane == row, work, 0.0), axis=1, keepdims=True)
-        growth_ref[...] = jnp.broadcast_to(0.5 * jnp.log(diagonal), shape)
+        across = jnp.sum(jnp.where(lane == row, work, 0.0), axis=0, keepdims=True)
+        growth_ref[...] = 0.5 * jnp.log(across[:, :count])
         work = work / jnp.sqrt(diagonal)
         for s, (i, j) in enumerate(pairs_of(count)):
             coef[s] = jnp.broadcast_to(
                 work[i : i + 1, count + j : count + j + 1], coef.shape[1:]
             )
 
+    for k, copy in enumerate(copies):
+        pl.when(step == k)(copy.wait)
+
     def body(t, carry):
-        part = pl.ds(pl.multiple_of(t * 16, 16), 16)
+        part = pl.ds(pl.multiple_of(step * rows + t * 16, 16), 16)
         tile = [x_ref[i, part] for i in range(count)]
         for i in range(count):
             total = None
@@ -763,7 +774,7 @@
 
 def row_chunk(rows):
     best = 16
-    for size in range(16, 800, 16):
+    for size in range(16, 400, 16):
         if rows % size == 0:
             best = size
     return best
@@ -774,13 +785,17 @@
     size = row_chunk(rows)
     tall = -(-count * count // nx)
     return pl.pallas_call(
-        functools.partial(gram_kernel, count),
+        functools.partial(gram_kernel, count, size),
         grid=(rows // size,),
-        in_specs=[pl.BlockSpec((count, size, nx), lambda g: (0, g, 0))],
+        in_specs=[ANY],
         out_specs=whole((tall, nx)),
         out_shape=jax.ShapeDtypeStruct((tall, nx), jnp.float32),
-        scratch_shapes=[pltpu.VMEM((count * (count + 1) // 2, 8, nx), jnp.float32)],
-        compiler_params=params(12),
+        scratch_shapes=[
+            pltpu.VMEM(cells.shape, jnp.float32),
+            pltpu.VMEM((count * (count + 1) // 2, 8, nx), jnp.float32),
+            pltpu.SemaphoreType.DMA((rows // size,)),
+        ],
+        compiler_params=params(14),
         cost_estimate=pl.CostEstimate(
             flops=count * cells.size, bytes_accessed=4 * cells.size, transcendentals=0
         ),
@@ -792,19 +807,20 @@
     count, rows, nx = cells.shape
     size = row_chunk(rows)
     return pl.pallas_call(
-        functools.partial(ortho_kernel, count, total_cells),
+        functools.partial(ortho_kernel, count, size, total_cells),
         grid=(rows // size,),
-        in_specs=[whole(parts.shape), pl.BlockSpec((count, size, nx), lambda g: (0, g, 0))],
-        out_specs=[
-            pl.BlockSpec((count, size, nx), lambda g: (0, g, 0)),
-            whole((max(8, count), nx)),
-        ],
+        in_specs=[whole(parts.shape), ANY],
+        out_specs=[whole(cells.shape), whole((1, count))],
         out_shape=[
             jax.ShapeDtypeStruct(cells.shape, jnp.float32),
-            jax.ShapeDtypeStruct((max(8, count), nx), jnp.float32),
+            jax.ShapeDtypeStruct((1, count), jnp.float32),
         ],
-        scratch_shapes=[pltpu.VMEM((count * (count + 1) // 2, 8, nx), jnp.float32)],
-        compiler_params=params(20),
+        scratch_shapes=[
+            pltpu.VMEM(cells.shape, jnp.float32),
+            pltpu.VMEM((count * (count + 1) // 2, 8, nx), jnp.float32),
+            pltpu.SemaphoreType.DMA((rows // size,)),
+        ],
+        compiler_params=params(24),
         cost_estimate=pl.CostEstimate(
             flops=count * cells.size, bytes_accessed=8 * cells.size, transcendentals=0
         ),
@@ -929,7 +945,7 @@
     else:
         parts = lax.psum(part, ("vec", "gz"))[None]
     ortho_cells, growth = ortho(parts, cells, 3.0 * nz * ny * nx)
-    ortho_cells, growth = lax.optimization_barrier((ortho_cells, growth[:vectors, 0]))
+    ortho_cells, growth = lax.optimization_barrier((ortho_cells, growth.reshape(vectors)))
     returned = lax.all_to_all(ortho_cells, "vec", split_axis=0, concat_axis=0, tiled=True)
     return (base_rows, returned.reshape(tangents.shape), growth)
 

time: 359 us -> 357 us (level)
  no operation moved by 1% of the time
where the time goes in v4:
time: 357 us; the launch traced here: 356 us
  blocking collectives  151 us (42%)
  waiting for transfers between devices  114 us (32%)
  Pallas kernels  56.9 us (16%)
  local copies, waits for them, and re-layouts  16.6 us (5%)
  starting transfers between devices  12.1 us (3%)
    all_to_all x1, blocking collectives, per_device(): lax.all_to_all(ortho_cells, 'vec', split_axis=0, concat_axis=0, tiled=True)  141 us
    all_to_all x1, waiting for transfers between devices, per_device(): lax.all_to_all(advanced.reshape(vectors, piece_rows, nx), 'vec', split_ax...  99.4 us
    pallas_call x2, Pallas kernels, rates(): pl.pallas_call(functools.partial(rate_kernel, tangent, len(halos) > 0, ch...  29.1 us
    ppermute x4, waiting for transfers between devices, side_sums(): lax.ppermute(jnp.concatenate([right, left], axis=0), 'gz', [(i, i ^ span)...  15.1 us
    pallas_call x2, Pallas kernels, solve(): pl.pallas_call(functools.partial(solve_kernel, chunk, layers, period, row...  14.1 us
    unnamed x35, local copies, waits for them, and re-layouts  13.7 us
    all_to_all x1, blocking collectives, per_device(): lax.all_to_all(jnp.broadcast_to(part[None], (devices,) + part.shape), ('v...  10.6 us
  transfers between devices with their start and end apart: 7, of which 5 were waited for; matrix products, arithmetic and copies ran while one was open for 1% of the time, Pallas kernels for 9%

profile of v4, /device:TPU:0, one launch (start us, length us, event | category | flops | bytes accessed | tf_op | source)
XLA Modules:
  0.0 356.0 jit_solution(10161206547551963871)
XLA Ops:
  0.6 1.3 slice_bitcast_fusion
  1.9 1.0 slice_bitcast_fusion.4
  2.9 2.4 collective-permute-start.1
  5.4 0.1 collective-permute-start
  5.5 0.1 pad_add_fusion.refs_0_
  5.5 0.0 copy-start.3
  5.6 0.9 copy-done.3
  6.5 0.8 copy-done.5
  7.3 16.4 %tangent_rates.1 = (f32[3,32,128,128]{3,2,1,0:T(8,128)}, f32[32,128,128]{2,1,0:T(8,128)}, f32[4,128,128]{2,1,0:T(8,128)S(1)}) custom-call(s32[2]{0:T(128)S(1)} %pad_add_fusion.refs_0_, f32[3,32,128,128]{3,2,1,0:T(8,128)} %bitcast.30, f32[3,32,128,128]{3,2,1,0:T(8,128)} %refs_2_.5, f32[128,128]{1,0:T(8,128)S(1)} %copy-done.5, bf16[512,256]{1,0:T(8,128)(2,1)S(1)} %copy-done.3), custom_call_target="tpu_custom_call" | custom-call | flops 94371840 | bytes 25165824 | tf_op jit(solution)/shard_map/tangent_rates/pallas_call | solution.py:682
  23.7 0.0 collective-permute-done.1.refs_4_
  23.7 0.0 collective-permute-done.refs_3_
  23.7 0.0 copy-done.4
  23.8 0.0 copy-start.13
  23.8 0.0 copy-start.14
  23.8 0.0 copy-start.15
  23.8 0.0 copy-start.12
  23.8 0.0 copy-start.6
  23.8 0.0 copy-start.9
  23.8 5.6 %tangent_edges.1 = (f32[3,32,128,128]{3,2,1,0:T(8,128)}, f32[32,128,128]{2,1,0:T(8,128)}, f32[4,128,128]{2,1,0:T(8,128)S(1)}) custom-call(s32[2]{0:T(128)S(1)} %pad_add_fusion.refs_0_, f32[3,32,128,128]{3,2,1,0:T(8,128)} %bitcast.31, f32[3,32,128,128]{3,2,1,0:T(8,128)} %refs_2_.5, ...), custom_call_target="tpu_custom_call", output_to_operand_aliasing={{0}: (5, {}), {1}: (6, {})} | custom-call | flops 11796480 | bytes 2621440 | tf_op jit(solution)/shard_map/tangent_edges/pallas_call | solution.py:707
  29.4 0.7 collective-permute-start.2
  30.1 1.2 collective-permute-done.2
  31.3 0.0 copy-done.13
  31.4 1.5 collective-permute-start.3
  32.9 0.0 copy-done.14
  32.9 0.0 copy-done.15
  32.9 0.0 copy-start.7
  33.0 0.0 copy-start.10
  33.0 0.0 copy-start.11
  33.0 7.0 %collective-permute-done.3 = f32[4,128,128]{2,1,0:T(8,128)S(1)} collective-permute-done((f32[4,128,128]{2,1,0:T(8,128)S(1)}, f32[4,128,128]{2,1,0:T(8,128)S(1)}, u32[]{:S(2)}, u32[]{:S(2)}) %collective-permute-start.3) | collective-permute-done | bytes 262176 | tf_op jit(solution)/shard_map/ppermute | solution.py:844
  40.0 0.0 copy-done.12
  40.0 0.1 add_select_fusion.9
  40.2 0.0 copy-done.6
  40.2 0.0 copy-done.9
  40.2 9.7 %tangent_solve.1 = f32[3,32,128,128]{3,2,1,0:T(8,128)} custom-call(s32[2]{0:T(128)S(1)} %pad_add_fusion.refs_0_, f32[32,128,128]{2,1,0:T(8,128)} %get-tuple-element.24.refs_1_, f32[4,128,128]{2,1,0:T(8,128)S(1)} %pad_maximum_fusion.3.refs_2_, f32[4,128,128]{2,1,0:T(8,128)S(1)} %pad_maximum_fusion.4.refs_3_, f32[128,128]{1,0:T(8,128)S(1)} %get-tuple-element.64.refs_4_, ...), custom_call_target="tpu_custom_call" | custom-call | flops 62914560 | bytes 18874368 | tf_op jit(solution)/shard_map/tangent_solve/pallas_call | solution.py:746
  49.9 0.0 copy-done.7
  49.9 0.0 copy-start.16
  49.9 5.8 %all-to-all-start = ((f32[8,1536,128]{2,1,0:T(8,128)}), f32[8,1536,128]{2,1,0:T(8,128)}, u32[]{:S(2)}, u32[]{:S(2)}) async-start(f32[8,1536,128]{2,1,0:T(8,128)} %bitcast.33), calls=%async_computation | async-start | bytes 12582912 | tf_op jit(solution)/shard_map/all_to_all | solution.py:916
  55.7 0.0 copy-done.16
  55.8 0.1 fusion.3
  55.9 0.0 copy-done.10
  55.9 0.0 copy-done.11
  55.9 0.0 copy-start
  55.9 2.8 copy-done
  58.7 12.7 %base_rates.1 = (f32[3,32,128,128]{3,2,1,0:T(8,128)S(1)}, f32[32,128,128]{2,1,0:T(8,128)S(1)}, f32[4,128,128]{2,1,0:T(8,128)S(1)}) custom-call(s32[2]{0:T(128)S(1)} %pad_add_fusion.refs_0_, f32[32]{0:T(128)S(1)} %broadcast_multiply_fusion.refs_1_, f32[3,32,128,128]{3,2,1,0:T(8,128)S(1)} %copy-done, f32[8,128,128]{2,1,0:T(8,128)S(1)} %collective-permute-done.refs_3_, ...), custom_call_target="tpu_custom_call" | custom-call | flops 94371840 | bytes 25165824 | tf_op jit(solution)/shard_map/base_rates/pallas_call | solution.py:682
  71.4 0.0 copy-start.1
  71.4 2.7 copy-done.1
  74.1 0.0 collective-permute-start.4
  74.1 1.5 collective-permute-done.4
  75.7 0.9 add_select_fusion.7
  76.6 1.5 collective-permute-start.5
  78.1 0.7 constant_dynamic-slice_fusion
  78.8 0.9 maximum_maximum_fusion.refs_7_
  79.8 5.4 %collective-permute-done.5 = f32[4,128,128]{2,1,0:T(8,128)} collective-permute-done((f32[4,128,128]{2,1,0:T(8,128)S(1)}, f32[4,128,128]{2,1,0:T(8,128)}, u32[]{:S(2)}, u32[]{:S(2)}) %collective-permute-start.5) | collective-permute-done | bytes 262176 | tf_op jit(solution)/shard_map/ppermute | solution.py:844
  85.1 1.1 add_select_fusion.5
  86.3 0.0 copy-start.2
  86.3 2.8 copy-done.2
  89.1 0.8 copy-done.8
  89.9 4.4 %base_solve.1 = f32[3,32,16,128]{3,2,1,0:T(8,128)} custom-call(s32[2]{0:T(128)S(1)} %pad_add_fusion.refs_0_, f32[32,128,128]{2,1,0:T(8,128)S(1)} %get-tuple-element.30.refs_1_, f32[4,128,128]{2,1,0:T(8,128)S(1)} %pad_maximum_fusion.6.refs_2_, f32[4,128,128]{2,1,0:T(8,128)S(1)} %pad_maximum_fusion.7.refs_3_, f32[128,128]{1,0:T(8,128)S(1)} %copy-done.8, ...), custom_call_target="tpu_custom_call" | custom-call | flops 62914560 | bytes 18874368 | tf_op jit(solution)/shard_map/base_solve/pallas_call | solution.py:746
  94.3 99.4 %all-to-all-done.x_hbm = f32[8,1536,128]{2,1,0:T(8,128)} async-done(((f32[8,1536,128]{2,1,0:T(8,128)}), f32[8,1536,128]{2,1,0:T(8,128)}, u32[]{:S(2)}, u32[]{:S(2)}) %all-to-all-start) | async-done | bytes 6291488 | tf_op jit(solution)/shard_map/all_to_all | solution.py:916
  193.7 4.0 %gram_parts.1 = f32[1,128]{1,0:T(1,128)S(1)} custom-call(f32[8,1536,128]{2,1,0:T(8,128)} %all-to-all-done.x_hbm), custom_call_target="tpu_custom_call" | custom-call | flops 12582912 | bytes 6291456 | tf_op jit(solution)/shard_map/gram_parts/pallas_call | solution.py:787
  197.7 10.6 %all_to_all.15.parts_ref = f32[32,1,128]{2,1,0:T(1,128)S(1)} all-to-all(f32[32,1,128]{2,1,0:T(1,128)S(1)} %broadcast_in_dim.5), channel_id=1, replica_groups=mesh['vec'=8,'gz'=4] {'vec','gz'}, dimensions={0} | all-to-all | bytes 32768 | tf_op jit(solution)/shard_map/all_to_all | solution.py:938
  208.3 4.1 %ortho_rows.1 = (f32[8,1536,128]{2,1,0:T(8,128)S(1)}, f32[1,8]{1,0:T(1,128)}) custom-call(f32[32,1,128]{2,1,0:T(1,128)S(1)} %all_to_all.15.parts_ref, f32[8,1536,128]{2,1,0:T(8,128)} %all-to-all-done.x_hbm), custom_call_target="tpu_custom_call" | custom-call | flops 12582912 | bytes 12582912 | tf_op jit(solution)/shard_map/ortho_rows/pallas_call | solution.py:809
  212.4 140.9 %all_to_all.16 = f32[8,1536,128]{2,1,0:T(8,128)S(1)} all-to-all(f32[8,1536,128]{2,1,0:T(8,128)S(1)} %get-tuple-element.37), channel_id=1, replica_groups=mesh['vec'=8,'gz'=4] {'vec'}, dimensions={0} | all-to-all | bytes 12582912 | tf_op jit(solution)/shard_map/all_to_all | solution.py:949
  353.3 2.7 copy.26
  (16 shorter events, 0.3 us)
Async XLA Ops:
  2.9 20.8 %collective-permute-start.1 = (f32[8,128,128]{2,1,0:T(8,128)S(1)}, f32[8,128,128]{2,1,0:T(8,128)S(1)}, u32[]{:S(2)}, u32[]{:S(2)}) collective-permute-start(f32[8,128,128]{2,1,0:T(8,128)S(1)} %pad_maximum_fusion.1), channel_id=1, source_target_pairs={{0,3},{1,0},{2,1},{3,2},{4,7},{5,4},{6,5},{7,6},{8,11},{9,8},{10,9... | collective-permute-start | bytes 1572872 | tf_op jit(solution)/shard_map/ppermute | solution.py:833
  5.4 18.3 %collective-permute-start = (f32[8,128,128]{2,1,0:T(8,128)S(1)}, f32[8,128,128]{2,1,0:T(8,128)S(1)}, u32[]{:S(2)}, u32[]{:S(2)}) collective-permute-start(f32[8,128,128]{2,1,0:T(8,128)S(1)} %pad_maximum_fusion), channel_id=1, source_target_pairs={{0,1},{1,2},{2,3},{3,0},{4,5},{5,6},{6,7},{7,4},{8,9},{9,10},{10,1... | collective-permute-start | bytes 1572872 | tf_op jit(solution)/shard_map/ppermute | solution.py:833
  5.5 1.0 copy-start.3
  6.5 0.8 copy-start.5
  7.3 16.4 %copy-start.4 = (bf16[512,256]{1,0:T(8,128)(2,1)S(1)}, bf16[512,256]{1,0:T(8,128)(2,1)}, u32[]{:S(2)}) copy-start(bf16[512,256]{1,0:T(8,128)(2,1)} %constant.144.clone.refs_4_.refs_9_.refs_6_) | copy-start | bytes 786436
  23.8 7.5 %copy-start.13 = (f32[128,128]{1,0:T(8,128)S(1)}, f32[128,128]{1,0:T(8,128)}, u32[]{:S(2)}) copy-start(f32[128,128]{1,0:T(8,128)} %constant.151) | copy-start | bytes 196612
  23.8 9.1 %copy-start.14 = (f32[128,128]{1,0:T(8,128)S(1)}, f32[128,128]{1,0:T(8,128)}, u32[]{:S(2)}) copy-start(f32[128,128]{1,0:T(8,128)} %constant.142.clone) | copy-start | bytes 196612
  23.8 9.1 %copy-start.15 = (f32[128,128]{1,0:T(8,128)S(1)}, f32[128,128]{1,0:T(8,128)}, u32[]{:S(2)}) copy-start(f32[128,128]{1,0:T(8,128)} %constant.143.clone) | copy-start | bytes 196612
  23.8 16.2 %copy-start.12 = (f32[128,128]{1,0:T(8,128)S(1)}, f32[128,128]{1,0:T(8,128)}, u32[]{:S(2)}) copy-start(f32[128,128]{1,0:T(8,128)} %constant.153) | copy-start | bytes 196612
  23.8 16.3 %copy-start.6 = (f32[128,128]{1,0:T(8,128)S(1)}, f32[128,128]{1,0:T(8,128)}, u32[]{:S(2)}) copy-start(f32[128,128]{1,0:T(8,128)} %constant.141.clone.refs_3_.refs_8_.refs_6_.refs_5_) | copy-start | bytes 196612
  23.8 16.3 %copy-start.9 = (bf16[544,256]{1,0:T(8,128)(2,1)S(1)}, bf16[544,256]{1,0:T(8,128)(2,1)}, u32[]{:S(2)}) copy-start(bf16[544,256]{1,0:T(8,128)(2,1)} %constant.158.refs_7_) | copy-start | bytes 835588
  29.4 1.9 collective-permute-start.2
  31.4 8.7 %collective-permute-start.3 = (f32[4,128,128]{2,1,0:T(8,128)S(1)}, f32[4,128,128]{2,1,0:T(8,128)S(1)}, u32[]{:S(2)}, u32[]{:S(2)}) collective-permute-start(f32[4,128,128]{2,1,0:T(8,128)S(1)} %pad_maximum_fusion.2), channel_id=1, source_target_pairs={{0,2},{1,3},{2,0},{3,1},{4,6},{5,7},{6,4},{7,5},{8,10},{9,11},{10,... | collective-permute-start | bytes 786440 | tf_op jit(solution)/shard_map/ppermute | solution.py:844
  32.9 16.9 %copy-start.7 = (f32[128,128]{1,0:T(8,128)}, f32[128,128]{1,0:T(8,128)S(1)}, u32[]{:S(2)}) copy-start(f32[128,128]{1,0:T(8,128)S(1)} %get-tuple-element.64.refs_4_) | copy-start | bytes 196612
  33.0 22.9 %copy-start.10 = (f32[128,128]{1,0:T(8,128)}, f32[128,128]{1,0:T(8,128)S(1)}, u32[]{:S(2)}) copy-start(f32[128,128]{1,0:T(8,128)S(1)} %get-tuple-element.65) | copy-start | bytes 196612
  33.0 22.9 %copy-start.11 = (f32[128,128]{1,0:T(8,128)}, f32[128,128]{1,0:T(8,128)S(1)}, u32[]{:S(2)}) copy-start(f32[128,128]{1,0:T(8,128)S(1)} %get-tuple-element.66) | copy-start | bytes 196612
  49.9 5.9 %copy-start.16 = (s32[4]{0:T(128)S(1)}, s32[4]{0:T(128)}, u32[]{:S(2)}) copy-start(s32[4]{0:T(128)} %param.14) | copy-start | bytes 52
  49.9 143.8 %all-to-all-start = ((f32[8,1536,128]{2,1,0:T(8,128)}), f32[8,1536,128]{2,1,0:T(8,128)}, u32[]{:S(2)}, u32[]{:S(2)}) async-start(f32[8,1536,128]{2,1,0:T(8,128)} %bitcast.33), calls=%async_computation | async-start | bytes 12582912 | tf_op jit(solution)/shard_map/all_to_all | solution.py:916
  55.9 2.8 copy-start
  71.4 2.7 copy-start.1
  74.1 1.5 collective-permute-start.4
  76.6 8.5 %collective-permute-start.5 = (f32[4,128,128]{2,1,0:T(8,128)S(1)}, f32[4,128,128]{2,1,0:T(8,128)}, u32[]{:S(2)}, u32[]{:S(2)}) collective-permute-start(f32[4,128,128]{2,1,0:T(8,128)S(1)} %pad_maximum_fusion.5), channel_id=1, source_target_pairs={{0,2},{1,3},{2,0},{3,1},{4,6},{5,7},{6,4},{7,5},{8,10},{9,11},{10,... | collective-permute-start | bytes 786440 | tf_op jit(solution)/shard_map/ppermute | solution.py:844
  86.3 2.8 copy-start.2
  89.1 0.8 copy-start.8

commit v5 on v4

--- a/solution.py
+++ b/solution.py
@@ -740,7 +740,7 @@
 
 def solve(place, f, sides, totals, wraps, tables, a, rows_out, period):
     layers, ny, nx = f.shape
-    chunk = 8 if layers % 8 == 0 else 2
+    chunk = next(size for size in (16, 8, 2) if layers % size == 0)
     tall = rows_out + 2 * PAD
     moments = whole((4, ny, nx))
     return pl.pallas_call(

time: 357 us -> 356 us (level)
  no operation moved by 1% of the time
where the time goes in v5:
time: 356 us; the launch traced here: 355 us
  blocking collectives  151 us (42%)
  waiting for transfers between devices  115 us (32%)
  Pallas kernels  55.4 us (16%)
  local copies, waits for them, and re-layouts  16.6 us (5%)
  starting transfers between devices  12.1 us (3%)
    all_to_all x1, blocking collectives, per_device(): lax.all_to_all(ortho_cells, 'vec', split_axis=0, concat_axis=0, tiled=True)  141 us
    all_to_all x1, waiting for transfers between devices, per_device(): lax.all_to_all(advanced.reshape(vectors, piece_rows, nx), 'vec', split_ax...  100 us
    pallas_call x2, Pallas kernels, rates(): pl.pallas_call(functools.partial(rate_kernel, tangent, len(halos) > 0, ch...  29.1 us
    ppermute x4, waiting for transfers between devices, side_sums(): lax.ppermute(jnp.concatenate([right, left], axis=0), 'gz', [(i, i ^ span)...  15.1 us
    unnamed x35, local copies, waits for them, and re-layouts  13.7 us
    pallas_call x2, Pallas kernels, solve(): pl.pallas_call(functools.partial(solve_kernel, chunk, layers, period, row...  12.6 us
    all_to_all x1, blocking collectives, per_device(): lax.all_to_all(jnp.broadcast_to(part[None], (devices,) + part.shape), ('v...  10.6 us
  transfers between devices with their start and end apart: 7, of which 5 were waited for; matrix products, arithmetic and copies ran while one was open for 1% of the time, Pallas kernels for 9%

profile of v5, /device:TPU:0, one launch (start us, length us, event | category | flops | bytes accessed | tf_op | source)
XLA Modules:
  0.0 355.3 jit_solution(5328199686001093083)
XLA Ops:
  0.6 1.3 slice_bitcast_fusion
  1.9 1.0 slice_bitcast_fusion.4
  2.9 2.4 collective-permute-start.1
  5.4 0.1 collective-permute-start
  5.5 0.1 pad_add_fusion.refs_0_
  5.5 0.0 copy-start.3
  5.6 0.9 copy-done.3
  6.5 0.8 copy-done.5
  7.3 16.4 %tangent_rates.1 = (f32[3,32,128,128]{3,2,1,0:T(8,128)}, f32[32,128,128]{2,1,0:T(8,128)}, f32[4,128,128]{2,1,0:T(8,128)S(1)}) custom-call(s32[2]{0:T(128)S(1)} %pad_add_fusion.refs_0_, f32[3,32,128,128]{3,2,1,0:T(8,128)} %bitcast.30, f32[3,32,128,128]{3,2,1,0:T(8,128)} %refs_2_.5, f32[128,128]{1,0:T(8,128)S(1)} %copy-done.5, bf16[512,256]{1,0:T(8,128)(2,1)S(1)} %copy-done.3), custom_call_target="tpu_custom_call" | custom-call | flops 94371840 | bytes 25165824 | tf_op jit(solution)/shard_map/tangent_rates/pallas_call | solution.py:682
  23.7 0.0 collective-permute-done.1.refs_4_
  23.7 0.0 collective-permute-done.refs_3_
  23.7 0.0 copy-done.4
  23.8 0.0 copy-start.13
  23.8 0.0 copy-start.14
  23.8 0.0 copy-start.15
  23.8 0.0 copy-start.12
  23.8 0.0 copy-start.6
  23.8 0.0 copy-start.9
  23.8 5.6 %tangent_edges.1 = (f32[3,32,128,128]{3,2,1,0:T(8,128)}, f32[32,128,128]{2,1,0:T(8,128)}, f32[4,128,128]{2,1,0:T(8,128)S(1)}) custom-call(s32[2]{0:T(128)S(1)} %pad_add_fusion.refs_0_, f32[3,32,128,128]{3,2,1,0:T(8,128)} %bitcast.31, f32[3,32,128,128]{3,2,1,0:T(8,128)} %refs_2_.5, ...), custom_call_target="tpu_custom_call", output_to_operand_aliasing={{0}: (5, {}), {1}: (6, {})} | custom-call | flops 11796480 | bytes 2621440 | tf_op jit(solution)/shard_map/tangent_edges/pallas_call | solution.py:707
  29.4 0.7 collective-permute-start.2
  30.1 1.2 collective-permute-done.2
  31.3 0.0 copy-done.13
  31.4 1.5 collective-permute-start.3
  32.9 0.0 copy-done.14
  32.9 0.0 copy-done.15
  32.9 0.0 copy-start.7
  33.0 0.0 copy-start.10
  33.0 0.0 copy-start.11
  33.0 7.0 %collective-permute-done.3 = f32[4,128,128]{2,1,0:T(8,128)S(1)} collective-permute-done((f32[4,128,128]{2,1,0:T(8,128)S(1)}, f32[4,128,128]{2,1,0:T(8,128)S(1)}, u32[]{:S(2)}, u32[]{:S(2)}) %collective-permute-start.3) | collective-permute-done | bytes 262176 | tf_op jit(solution)/shard_map/ppermute | solution.py:844
  40.0 0.0 copy-done.12
  40.0 0.1 add_select_fusion.9
  40.2 0.0 copy-done.6
  40.2 0.0 copy-done.9
  40.2 9.0 %tangent_solve.1 = f32[3,32,128,128]{3,2,1,0:T(8,128)} custom-call(s32[2]{0:T(128)S(1)} %pad_add_fusion.refs_0_, f32[32,128,128]{2,1,0:T(8,128)} %get-tuple-element.24.refs_1_, f32[4,128,128]{2,1,0:T(8,128)S(1)} %pad_maximum_fusion.3.refs_2_, f32[4,128,128]{2,1,0:T(8,128)S(1)} %pad_maximum_fusion.4.refs_3_, f32[128,128]{1,0:T(8,128)S(1)} %get-tuple-element.64.refs_4_, ...), custom_call_target="tpu_custom_call" | custom-call | flops 62914560 | bytes 18874368 | tf_op jit(solution)/shard_map/tangent_solve/pallas_call | solution.py:746
  49.2 0.0 copy-done.7
  49.2 0.0 copy-start.16
  49.2 5.8 %all-to-all-start = ((f32[8,1536,128]{2,1,0:T(8,128)}), f32[8,1536,128]{2,1,0:T(8,128)}, u32[]{:S(2)}, u32[]{:S(2)}) async-start(f32[8,1536,128]{2,1,0:T(8,128)} %bitcast.33), calls=%async_computation | async-start | bytes 12582912 | tf_op jit(solution)/shard_map/all_to_all | solution.py:916
  55.1 0.0 copy-done.16
  55.1 0.1 fusion.3
  55.2 0.0 copy-done.10
  55.2 0.0 copy-done.11
  55.2 0.0 copy-start
  55.2 2.8 copy-done
  58.0 12.7 %base_rates.1 = (f32[3,32,128,128]{3,2,1,0:T(8,128)S(1)}, f32[32,128,128]{2,1,0:T(8,128)S(1)}, f32[4,128,128]{2,1,0:T(8,128)S(1)}) custom-call(s32[2]{0:T(128)S(1)} %pad_add_fusion.refs_0_, f32[32]{0:T(128)S(1)} %broadcast_multiply_fusion.refs_1_, f32[3,32,128,128]{3,2,1,0:T(8,128)S(1)} %copy-done, f32[8,128,128]{2,1,0:T(8,128)S(1)} %collective-permute-done.refs_3_, ...), custom_call_target="tpu_custom_call" | custom-call | flops 94371840 | bytes 25165824 | tf_op jit(solution)/shard_map/base_rates/pallas_call | solution.py:682
  70.8 0.0 copy-start.1
  70.8 2.7 copy-done.1
  73.5 0.0 collective-permute-start.4
  73.5 1.5 collective-permute-done.4
  75.0 0.9 add_select_fusion.7
  75.9 1.5 collective-permute-start.5
  77.4 0.7 constant_dynamic-slice_fusion
  78.1 0.9 maximum_maximum_fusion.refs_7_
  79.1 5.4 %collective-permute-done.5 = f32[4,128,128]{2,1,0:T(8,128)} collective-permute-done((f32[4,128,128]{2,1,0:T(8,128)S(1)}, f32[4,128,128]{2,1,0:T(8,128)}, u32[]{:S(2)}, u32[]{:S(2)}) %collective-permute-start.5) | collective-permute-done | bytes 262176 | tf_op jit(solution)/shard_map/ppermute | solution.py:844
  84.4 1.1 add_select_fusion.5
  85.6 0.0 copy-start.2
  85.6 2.8 copy-done.2
  88.4 0.8 copy-done.8
  89.2 3.6 %base_solve.1 = f32[3,32,16,128]{3,2,1,0:T(8,128)} custom-call(s32[2]{0:T(128)S(1)} %pad_add_fusion.refs_0_, f32[32,128,128]{2,1,0:T(8,128)S(1)} %get-tuple-element.30.refs_1_, f32[4,128,128]{2,1,0:T(8,128)S(1)} %pad_maximum_fusion.6.refs_2_, f32[4,128,128]{2,1,0:T(8,128)S(1)} %pad_maximum_fusion.7.refs_3_, f32[128,128]{1,0:T(8,128)S(1)} %copy-done.8, ...), custom_call_target="tpu_custom_call" | custom-call | flops 62914560 | bytes 18874368 | tf_op jit(solution)/shard_map/base_solve/pallas_call | solution.py:746
  92.9 100.1 %all-to-all-done.x_hbm = f32[8,1536,128]{2,1,0:T(8,128)} async-done(((f32[8,1536,128]{2,1,0:T(8,128)}), f32[8,1536,128]{2,1,0:T(8,128)}, u32[]{:S(2)}, u32[]{:S(2)}) %all-to-all-start) | async-done | bytes 6291488 | tf_op jit(solution)/shard_map/all_to_all | solution.py:916
  193.0 4.0 %gram_parts.1 = f32[1,128]{1,0:T(1,128)S(1)} custom-call(f32[8,1536,128]{2,1,0:T(8,128)} %all-to-all-done.x_hbm), custom_call_target="tpu_custom_call" | custom-call | flops 12582912 | bytes 6291456 | tf_op jit(solution)/shard_map/gram_parts/pallas_call | solution.py:787
  197.1 10.6 %all_to_all.15.parts_ref = f32[32,1,128]{2,1,0:T(1,128)S(1)} all-to-all(f32[32,1,128]{2,1,0:T(1,128)S(1)} %broadcast_in_dim.5), channel_id=1, replica_groups=mesh['vec'=8,'gz'=4] {'vec','gz'}, dimensions={0} | all-to-all | bytes 32768 | tf_op jit(solution)/shard_map/all_to_all | solution.py:938
  207.6 4.1 %ortho_rows.1 = (f32[8,1536,128]{2,1,0:T(8,128)S(1)}, f32[1,8]{1,0:T(1,128)}) custom-call(f32[32,1,128]{2,1,0:T(1,128)S(1)} %all_to_all.15.parts_ref, f32[8,1536,128]{2,1,0:T(8,128)} %all-to-all-done.x_hbm), custom_call_target="tpu_custom_call" | custom-call | flops 12582912 | bytes 12582912 | tf_op jit(solution)/shard_map/ortho_rows/pallas_call | solution.py:809
  211.7 140.9 %all_to_all.16 = f32[8,1536,128]{2,1,0:T(8,128)S(1)} all-to-all(f32[8,1536,128]{2,1,0:T(8,128)S(1)} %get-tuple-element.37), channel_id=1, replica_groups=mesh['vec'=8,'gz'=4] {'vec'}, dimensions={0} | all-to-all | bytes 12582912 | tf_op jit(solution)/shard_map/all_to_all | solution.py:949
  352.6 2.7 copy.26
  (16 shorter events, 0.3 us)
Async XLA Ops:
  2.9 20.8 %collective-permute-start.1 = (f32[8,128,128]{2,1,0:T(8,128)S(1)}, f32[8,128,128]{2,1,0:T(8,128)S(1)}, u32[]{:S(2)}, u32[]{:S(2)}) collective-permute-start(f32[8,128,128]{2,1,0:T(8,128)S(1)} %pad_maximum_fusion.1), channel_id=1, source_target_pairs={{0,3},{1,0},{2,1},{3,2},{4,7},{5,4},{6,5},{7,6},{8,11},{9,8},{10,9... | collective-permute-start | bytes 1572872 | tf_op jit(solution)/shard_map/ppermute | solution.py:833
  5.4 18.3 %collective-permute-start = (f32[8,128,128]{2,1,0:T(8,128)S(1)}, f32[8,128,128]{2,1,0:T(8,128)S(1)}, u32[]{:S(2)}, u32[]{:S(2)}) collective-permute-start(f32[8,128,128]{2,1,0:T(8,128)S(1)} %pad_maximum_fusion), channel_id=1, source_target_pairs={{0,1},{1,2},{2,3},{3,0},{4,5},{5,6},{6,7},{7,4},{8,9},{9,10},{10,1... | collective-permute-start | bytes 1572872 | tf_op jit(solution)/shard_map/ppermute | solution.py:833
  5.5 1.0 copy-start.3
  6.5 0.8 copy-start.5
  7.3 16.4 %copy-start.4 = (bf16[512,256]{1,0:T(8,128)(2,1)S(1)}, bf16[512,256]{1,0:T(8,128)(2,1)}, u32[]{:S(2)}) copy-start(bf16[512,256]{1,0:T(8,128)(2,1)} %constant.144.clone.refs_4_.refs_9_.refs_6_) | copy-start | bytes 786436
  23.8 7.5 %copy-start.13 = (f32[128,128]{1,0:T(8,128)S(1)}, f32[128,128]{1,0:T(8,128)}, u32[]{:S(2)}) copy-start(f32[128,128]{1,0:T(8,128)} %constant.151) | copy-start | bytes 196612
  23.8 9.1 %copy-start.14 = (f32[128,128]{1,0:T(8,128)S(1)}, f32[128,128]{1,0:T(8,128)}, u32[]{:S(2)}) copy-start(f32[128,128]{1,0:T(8,128)} %constant.142.clone) | copy-start | bytes 196612
  23.8 9.1 %copy-start.15 = (f32[128,128]{1,0:T(8,128)S(1)}, f32[128,128]{1,0:T(8,128)}, u32[]{:S(2)}) copy-start(f32[128,128]{1,0:T(8,128)} %constant.143.clone) | copy-start | bytes 196612
  23.8 16.2 %copy-start.12 = (f32[128,128]{1,0:T(8,128)S(1)}, f32[128,128]{1,0:T(8,128)}, u32[]{:S(2)}) copy-start(f32[128,128]{1,0:T(8,128)} %constant.153) | copy-start | bytes 196612
  23.8 16.3 %copy-start.6 = (f32[128,128]{1,0:T(8,128)S(1)}, f32[128,128]{1,0:T(8,128)}, u32[]{:S(2)}) copy-start(f32[128,128]{1,0:T(8,128)} %constant.141.clone.refs_3_.refs_8_.refs_6_.refs_5_) | copy-start | bytes 196612
  23.8 16.3 %copy-start.9 = (bf16[544,256]{1,0:T(8,128)(2,1)S(1)}, bf16[544,256]{1,0:T(8,128)(2,1)}, u32[]{:S(2)}) copy-start(bf16[544,256]{1,0:T(8,128)(2,1)} %constant.158.refs_7_) | copy-start | bytes 835588
  29.4 1.9 collective-permute-start.2
  31.4 8.7 %collective-permute-start.3 = (f32[4,128,128]{2,1,0:T(8,128)S(1)}, f32[4,128,128]{2,1,0:T(8,128)S(1)}, u32[]{:S(2)}, u32[]{:S(2)}) collective-permute-start(f32[4,128,128]{2,1,0:T(8,128)S(1)} %pad_maximum_fusion.2), channel_id=1, source_target_pairs={{0,2},{1,3},{2,0},{3,1},{4,6},{5,7},{6,4},{7,5},{8,10},{9,11},{10,... | collective-permute-start | bytes 786440 | tf_op jit(solution)/shard_map/ppermute | solution.py:844
  32.9 16.2 %copy-start.7 = (f32[128,128]{1,0:T(8,128)}, f32[128,128]{1,0:T(8,128)S(1)}, u32[]{:S(2)}) copy-start(f32[128,128]{1,0:T(8,128)S(1)} %get-tuple-element.64.refs_4_) | copy-start | bytes 196612
  33.0 22.3 %copy-start.10 = (f32[128,128]{1,0:T(8,128)}, f32[128,128]{1,0:T(8,128)S(1)}, u32[]{:S(2)}) copy-start(f32[128,128]{1,0:T(8,128)S(1)} %get-tuple-element.65) | copy-start | bytes 196612
  33.0 22.3 %copy-start.11 = (f32[128,128]{1,0:T(8,128)}, f32[128,128]{1,0:T(8,128)S(1)}, u32[]{:S(2)}) copy-start(f32[128,128]{1,0:T(8,128)S(1)} %get-tuple-element.66) | copy-start | bytes 196612
  49.2 5.9 %copy-start.16 = (s32[4]{0:T(128)S(1)}, s32[4]{0:T(128)}, u32[]{:S(2)}) copy-start(s32[4]{0:T(128)} %param.14) | copy-start | bytes 52
  49.2 143.8 %all-to-all-start = ((f32[8,1536,128]{2,1,0:T(8,128)}), f32[8,1536,128]{2,1,0:T(8,128)}, u32[]{:S(2)}, u32[]{:S(2)}) async-start(f32[8,1536,128]{2,1,0:T(8,128)} %bitcast.33), calls=%async_computation | async-start | bytes 12582912 | tf_op jit(solution)/shard_map/all_to_all | solution.py:916
  55.2 2.8 copy-start
  70.8 2.7 copy-start.1
  73.5 1.5 collective-permute-start.4
  75.9 8.5 %collective-permute-start.5 = (f32[4,128,128]{2,1,0:T(8,128)S(1)}, f32[4,128,128]{2,1,0:T(8,128)}, u32[]{:S(2)}, u32[]{:S(2)}) collective-permute-start(f32[4,128,128]{2,1,0:T(8,128)S(1)} %pad_maximum_fusion.5), channel_id=1, source_target_pairs={{0,2},{1,3},{2,0},{3,1},{4,6},{5,7},{6,4},{7,5},{8,10},{9,11},{10,... | collective-permute-start | bytes 786440 | tf_op jit(solution)/shard_map/ppermute | solution.py:844
  85.6 2.8 copy-start.2
  88.4 0.8 copy-start.8
